TPU v7x, 32 devices: a whole 2x2x4 slice. The times are simulated.
32 devices in a mesh: lat: 4 (over x, core), lon: 8 (over z, y).
Axes of the slice: x: 2, y: 2, z: 4, core: 2. Of those that a mesh axis runs over, the one named last changes fastest.
Arguments:
- obs_value: float32 [32, 21, 32, 128], P(('lat', 'lon')), may hold values from -6 to 6
- obs_cell: int32 [32, 32, 128], P(('lat', 'lon')), may hold values from 0 to 12287
- obs_count: int32 [32, 32], P(('lat', 'lon')), may hold values from 0 to 128, as said below
- bottom_level: int32 [192, 2048], P('lat', 'lon'), may hold values from 0 to 10
- diffusivity: float32 [2, 192, 2048], P(None, 'lat', 'lon'), may hold values from 0.5 to 16
- partner: int32 [2048], P('lon'), may hold values from 0 to 2047, as said below
- length_scale: float32 [21], replicated, may hold values from 0.25 to 2
- sigma: float32 [21], replicated, may hold values from 0.5 to 2
Outputs:
- obs_fit: float32 [32, 21, 32, 128], P(('lat', 'lon'))
- diffused: float32 [21, 192, 2048], P(None, 'lat', 'lon')
Inputs may be any that keep to these rules, and one draw needn't show every extreme that they name: `obs_count`: at most 128 live slots from one device to one owner; in every draw one owner receives 128 from every device. partner[i] = (centre - i) mod 2048 for one centre of each draw.
All inputs are finite; a program needn't handle non-finite values.
Results may differ from a plain program's by a relative error of at most 0.00002.
Values sent between devices are 32-bit elements; how exact they have to be, the bound alone decides.
No kernel may reach another device: no remote copies, remote signals or barrier semaphores. Data moves between devices by JAX's collectives and lax.ppermute only.
A program may use at most 128 MiB of HBM per device.

v0:
```python
import jax
import jax.numpy as jnp
from jax import lax
from jax.sharding import PartitionSpec as P

LEV = 10
STEPS = 2
SWEEPS = 6


def with_halo(block, sides, width, periodic):
    for axis, dim in sides:
        count = lax.axis_size(axis)
        forward = [(i, i + 1) for i in range(count - 1)]
        if periodic:
            forward.append((count - 1, 0))
        backward = [(target, source) for source, target in forward]
        low = lax.ppermute(
            lax.slice_in_dim(block, block.shape[dim] - width, None, axis=dim), axis, forward
        )
        high = lax.ppermute(lax.slice_in_dim(block, 0, width, axis=dim), axis, backward)
        block = jnp.concatenate([low, block, high], axis=dim)
    return block


def extend_deep(block, depth, partner_wide, top_band):
    tile_rows = block.shape[1]
    sideways = with_halo(block, (("lon", 2),), depth, True)
    extended = with_halo(sideways, (("lat", 1),), depth, False)
    top_rows = lax.all_gather(block[:, tile_rows - depth :, :], "lon", axis=2, tiled=True)
    ghost = jnp.take(top_rows, partner_wide, axis=2)[:, ::-1, :]
    upper = jnp.where(top_band, ghost, extended[:, tile_rows + depth :, :])
    return extended.at[:, tile_rows + depth :, :].set(upper)


def face_weights(coef_pad, channels, scale):
    centre = coef_pad[:, 1:-1, 1:-1]
    wet_mask = centre[:channels]
    kappa_lon = centre[channels][None]
    kappa_lat = centre[channels + 1][None]
    wet_pad = coef_pad[:channels]
    lon_pad = coef_pad[channels][None]
    lat_pad = coef_pad[channels + 1][None]
    w_east = scale * (0.5 * (kappa_lon + lon_pad[:, 1:-1, 2:])) * wet_mask * wet_pad[:, 1:-1, 2:]
    w_west = scale * (0.5 * (kappa_lon + lon_pad[:, 1:-1, :-2])) * wet_mask * wet_pad[:, 1:-1, :-2]
    w_north = scale * (0.5 * (kappa_lat + lat_pad[:, 2:, 1:-1])) * wet_mask * wet_pad[:, 2:, 1:-1]
    w_south = scale * (0.5 * (kappa_lat + lat_pad[:, :-2, 1:-1])) * wet_mask * wet_pad[:, :-2, 1:-1]
    diagonal_sum = 1.0 + w_east + w_west + w_north + w_south
    return (w_east, w_west, w_north, w_south, diagonal_sum)


def trim_margin(array, outer, inner):
    offset = outer - inner
    return array[:, offset : array.shape[1] - offset, offset : array.shape[2] - offset]


def per_device(
    obs_value, obs_cell, obs_count, bottom_level, diffusivity, partner, length_scale, sigma
):
    channels = obs_value.shape[1]
    devices = obs_value.shape[2]
    slots = obs_value.shape[3]
    lat_count = lax.axis_size("lat")
    top_band = lax.axis_index("lat") == lat_count - 1
    level_of = jnp.concatenate(
        [
            jnp.arange(LEV, dtype=jnp.int32),
            jnp.arange(LEV, dtype=jnp.int32),
            jnp.zeros((1,), jnp.int32),
        ]
    )
    wet_mask = (level_of[:, None, None] < bottom_level[None]).astype(jnp.float32)
    live_slots = (jnp.arange(slots, dtype=jnp.int32)[None, :] < obs_count[0][:, None]).astype(
        jnp.float32
    )
    outgoing = obs_value * live_slots[None, None]
    cell_block = obs_cell.reshape(1, 1, devices, slots)
    arrived, cell_ids = (
        lax.all_to_all(outgoing, ("lat", "lon"), split_axis=2, concat_axis=2, tiled=True),
        lax.all_to_all(cell_block, ("lat", "lon"), split_axis=2, concat_axis=2, tiled=True),
    )
    spread = arrived.reshape(channels, -1)
    cell_ids = cell_ids.reshape(-1)
    tile_rows = bottom_level.shape[0]
    tile_cols = bottom_level.shape[1]
    field = jnp.zeros((channels, tile_rows * tile_cols), jnp.float32).at[:, cell_ids].add(spread)
    field = field.reshape(channels, tile_rows, tile_cols) * (sigma[:, None, None] * wet_mask)
    coef_stack = jnp.concatenate([wet_mask, diffusivity], axis=0)
    scale = length_scale[:, None, None]
    state = field
    depth = SWEEPS
    partner_wide = with_halo(partner, (("lon", 0),), depth + 1, True)
    coef_pad = extend_deep(coef_stack, depth + 1, partner_wide, top_band)
    w_east, w_west, w_north, w_south, diagonal_sum = face_weights(coef_pad, channels, scale)
    partner_mid = partner_wide[1:-1]
    for step_index in range(STEPS):
        source_wide = extend_deep(state, depth, partner_mid, top_band)
        current = source_wide
        for sweep_index in range(SWEEPS):
            inner = depth - sweep_index - 1
            current = (
                trim_margin(source_wide, depth, inner)
                + trim_margin(w_east, depth, inner) * current[:, 1:-1, 2:]
                + trim_margin(w_west, depth, inner) * current[:, 1:-1, :-2]
                + trim_margin(w_north, depth, inner) * current[:, 2:, 1:-1]
                + trim_margin(w_south, depth, inner) * current[:, :-2, 1:-1]
            ) / trim_margin(diagonal_sum, depth, inner)
        state = current
    diffused = sigma[:, None, None] * state
    local_fit = diffused.reshape(channels, -1)[:, cell_ids]
    returned = lax.all_to_all(
        local_fit.reshape(1, channels, devices, slots),
        ("lat", "lon"),
        split_axis=2,
        concat_axis=2,
        tiled=True,
    )
    obs_fit = returned * live_slots[None, None]
    return (obs_fit, diffused)


def solution(mesh):
    return jax.shard_map(
        per_device,
        mesh=mesh,
        in_specs=(
            P(("lat", "lon"), None, None, None),
            P(("lat", "lon"), None, None),
            P(("lat", "lon"), None),
            P("lat", "lon"),
            P(None, "lat", "lon"),
            P("lon"),
            P(),
            P(),
        ),
        out_specs=(P(("lat", "lon"), None, None, None), P(None, "lat", "lon")),
        check_vma=False,
    )
```

profile of v0, /device:TPU:0, one launch (start us, length us, event | category | flops | bytes accessed | tf_op | source)
XLA Modules:
  0.0 462.3 jit_solution(18290541344450033408)
XLA Ops:
  7.2 7.3 %all-to-all-start = ((s32[1,1,32,128]{3,1,0,2:T(1,128)}), s32[1,1,32,128]{3,1,0,2:T(1,128)S(1)}, u32[]{:S(2)}, u32[]{:S(2)}) async-start(s32[1,1,32,128]{3,1,0,2:T(1,128)} %bitcast.43), calls=%async_computation | async-start | bytes 32768 | tf_op jit(solution)/shard_map/all_to_all | solution.py:80
  15.4 4.6 collective-permute-start.5
  20.9 1.1 fusion.64
  22.2 4.8 %collective-permute-start.7 = (f32[23,48,7]{1,0,2:T(8,128)S(1)}, f32[23,48,7]{1,0,2:T(8,128)S(1)}, u32[]{:S(2)}, u32[]{:S(2)}) collective-permute-start(f32[23,48,7]{1,0,2:T(8,128)S(1)} %copy.172), channel_id=1, source_target_pairs={{1,0},{2,1},{3,2},{4,3},{5,4},{6,5},{7,6},{0,7},{9,8},{10,9},{11,1... | collective-permute-start | bytes 92744 | tf_op jit(solution)/shard_map/ppermute | solution.py:21
  28.8 1.0 copy_multiply_fusion
  32.1 2.3 collective-permute-done.6
  35.8 1.3 collective-permute-start.9
  37.1 3.0 collective-permute-start.8
  40.1 3.7 all-to-all-start.1
  44.6 1.6 copy.155
  46.2 1.7 pad_maximum_fusion
  47.9 12.0 %all-to-all-done.1 = f32[1,21,32,128]{3,1,0,2:T(8,128)S(1)} async-done(((f32[1,21,32,128]{3,1,0,2:T(8,128)}), f32[1,21,32,128]{3,1,0,2:T(8,128)S(1)}, u32[]{:S(2)}, u32[]{:S(2)}) %all-to-all-start.1) | async-done | bytes 344096 | tf_op jit(solution)/shard_map/all_to_all | solution.py:79
  61.0 25.4 %scatter_custom_fusion = f32[21,12288]{0,1:T(8,128)} fusion(s32[4096]{0:T(1024)S(1)} %bitcast.42, f32[4096,21]{1,0:T(8,128)S(1)} %copy.135, f32[]{:T(128)} %constant.109.clone.1), kind=kCustom, calls=%fused_computation.5 | custom fusion | flops 86016 | bytes 1032196 | tf_op jit(solution)/shard_map/scatter-add | solution.py:86
  86.4 4.6 copy.136
  91.2 1.1 fusion.78
  92.3 1.4 collective-permute-start.1
  94.4 52.0 %all_gather.9 = f32[21,6,2048]{2,0,1:T(8,128)S(1)} all-gather(f32[21,6,256]{2,0,1:T(8,128)S(1)} %copy.141), channel_id=1, replica_groups=mesh['lat'=4,'lon'=8] {'lon'}, dimensions={2}, use_global_device_ids=true | all-gather | bytes 1161216 | tf_op jit(solution)/shard_map/all_gather | solution.py:30
  146.3 4.8 %copy.142 = f32[21,6,2048]{0,1,2:T(8,128)} copy(f32[21,6,2048]{2,0,1:T(8,128)S(1)} %all_gather.9) | data formatting | bytes 2064384 | tf_op jit(solution)/shard_map/all_gather | solution.py:30
  151.1 5.1 %gather_fusion.2 = f32[268,21,6]{1,2,0:T(8,128)} fusion(f32[21,6,2048]{0,1,2:T(8,128)} %copy.142, s32[1024]{0:T(1024)S(1)} %pad_clamp_fusion.1), kind=kCustom, calls=%fused_computation.clone | custom fusion | bytes 271216 | tf_op jit(solution)/shard_map/jit(_take)/gather | solution.py:31
  156.3 1.4 pad_maximum_fusion.10
  157.7 1.3 collective-permute-start.3
  159.4 1.7 rev.9
  161.2 3.5 collective-permute-start.2
  165.4 1.2 broadcast_select_fusion.2
  166.6 1.7 copy.144
  168.3 1.0 copy.140
  169.4 1.9 pad_maximum_fusion.1
  171.8 6.5 %copy.154 = f32[23,7,2048]{0,1,2:T(8,128)} copy(f32[23,7,2048]{2,0,1:T(8,128)} %all-gather.2.cloned.1.call-done) | data formatting | bytes 2637824 | tf_op jit(solution)/shard_map/all_gather | solution.py:30
  178.2 4.2 gather_fusion
  184.4 3.4 scatter.11
  187.7 1.3 fusion.67
  189.1 8.3 %add_add_fusion = (f32[21,60,268]{2,1,0:T(8,128)S(1)}, f32[21,60,268]{2,1,0:T(8,128)S(1)}, f32[21,60,268]{2,1,0:T(8,128)S(1)}, f32[21,60,268]{2,1,0:T(8,128)S(1)}, f32[21,60,268]{2,1,0:T(8,128)}) fusion(f32[23,62,270]{2,1,0:T(8,128)} %scatter.11, f32[60,268]{1,0:T(8,128)S(1)} %get-tuple-element.59, f32[21]{0:T(128)S(1)} %copy-done.29, ...), kind=kLoop, calls=%fused_computation.32 | loop fusion | flops 5402880 | bytes 13764564 | tf_op jit(solution)/shard_map/add | solution.py:48
  197.3 13.6 %fusion.8 = f32[21,58,266]{2,1,0:T(8,128)} fusion(f32[21,60,268]{2,1,0:T(8,128)} %copy-done.8, f32[21,60,268]{2,1,0:T(8,128)S(1)} %get-tuple-element.51, f32[21,60,268]{2,1,0:T(8,128)} %get-tuple-element.55, f32[21,60,268]{2,1,0:T(8,128)S(1)} %get-tuple-element.54, f32[21,60,268]{2,1,0:T(8,128)S(1)} %get-tuple-element.53, ...), kind=kLoop, calls=%fused_computation.19 | loop fusion | flops 2915892 | bytes 14255472 | tf_op jit(solution)/shard_map/div | solution.py:101
  211.0 11.1 %fusion.48 = f32[21,56,264]{2,1,0:T(8,128)} fusion(f32[21,58,266]{2,1,0:T(8,128)} %fusion.8, f32[21,60,268]{2,1,0:T(8,128)} %copy-done.8, f32[21,60,268]{2,1,0:T(8,128)S(1)} %get-tuple-element.51, f32[21,60,268]{2,1,0:T(8,128)} %get-tuple-element.55, f32[21,60,268]{2,1,0:T(8,128)S(1)} %get-tuple-element.54, f32[21,60,268]{2,1,0:T(8,128)S(1)} %get-tuple-element.53, ...), kind=kLoop, calls=%fused_computation.101 | loop fusion | flops 2794176 | bytes 13660416 | tf_op jit(solution)/shard_map/div | solution.py:101
  222.1 10.9 %fusion.43 = f32[21,54,262]{2,1,0:T(8,128)} fusion(f32[21,56,264]{2,1,0:T(8,128)} %fusion.48, f32[21,60,268]{2,1,0:T(8,128)} %copy-done.8, f32[21,60,268]{2,1,0:T(8,128)S(1)} %get-tuple-element.51, f32[21,60,268]{2,1,0:T(8,128)} %get-tuple-element.55, f32[21,60,268]{2,1,0:T(8,128)S(1)} %get-tuple-element.54, f32[21,60,268]{2,1,0:T(8,128)S(1)} %get-tuple-element.53, ...), kind=kLoop, calls=%fused_computation.92 | loop fusion | flops 2673972 | bytes 13072752 | tf_op jit(solution)/shard_map/div | solution.py:101
  233.0 10.5 %fusion.38 = f32[21,52,260]{2,1,0:T(8,128)} fusion(f32[21,54,262]{2,1,0:T(8,128)} %fusion.43, f32[21,60,268]{2,1,0:T(8,128)} %copy-done.8, f32[21,60,268]{2,1,0:T(8,128)S(1)} %get-tuple-element.51, f32[21,60,268]{2,1,0:T(8,128)S(1)} %copy-done.6, f32[21,60,268]{2,1,0:T(8,128)S(1)} %get-tuple-element.54, f32[21,60,268]{2,1,0:T(8,128)S(1)} %get-tuple-element.53, ...), kind=kLoop, calls=%fused_computation.83 | loop fusion | flops 2555280 | bytes 12492480 | tf_op jit(solution)/shard_map/div | solution.py:101
  243.5 10.4 %fusion.33 = f32[21,50,258]{2,1,0:T(8,128)} fusion(f32[21,52,260]{2,1,0:T(8,128)} %fusion.38, f32[21,60,268]{2,1,0:T(8,128)} %copy-done.8, f32[21,60,268]{2,1,0:T(8,128)S(1)} %get-tuple-element.51, f32[21,60,268]{2,1,0:T(8,128)S(1)} %copy-done.6, f32[21,60,268]{2,1,0:T(8,128)S(1)} %get-tuple-element.54, f32[21,60,268]{2,1,0:T(8,128)S(1)} %get-tuple-element.53, ...), kind=kLoop, calls=%fused_computation.74 | loop fusion | flops 2438100 | bytes 11919600 | tf_op jit(solution)/shard_map/div | solution.py:101
  253.9 6.7 %fusion.60 = f32[21,48,256]{2,1,0:T(8,128)S(1)} fusion(f32[21,50,258]{2,1,0:T(8,128)} %fusion.33, f32[21,60,268]{2,1,0:T(8,128)} %copy-done.8, f32[21,60,268]{2,1,0:T(8,128)S(1)} %get-tuple-element.51, f32[21,60,268]{2,1,0:T(8,128)S(1)} %copy-done.6, f32[21,60,268]{2,1,0:T(8,128)S(1)} %get-tuple-element.54, f32[21,60,268]{2,1,0:T(8,128)S(1)} %get-tuple-element.53, ...), kind=kLoop, calls=%fused_computation.129 | loop fusion | flops 2322432 | bytes 11354112 | tf_op jit(solution)/shard_map/div | solution.py:101
  260.6 1.1 fusion.77
  261.7 3.0 collective-permute-start.11
  264.8 52.9 %all_gather.11 = f32[21,6,2048]{2,0,1:T(8,128)} all-gather(f32[21,6,256]{2,0,1:T(8,128)S(1)} %copy.161), channel_id=1, replica_groups=mesh['lat'=4,'lon'=8] {'lon'}, dimensions={2}, use_global_device_ids=true | all-gather | bytes 1161216 | tf_op jit(solution)/shard_map/all_gather | solution.py:30
  317.7 6.1 %copy.162 = f32[21,6,2048]{0,1,2:T(8,128)} copy(f32[21,6,2048]{2,0,1:T(8,128)} %all_gather.11) | data formatting | bytes 2064384 | tf_op jit(solution)/shard_map/all_gather | solution.py:30
  323.8 5.2 %gather_fusion.3 = f32[268,21,6]{1,2,0:T(8,128)} fusion(f32[21,6,2048]{0,1,2:T(8,128)} %copy.162, s32[1024]{0:T(1024)S(1)} %copy-done.20), kind=kCustom, calls=%fused_computation.1.clone | custom fusion | bytes 271216 | tf_op jit(solution)/shard_map/jit(_take)/gather | solution.py:31
  329.1 1.4 pad_maximum_fusion.7
  331.1 1.3 collective-permute-start.13
  332.4 1.4 select_bitcast_fusion.1
  333.8 2.7 rev.11
  337.2 3.7 collective-permute-start.12
  341.0 2.4 copy.163
  343.4 2.4 broadcast_select_fusion.1
  345.8 1.7 copy.164
  347.6 1.0 copy.160
  348.6 1.0 copy.159
  349.6 3.3 pad_maximum_fusion.2
  352.9 2.3 scatter.14
  355.2 13.1 %fusion.3 = f32[21,58,266]{2,1,0:T(8,128)} fusion(f32[21,60,268]{2,1,0:T(8,128)} %scatter.14, f32[21,60,268]{2,1,0:T(8,128)S(1)} %get-tuple-element.51, f32[21,60,268]{2,1,0:T(8,128)} %get-tuple-element.55, f32[21,60,268]{2,1,0:T(8,128)} %copy-done.4, f32[21,60,268]{2,1,0:T(8,128)} %copy-done.2, f32[21,60,268]{2,1,0:T(8,128)} %copy-done), kind=kLoop, calls=%fused_computation.10 | loop fusion | flops 2915892 | bytes 14255472 | tf_op jit(solution)/shard_map/div | solution.py:101
  368.3 10.9 %fusion.28 = f32[21,56,264]{2,1,0:T(8,128)} fusion(f32[21,58,266]{2,1,0:T(8,128)} %fusion.3, f32[21,60,268]{2,1,0:T(8,128)} %scatter.14, f32[21,60,268]{2,1,0:T(8,128)S(1)} %get-tuple-element.51, f32[21,60,268]{2,1,0:T(8,128)} %get-tuple-element.55, f32[21,60,268]{2,1,0:T(8,128)S(1)} %copy-done.5, f32[21,60,268]{2,1,0:T(8,128)S(1)} %copy-done.3, ...), kind=kLoop, calls=%fused_computation.65 | loop fusion | flops 2794176 | bytes 13660416 | tf_op jit(solution)/shard_map/div | solution.py:101
  379.2 11.0 %fusion.23 = f32[21,54,262]{2,1,0:T(8,128)} fusion(f32[21,56,264]{2,1,0:T(8,128)} %fusion.28, f32[21,60,268]{2,1,0:T(8,128)} %scatter.14, f32[21,60,268]{2,1,0:T(8,128)S(1)} %get-tuple-element.51, f32[21,60,268]{2,1,0:T(8,128)} %get-tuple-element.55, f32[21,60,268]{2,1,0:T(8,128)S(1)} %copy-done.5, f32[21,60,268]{2,1,0:T(8,128)S(1)} %copy-done.3, ...), kind=kLoop, calls=%fused_computation.56 | loop fusion | flops 2673972 | bytes 13072752 | tf_op jit(solution)/shard_map/div | solution.py:101
  390.2 10.5 %fusion.18 = f32[21,52,260]{2,1,0:T(8,128)} fusion(f32[21,54,262]{2,1,0:T(8,128)} %fusion.23, f32[21,60,268]{2,1,0:T(8,128)} %scatter.14, f32[21,60,268]{2,1,0:T(8,128)S(1)} %get-tuple-element.51, f32[21,60,268]{2,1,0:T(8,128)S(1)} %copy-done.7, f32[21,60,268]{2,1,0:T(8,128)S(1)} %copy-done.5, f32[21,60,268]{2,1,0:T(8,128)S(1)} %copy-done.3, ...), kind=kLoop, calls=%fused_computation.47 | loop fusion | flops 2555280 | bytes 12492480 | tf_op jit(solution)/shard_map/div | solution.py:101
  400.7 10.6 %fusion.13 = f32[21,50,258]{2,1,0:T(8,128)} fusion(f32[21,52,260]{2,1,0:T(8,128)} %fusion.18, f32[21,60,268]{2,1,0:T(8,128)} %scatter.14, f32[21,60,268]{2,1,0:T(8,128)S(1)} %get-tuple-element.51, f32[21,60,268]{2,1,0:T(8,128)S(1)} %copy-done.7, f32[21,60,268]{2,1,0:T(8,128)S(1)} %copy-done.5, f32[21,60,268]{2,1,0:T(8,128)S(1)} %copy-done.3, ...), kind=kLoop, calls=%fused_computation.38 | loop fusion | flops 2438100 | bytes 11919600 | tf_op jit(solution)/shard_map/div | solution.py:101
  411.3 6.7 %fusion.55 = f32[21,48,256]{2,1,0:T(8,128)S(1)} fusion(f32[21,50,258]{2,1,0:T(8,128)} %fusion.13, f32[21,60,268]{2,1,0:T(8,128)} %scatter.14, f32[21,60,268]{2,1,0:T(8,128)S(1)} %get-tuple-element.51, f32[21,60,268]{2,1,0:T(8,128)S(1)} %copy-done.7, f32[21,60,268]{2,1,0:T(8,128)S(1)} %copy-done.5, f32[21,60,268]{2,1,0:T(8,128)S(1)} %copy-done.3, ...), kind=kLoop, calls=%fused_computation.120 | loop fusion | flops 2580480 | bytes 11354196 | tf_op jit(solution)/shard_map/mul | solution.py:109
  418.0 4.1 copy.168
  422.1 13.5 %gather_fusion.1 = f32[4096,21]{1,0:T(8,128)S(1)} fusion(f32[21,12288]{0,1:T(8,128)} %bitcast.36, s32[4096]{0:T(1024)S(1)} %copy-done.18), kind=kCustom, calls=%fused_computation.3 | custom fusion | bytes 704512 | tf_op jit(solution)/shard_map/gather | solution.py:110
  436.2 18.2 %all_to_all.15 = f32[1,21,32,128]{3,1,0,2:T(8,128)S(1)} all-to-all(f32[1,21,32,128]{3,1,0,2:T(8,128)S(1)} %copy.166), channel_id=1, replica_groups=mesh['lat'=4,'lon'=8] {'lat','lon'}, dimensions={2} | all-to-all | bytes 688128 | tf_op jit(solution)/shard_map/all_to_all | solution.py:111
  (131 shorter events, 16.7 us)
Async XLA Ops:
  7.2 33.0 %all-to-all-start = ((s32[1,1,32,128]{3,1,0,2:T(1,128)}), s32[1,1,32,128]{3,1,0,2:T(1,128)S(1)}, u32[]{:S(2)}, u32[]{:S(2)}) async-start(s32[1,1,32,128]{3,1,0,2:T(1,128)} %bitcast.43), calls=%async_computation | async-start | bytes 32768 | tf_op jit(solution)/shard_map/all_to_all | solution.py:80
  14.5 157.3 %all-gather.2.cloned.1.call-start = ((), (), s32[]{:S(2)}) async-start(), calls=%async_computation.3 | async-start | bytes 1548288 | tf_op jit(solution)/shard_map/all_gather | solution.py:30
  15.4 14.4 %collective-permute-start.5 = (s32[7]{0:T(128)S(1)}, s32[7]{0:T(128)S(1)}, u32[]{:S(2)}, u32[]{:S(2)}) collective-permute-start(s32[7]{0:T(128)S(1)} %get-tuple-element.73), channel_id=1, source_target_pairs={{1,0},{2,1},{3,2},{4,3},{5,4},{6,5},{7,6},{0,7},{9,8},{10,9},{11,1... | collective-permute-start | bytes 92 | tf_op jit(solution)/shard_map/ppermute | solution.py:21
  19.9 9.9 %collective-permute-start.4 = (s32[7]{0:T(128)S(1)}, s32[7]{0:T(128)S(1)}, u32[]{:S(2)}, u32[]{:S(2)}) collective-permute-start(s32[7]{0:T(128)S(1)} %get-tuple-element.72), channel_id=1, source_target_pairs={{0,1},{1,2},{2,3},{3,4},{4,5},{5,6},{6,7},{7,0},{8,9},{9,10},{10,1... | collective-permute-start | bytes 92 | tf_op jit(solution)/shard_map/ppermute | solution.py:18
  20.8 6.4 %copy-start.15 = (f32[2,48,256]{2,1,0:T(8,128)S(1)}, f32[2,48,256]{2,1,0:T(8,128)}, u32[]{:S(2)}) copy-start(f32[2,48,256]{2,1,0:T(8,128)} %param.20) | copy-start | bytes 294916
  22.2 9.7 %collective-permute-start.7 = (f32[23,48,7]{1,0,2:T(8,128)S(1)}, f32[23,48,7]{1,0,2:T(8,128)S(1)}, u32[]{:S(2)}, u32[]{:S(2)}) collective-permute-start(f32[23,48,7]{1,0,2:T(8,128)S(1)} %copy.172), channel_id=1, source_target_pairs={{1,0},{2,1},{3,2},{4,3},{5,4},{6,5},{7,6},{0,7},{9,8},{10,9},{11,1... | collective-permute-start | bytes 92744 | tf_op jit(solution)/shard_map/ppermute | solution.py:21
  27.2 7.2 %collective-permute-start.6 = (f32[23,48,7]{1,0,2:T(8,128)S(1)}, f32[23,48,7]{1,0,2:T(8,128)S(1)}, u32[]{:S(2)}, u32[]{:S(2)}) collective-permute-start(f32[23,48,7]{1,0,2:T(8,128)S(1)} %copy.171), channel_id=1, source_target_pairs={{0,1},{1,2},{2,3},{3,4},{4,5},{5,6},{6,7},{7,0},{8,9},{9,10},{10,1... | collective-permute-start | bytes 92744 | tf_op jit(solution)/shard_map/ppermute | solution.py:18
  27.3 1.4 copy-start.30
  27.4 1.5 copy-start.16
  27.4 2.4 copy-start.21
  30.6 120.6 %copy-start.19 = (s32[1024]{0:T(1024)}, s32[1024]{0:T(1024)S(1)}, u32[]{:S(2)}) copy-start(s32[1024]{0:T(1024)S(1)} %pad_clamp_fusion.1) | copy-start | bytes 12292
  35.8 8.7 %collective-permute-start.9 = (f32[23,7,270]{2,0,1:T(8,128)S(1)}, f32[23,7,270]{2,0,1:T(8,128)S(1)}, u32[]{:S(2)}, u32[]{:S(2)}) collective-permute-start(f32[23,7,270]{2,0,1:T(8,128)S(1)} %get-tuple-element.65), channel_id=1, source_target_pairs={{8,0},{16,8},{24,16},{9,1},{17,9},{25,17},{10,2},{18,10},{26,18},{... | collective-permute-start | bytes 521648 | tf_op jit(solution)/shard_map/ppermute | solution.py:21
  37.1 9.1 %collective-permute-start.8 = (f32[23,7,270]{2,0,1:T(8,128)S(1)}, f32[23,7,270]{2,0,1:T(8,128)S(1)}, u32[]{:S(2)}, u32[]{:S(2)}) collective-permute-start(f32[23,7,270]{2,0,1:T(8,128)S(1)} %get-tuple-element.64), channel_id=1, source_target_pairs={{0,8},{8,16},{16,24},{1,9},{9,17},{17,25},{2,10},{10,18},{18,26},{... | collective-permute-start | bytes 521648 | tf_op jit(solution)/shard_map/ppermute | solution.py:18
  40.1 19.8 %all-to-all-start.1 = ((f32[1,21,32,128]{3,1,0,2:T(8,128)}), f32[1,21,32,128]{3,1,0,2:T(8,128)S(1)}, u32[]{:S(2)}, u32[]{:S(2)}) async-start(f32[1,21,32,128]{3,1,0,2:T(8,128)} %copy_multiply_fusion), calls=%async_computation.1 | async-start | bytes 786432 | tf_op jit(solution)/shard_map/all_to_all | solution.py:79
  86.3 4.6 copy-start.17
  86.3 4.6 copy-start.26
  86.3 4.6 copy-start.28
  92.3 64.0 %collective-permute-start.1 = (f32[21,48,6]{2,1,0:T(8,128)}, f32[21,48,6]{2,1,0:T(8,128)S(1)}, u32[]{:S(2)}, u32[]{:S(2)}) collective-permute-start(f32[21,48,6]{2,1,0:T(8,128)} %get-tuple-element.71), channel_id=1, source_target_pairs={{1,0},{2,1},{3,2},{4,3},{5,4},{6,5},{7,6},{0,7},{9,8},{10,9},{11,1... | collective-permute-start | bytes 72584 | tf_op jit(solution)/shard_map/ppermute | solution.py:21
  93.7 62.6 %collective-permute-start = (f32[21,48,6]{2,1,0:T(8,128)}, f32[21,48,6]{2,1,0:T(8,128)}, u32[]{:S(2)}, u32[]{:S(2)}) collective-permute-start(f32[21,48,6]{2,1,0:T(8,128)} %get-tuple-element.70), channel_id=1, source_target_pairs={{0,1},{1,2},{2,3},{3,4},{4,5},{5,6},{6,7},{7,0},{8,9},{9,10},{10,1... | collective-permute-start | bytes 72584 | tf_op jit(solution)/shard_map/ppermute | solution.py:18
  151.1 7.9 %copy-start.23 = (pred[268]{0:T(512)(128)(4,1)S(1)}, pred[268]{0:T(512)(128)(4,1)}, u32[]{:S(2)}) copy-start(pred[268]{0:T(512)(128)(4,1)} %compare_and_fusion) | copy-start | bytes 808
  156.3 2.8 copy-start.13
  156.3 3.1 copy-start.11
  157.7 7.0 %collective-permute-start.3 = (f32[21,6,268]{2,0,1:T(8,128)S(1)}, f32[21,6,268]{2,0,1:T(8,128)S(1)}, u32[]{:S(2)}, u32[]{:S(2)}) collective-permute-start(f32[21,6,268]{2,0,1:T(8,128)S(1)} %copy.170), channel_id=1, source_target_pairs={{8,0},{16,8},{24,16},{9,1},{17,9},{25,17},{10,2},{18,10},{26,18},{... | collective-permute-start | bytes 405224 | tf_op jit(solution)/shard_map/ppermute | solution.py:21
  161.2 8.1 %collective-permute-start.2 = (f32[21,6,268]{2,0,1:T(8,128)S(1)}, f32[21,6,268]{2,0,1:T(8,128)S(1)}, u32[]{:S(2)}, u32[]{:S(2)}) collective-permute-start(f32[21,6,268]{2,0,1:T(8,128)S(1)} %copy.169), channel_id=1, source_target_pairs={{0,8},{8,16},{16,24},{1,9},{9,17},{17,25},{2,10},{10,18},{18,26},{... | collective-permute-start | bytes 405224 | tf_op jit(solution)/shard_map/ppermute | solution.py:18
  164.7 0.7 copy-start.14
  171.7 6.5 %copy-start.8 = (f32[21,60,268]{2,1,0:T(8,128)}, f32[21,60,268]{2,1,0:T(8,128)S(1)}, u32[]{:S(2)}) copy-start(f32[21,60,268]{2,1,0:T(8,128)S(1)} %scatter.10) | copy-start | bytes 4052164
  171.7 6.5 %copy-start.22 = (s32[1024]{0:T(1024)S(1)}, s32[1024]{0:T(1024)}, u32[]{:S(2)}) copy-start(s32[1024]{0:T(1024)} %pad_clamp_fusion) | copy-start | bytes 12292
  171.7 10.7 %copy-start.25 = (pred[270]{0:T(512)(128)(4,1)S(1)}, pred[270]{0:T(512)(128)(4,1)}, u32[]{:S(2)}) copy-start(pred[270]{0:T(512)(128)(4,1)} %compare_and_fusion.1) | copy-start | bytes 814
  182.4 1.2 copy-start.9
  183.8 5.3 %copy-start.29 = (f32[21]{0:T(128)S(1)}, f32[21]{0:T(128)}, u32[]{:S(2)}) copy-start(f32[21]{0:T(128)} %param.22) | copy-start | bytes 256
  197.3 56.6 %copy-start = (f32[21,60,268]{2,1,0:T(8,128)}, f32[21,60,268]{2,1,0:T(8,128)S(1)}, u32[]{:S(2)}) copy-start(f32[21,60,268]{2,1,0:T(8,128)S(1)} %get-tuple-element.52) | copy-start | bytes 4052164
  197.3 56.6 %copy-start.2 = (f32[21,60,268]{2,1,0:T(8,128)}, f32[21,60,268]{2,1,0:T(8,128)S(1)}, u32[]{:S(2)}) copy-start(f32[21,60,268]{2,1,0:T(8,128)S(1)} %get-tuple-element.53) | copy-start | bytes 4052164
  197.3 56.6 %copy-start.4 = (f32[21,60,268]{2,1,0:T(8,128)}, f32[21,60,268]{2,1,0:T(8,128)S(1)}, u32[]{:S(2)}) copy-start(f32[21,60,268]{2,1,0:T(8,128)S(1)} %get-tuple-element.54) | copy-start | bytes 4052164
  222.1 10.9 %copy-start.6 = (f32[21,60,268]{2,1,0:T(8,128)S(1)}, f32[21,60,268]{2,1,0:T(8,128)}, u32[]{:S(2)}) copy-start(f32[21,60,268]{2,1,0:T(8,128)} %get-tuple-element.55) | copy-start | bytes 4052164
  261.7 67.3 %collective-permute-start.11 = (f32[21,48,6]{2,1,0:T(8,128)}, f32[21,48,6]{2,1,0:T(8,128)}, u32[]{:S(2)}, u32[]{:S(2)}) collective-permute-start(f32[21,48,6]{2,1,0:T(8,128)} %get-tuple-element.69), channel_id=1, source_target_pairs={{1,0},{2,1},{3,2},{4,3},{5,4},{6,5},{7,6},{0,7},{9,8},{10,9},{11,1... | collective-permute-start | bytes 72584 | tf_op jit(solution)/shard_map/ppermute | solution.py:21
  264.7 64.3 %collective-permute-start.10 = (f32[21,48,6]{2,1,0:T(8,128)}, f32[21,48,6]{2,1,0:T(8,128)}, u32[]{:S(2)}, u32[]{:S(2)}) collective-permute-start(f32[21,48,6]{2,1,0:T(8,128)} %get-tuple-element.68), channel_id=1, source_target_pairs={{0,1},{1,2},{2,3},{3,4},{4,5},{5,6},{6,7},{7,0},{8,9},{9,10},{10,1... | collective-permute-start | bytes 72584 | tf_op jit(solution)/shard_map/ppermute | solution.py:18
  317.7 6.1 %copy-start.20 = (s32[1024]{0:T(1024)S(1)}, s32[1024]{0:T(1024)}, u32[]{:S(2)}) copy-start(s32[1024]{0:T(1024)} %copy-done.19) | copy-start | bytes 12292
  323.8 8.6 %copy-start.24 = (pred[268]{0:T(512)(128)(4,1)S(1)}, pred[268]{0:T(512)(128)(4,1)}, u32[]{:S(2)}) copy-start(pred[268]{0:T(512)(128)(4,1)} %compare_and_fusion) | copy-start | bytes 808
  329.0 3.4 copy-start.12
  331.1 9.8 %collective-permute-start.13 = (f32[21,6,268]{2,0,1:T(8,128)}, f32[21,6,268]{2,0,1:T(8,128)}, u32[]{:S(2)}, u32[]{:S(2)}) collective-permute-start(f32[21,6,268]{2,0,1:T(8,128)} %copy.174), channel_id=1, source_target_pairs={{8,0},{16,8},{24,16},{9,1},{17,9},{25,17},{10,2},{18,10},{26,18},{... | collective-permute-start | bytes 405224 | tf_op jit(solution)/shard_map/ppermute | solution.py:21
  337.2 11.3 %collective-permute-start.12 = (f32[21,6,268]{2,0,1:T(8,128)}, f32[21,6,268]{2,0,1:T(8,128)}, u32[]{:S(2)}, u32[]{:S(2)}) collective-permute-start(f32[21,6,268]{2,0,1:T(8,128)} %copy.173), channel_id=1, source_target_pairs={{0,8},{8,16},{16,24},{1,9},{9,17},{17,25},{2,10},{10,18},{18,26},{... | collective-permute-start | bytes 405224 | tf_op jit(solution)/shard_map/ppermute | solution.py:18
  355.1 13.1 %copy-start.1 = (f32[21,60,268]{2,1,0:T(8,128)S(1)}, f32[21,60,268]{2,1,0:T(8,128)}, u32[]{:S(2)}) copy-start(f32[21,60,268]{2,1,0:T(8,128)} %copy-done) | copy-start | bytes 4052164
  355.1 13.1 %copy-start.3 = (f32[21,60,268]{2,1,0:T(8,128)S(1)}, f32[21,60,268]{2,1,0:T(8,128)}, u32[]{:S(2)}) copy-start(f32[21,60,268]{2,1,0:T(8,128)} %copy-done.2) | copy-start | bytes 4052164
  355.1 13.1 %copy-start.5 = (f32[21,60,268]{2,1,0:T(8,128)S(1)}, f32[21,60,268]{2,1,0:T(8,128)}, u32[]{:S(2)}) copy-start(f32[21,60,268]{2,1,0:T(8,128)} %copy-done.4) | copy-start | bytes 4052164
  379.2 11.0 %copy-start.7 = (f32[21,60,268]{2,1,0:T(8,128)S(1)}, f32[21,60,268]{2,1,0:T(8,128)}, u32[]{:S(2)}) copy-start(f32[21,60,268]{2,1,0:T(8,128)} %get-tuple-element.55) | copy-start | bytes 4052164
  400.7 10.6 %copy-start.27 = (f32[21]{0:T(128)S(1)}, f32[21]{0:T(128)}, u32[]{:S(2)}) copy-start(f32[21]{0:T(128)} %param.23) | copy-start | bytes 256
  418.0 4.1 copy-start.10
  418.0 4.1 copy-start.18
Sparse Core Ops, SparseCore 0:
  28.9 48.0 all-gather.1
where the time goes:
time: 472 us; the launch traced here: 462 us
  other arithmetic  183 us (39%)
  blocking collectives  123 us (26%)
  local copies, waits for them, and re-layouts  87.2 us (18%)
  starting transfers between devices  39.6 us (8%)
  between operations  14.9 us (3%)
  waiting for transfers between devices  14.4 us (3%)
    div x11, other arithmetic, per_device(): (trim_margin(source_wide, depth, inner) + trim_margin(w_east, depth, inne...  119 us
    all_gather x2, blocking collectives, extend_deep(): lax.all_gather(block[:, tile_rows - depth:, :], 'lon', axis=2, tiled=True)  105 us
    scatter-add x1, other arithmetic, per_device(): jnp.zeros((channels, tile_rows * tile_cols), jnp.float32).at[:, cell_ids]  25.4 us
    all_to_all x1, blocking collectives, per_device(): lax.all_to_all(local_fit.reshape(1, channels, devices, slots), ('lat', 'l...  18.2 us
    ppermute x7, starting transfers between devices, with_halo(): lax.ppermute(lax.slice_in_dim(block, 0, width, axis=dim), axis, backward)  17.6 us
    all_gather x3, local copies, waits for them, and re-layouts, extend_deep(): lax.all_gather(block[:, tile_rows - depth:, :], 'lon', axis=2, tiled=True)  17.4 us
    gather x3, local copies, waits for them, and re-layouts, extend_deep(): ghost = jnp.take(top_rows, partner_wide, axis=2)[:, ::-1, :]  14.5 us
    gather x1, local copies, waits for them, and re-layouts, per_device(): local_fit = diffused.reshape(channels, -1)[:, cell_ids]  13.5 us
  transfers between devices with their start and end apart: 17, of which 2 were waited for; matrix products, arithmetic and copies ran while one was open for 19% of the time, Pallas kernels for 0%

commit v1 on v0

v1 whole, which is shorter than its diff:
```python
import functools

import jax
import jax.numpy as jnp
from jax import lax
from jax.experimental import pallas as pl
from jax.experimental.pallas import tpu as pltpu
from jax.sharding import PartitionSpec as P

LEV = 10
STEPS = 2
SWEEPS = 6
DEPTH = STEPS * SWEEPS
LANES = 128
SUB = 8
PER = LANES // DEPTH
VMEM_LIMIT = 40 * 1024 * 1024


def params(**extra):
    return pltpu.CompilerParams(vmem_limit_bytes=VMEM_LIMIT, **extra)


def lane_iota(shape):
    return lax.broadcasted_iota(jnp.int32, shape, len(shape) - 1)


def roll_lanes(x, shift):
    shift = shift % LANES
    return x if shift == 0 else pltpu.roll(x, shift, x.ndim - 1)


def pack_kernel(channels, padded, cols, count_ref, value_ref, cell_ref, out_ref):
    owners, slots = cell_ref.shape
    for c in range(channels):
        out_ref[pl.ds(c, owners, stride=padded), :] = value_ref[pl.ds(c * owners, owners), :]
    owner = lax.broadcasted_iota(jnp.int32, (owners, slots), 0)
    count = jnp.zeros((owners, slots), jnp.int32)
    for d in range(owners):
        count = jnp.where(owner == d, count_ref[0, d], count)
    cell = cell_ref[...].astype(jnp.float32)
    row = jnp.floor((cell + 0.5) * (1.0 / cols))
    col = cell - row * cols
    row = jnp.where(lane_iota((owners, slots)) < count, row, -1.0)
    out_ref[pl.ds(channels, owners, stride=padded), :] = row
    out_ref[pl.ds(channels + 1, owners, stride=padded), :] = col
    for c in range(channels + 2, padded):
        out_ref[pl.ds(c, owners, stride=padded), :] = jnp.zeros((owners, slots), jnp.float32)


def unpack_kernel(channels, padded, in_ref, out_ref):
    owners = out_ref.shape[1]
    for c in range(channels):
        out_ref[c] = in_ref[pl.ds(c, owners, stride=padded), :]


def pack_strip(read, count, east, out_ref):
    for v in range(out_ref.shape[0]):
        total = None
        for s in range(min(PER, count - v * PER)):
            x = read(v * PER + s)
            x = roll_lanes(x, s * DEPTH + (DEPTH if east else 0))
            if total is None:
                total = x
            else:
                total = jnp.where(lane_iota(x.shape) >= s * DEPTH, x, total)
        out_ref[v] = total


def strip_count(rows):
    return -(-rows // PER)


def emit_strips(own_ref, west_ref, east_ref, top_ref, bottom_ref):
    rows, _, cols = own_ref.shape
    pack_strip(lambda j: own_ref[j, :, :LANES], rows, False, west_ref)
    pack_strip(lambda j: own_ref[j, :, cols - LANES :], rows, True, east_ref)
    top_ref[...] = own_ref[rows - DEPTH :]
    bottom_ref[...] = own_ref[:DEPTH]


def strip_shapes(rows, width, cols):
    strip = jax.ShapeDtypeStruct((strip_count(rows), width, LANES), jnp.float32)
    slab = jax.ShapeDtypeStruct((DEPTH, width, cols), jnp.float32)
    return (strip, strip, slab, slab)


def coef_kernel(bottom_ref, kappa_ref, own_ref, west_ref, east_ref, top_ref, low_ref):
    rows, cols = bottom_ref.shape
    part = lax.broadcasted_iota(jnp.int32, (SUB, cols), 0)
    bottom = bottom_ref[...].astype(jnp.float32)
    for j in range(rows):
        plane = jnp.where(
            part == 0,
            bottom[j : j + 1, :],
            jnp.where(part == 1, kappa_ref[0, j : j + 1, :], kappa_ref[1, j : j + 1, :]),
        )
        own_ref[j] = plane
    emit_strips(own_ref, west_ref, east_ref, top_ref, low_ref)


def ghost_kernel(where_ref, north_ref, first_ref, second_ref, south_ref, ghost_ref, west_ref, east_ref):
    depth, width, cols = north_ref.shape

    @pl.when(where_ref[0] == 1)
    def _():
        source = lax.broadcasted_iota(jnp.int32, (cols, cols), 0)
        target = lax.broadcasted_iota(jnp.int32, (cols, cols), 1)
        near = (source == where_ref[1] - target).astype(jnp.float32)
        far = (source == where_ref[1] - target + cols).astype(jnp.float32)
        first = first_ref[...].reshape(depth * width, cols)
        second = second_ref[...].reshape(depth * width, cols)
        dot = functools.partial(
            jnp.dot, preferred_element_type=jnp.float32, precision=lax.Precision.HIGHEST
        )
        mirrored = (dot(first, near) + dot(second, far)).reshape(depth, width, cols)
        for j in range(depth):
            ghost_ref[j] = mirrored[depth - 1 - j]

    @pl.when(where_ref[0] == 0)
    def _():
        ghost_ref[...] = north_ref[...]

    def read(lo):
        return lambda j: (
            south_ref[j, :, lo : lo + LANES] if j < depth else ghost_ref[j - depth, :, lo : lo + LANES]
        )

    pack_strip(read(0), 2 * depth, False, west_ref)
    pack_strip(read(cols - LANES), 2 * depth, True, east_ref)


def with_halo(own, west, east, top, low, centre_tile, where, n_lat, n_lon):
    width, cols = own.shape[1:]
    to_east = [(i, (i + 1) % n_lon) for i in range(n_lon)]
    to_west = [(b, a) for a, b in to_east]
    to_north = [(i, i + 1) for i in range(n_lat - 1)]
    to_south = [(b, a) for a, b in to_north]
    west_halo = lax.ppermute(east, "lon", to_east)
    east_halo = lax.ppermute(west, "lon", to_west)
    south = lax.ppermute(top, "lat", to_north)
    north = lax.ppermute(low, "lat", to_south)
    first_dev = (n_lat - 1) * n_lon

    def fold(tile):
        def send(block):
            return tuple(
                lax.ppermute(
                    block,
                    ("lat", "lon"),
                    [(first_dev + s, first_dev + (tile - part - s) % n_lon) for s in range(n_lon)],
                )
                for part in (0, 1)
            )

        return send

    first, second = lax.switch(centre_tile, [fold(t) for t in range(n_lon)], top)
    corner = jax.ShapeDtypeStruct((strip_count(2 * DEPTH), width, LANES), jnp.float32)
    vmem = pl.BlockSpec(memory_space=pltpu.VMEM)
    ghost, corner_west, corner_east = pl.pallas_call(
        ghost_kernel,
        out_shape=(jax.ShapeDtypeStruct((DEPTH, width, cols), jnp.float32), corner, corner),
        in_specs=[pl.BlockSpec(memory_space=pltpu.SMEM)] + [vmem] * 4,
        out_specs=(vmem,) * 3,
        compiler_params=params(),
        name="north_ghost",
    )(where, north, first, second, south)
    corner_w = lax.ppermute(corner_east, "lon", to_east)
    corner_e = lax.ppermute(corner_west, "lon", to_west)
    return (own, south, ghost, west_halo, east_halo, corner_w, corner_e)


def tile_starts(cols):
    count = max(1, -(-cols // (LANES - 2 * DEPTH)))
    if count == 1:
        return [-DEPTH]
    span = cols + 2 * DEPTH - LANES
    return [-DEPTH + (k * span) // (count - 1) for k in range(count)]


def tile_bounds(cols):
    starts = tile_starts(cols)
    inner = [
        (starts[k] + LANES - DEPTH + starts[k + 1] + DEPTH) // 2 for k in range(len(starts) - 1)
    ]
    return [0] + inner + [cols]


def tile_row(j, start, refs):
    own_ref, south_ref, north_ref, west_ref, east_ref, corner_w_ref, corner_e_ref = refs
    rows, _, cols = own_ref.shape
    if j < DEPTH:
        body, at, west, east, s = south_ref, j, corner_w_ref, corner_e_ref, j
    elif j < DEPTH + rows:
        body, at, west, east, s = own_ref, j - DEPTH, west_ref, east_ref, j - DEPTH
    else:
        at = j - DEPTH - rows
        body, west, east, s = north_ref, corner_w_ref, corner_e_ref, at + DEPTH
    out = None
    for m in range(-(-cols // LANES)):
        lo, hi = max(0, m * LANES - start), min(LANES, (m + 1) * LANES - start)
        if lo >= hi:
            continue
        piece = roll_lanes(body[at, :, m * LANES : (m + 1) * LANES], m * LANES - start)
        out = piece if out is None else jnp.where(lane_iota(piece.shape) >= lo, piece, out)
    if start < 0:
        piece = roll_lanes(west[s // PER], -start - DEPTH - (s % PER) * DEPTH)
        out = jnp.where(lane_iota(out.shape) < -start, piece, out)
    if start + LANES > cols:
        piece = roll_lanes(east[s // PER], cols - start - (s % PER) * DEPTH)
        out = jnp.where(lane_iota(out.shape) >= cols - start, piece, out)
    return out


def channel_vector(ref, group, fill):
    sub = lax.broadcasted_iota(jnp.int32, (SUB, LANES), 0)
    out = jnp.full((SUB, LANES), fill, jnp.float32)
    for s in range(SUB):
        c = group * SUB + s
        if c < ref.shape[0]:
            out = jnp.where(sub == s, ref[c], out)
    return out


def channel_level(group):
    c = lax.broadcasted_iota(jnp.int32, (SUB, LANES), 0) + group * SUB
    level = jnp.where(c < LEV, c, jnp.where(c < 2 * LEV, c - LEV, jnp.where(c == 2 * LEV, 0, LEV)))
    return level.astype(jnp.float32)


def weight_kernel(starts, groups, scale_ref, sigma_ref, *refs):
    halo_refs, (be_ref, bn_ref, q_ref, r_ref, ext_ref) = refs[:7], refs[7:]
    total = ext_ref.shape[0]
    tile = pl.program_id(0)
    for k, start in enumerate(starts):

        @pl.when(tile == k)
        def _():
            for j in range(total):
                ext_ref[j] = tile_row(j, start, halo_refs)

    levels = [channel_level(g) for g in range(groups)]
    scales = [channel_vector(scale_ref, g, 0.0) for g in range(groups)]
    sigmas = [channel_vector(sigma_ref, g, 0.0) for g in range(groups)]

    def spread(x, part):
        return jnp.broadcast_to(x[part : part + 1, :], (SUB, LANES))

    below = [jnp.zeros((SUB, LANES), jnp.float32)] * groups
    root_below = [None] * groups
    x = ext_ref[0]
    for j in range(total):
        x_north = ext_ref[j + 1] if j + 1 < total else None
        x_east = roll_lanes(x, -1)
        bottom = spread(x, 0)
        bottom_e = spread(jnp.minimum(x, x_east), 0)
        kappa_e = spread(0.5 * (x + x_east), 1)
        if x_north is not None:
            bottom_n = spread(jnp.minimum(x, x_north), 0)
            kappa_n = spread(0.5 * (x + x_north), 2)
        for g in range(groups):
            a_e = jnp.where(levels[g] < bottom_e, scales[g] * kappa_e, 0.0)
            if x_north is not None:
                a_n = jnp.where(levels[g] < bottom_n, scales[g] * kappa_n, 0.0)
            else:
                a_n = jnp.zeros((SUB, LANES), jnp.float32)
            d = 1.0 + a_e + roll_lanes(a_e, 1) + a_n + below[g]
            root = lax.rsqrt(d)
            root = root * (1.5 - 0.5 * d * root * root)
            r_ref[0, g, j] = root
            be_ref[0, g, j] = a_e * root * roll_lanes(root, -1)
            q_ref[0, g, j] = jnp.where(levels[g] < bottom, sigmas[g] * (d * root), 0.0)
            if j > 0:
                bn_ref[0, g, j - 1] = below[g] * root_below[g] * root
            below[g] = a_n
            root_below[g] = root
        x = x_north
    for g in range(groups):
        bn_ref[0, g, total - 1] = jnp.zeros((SUB, LANES), jnp.float32)


def weights(halo, length_scale, sigma, groups):
    rows, _, cols = halo[0].shape
    starts = tile_starts(cols)
    total = rows + 2 * DEPTH
    vmem = pl.BlockSpec(memory_space=pltpu.VMEM)
    smem = pl.BlockSpec(memory_space=pltpu.SMEM)
    shape = jax.ShapeDtypeStruct((len(starts), groups, total, SUB, LANES), jnp.float32)
    block = pl.BlockSpec((1, groups, total, SUB, LANES), lambda k: (k, 0, 0, 0, 0))
    cells = rows * cols * groups * SUB
    return pl.pallas_call(
        functools.partial(weight_kernel, starts, groups),
        grid=(len(starts),),
        out_shape=(shape,) * 4,
        in_specs=[smem, smem] + [vmem] * 7,
        out_specs=(block,) * 4,
        scratch_shapes=[pltpu.VMEM((total, SUB, LANES), jnp.float32)],
        compiler_params=params(),
        cost_estimate=pl.CostEstimate(flops=20 * cells, bytes_accessed=24 * cells, transcendentals=cells),
        name="weights",
    )(length_scale, sigma, *halo)


def split(x):
    high = x.astype(jnp.bfloat16)
    low = (x - high.astype(jnp.float32)).astype(jnp.bfloat16)
    return high, low


def scatter_kernel(channels, chunk, obs_ref, own_ref, west_ref, east_ref, top_ref, low_ref, left_ref, right_ref, sum_ref):
    senders, padded, slots = obs_ref.shape
    rows, _, cols = own_ref.shape
    row_iota = lax.broadcasted_iota(jnp.int32, (rows, slots), 0).astype(jnp.float32)
    col_iota = lax.broadcasted_iota(jnp.int32, (cols, slots), 0).astype(jnp.float32)

    def body(step, carry):
        for s in range(chunk):
            x = obs_ref[step * chunk + s]
            high, low = split(x)
            on_row = (row_iota == x[channels : channels + 1, :]).astype(jnp.bfloat16)
            on_col = (col_iota == x[channels + 1 : channels + 2, :]).astype(jnp.bfloat16)
            at = s * 2 * slots
            right_ref[:, at : at + slots] = on_col
            right_ref[:, at + slots : at + 2 * slots] = on_col
            for c in range(padded):
                left_ref[c * rows : (c + 1) * rows, at : at + slots] = on_row * high[c : c + 1, :]
                left_ref[c * rows : (c + 1) * rows, at + slots : at + 2 * slots] = on_row * low[c : c + 1, :]
        part = lax.dot_general(
            left_ref[...], right_ref[...], (((1,), (1,)), ((), ())), preferred_element_type=jnp.float32
        )
        for m in range(cols // LANES):
            piece = part[:, m * LANES : (m + 1) * LANES]

            @pl.when(step == 0)
            def _():
                sum_ref[m] = piece

            @pl.when(step > 0)
            def _():
                sum_ref[m] += piece

        return carry

    lax.fori_loop(0, senders // chunk, body, 0)
    for m in range(cols // LANES):
        for g in range(padded // SUB):
            for j in range(rows):
                own_ref[j, g * SUB : (g + 1) * SUB, m * LANES : (m + 1) * LANES] = sum_ref[
                    m, pl.ds(g * SUB * rows + j, SUB, stride=rows), :
                ]
    emit_strips(own_ref, west_ref, east_ref, top_ref, low_ref)


def scatter(obs, channels, rows, cols):
    senders, padded, slots = obs.shape
    chunk = 8 if senders % 8 == 0 else 1
    vmem = pl.BlockSpec(memory_space=pltpu.VMEM)
    own = jax.ShapeDtypeStruct((rows, padded, cols), jnp.float32)
    return pl.pallas_call(
        functools.partial(scatter_kernel, channels, chunk),
        out_shape=(own,) + strip_shapes(rows, padded, cols),
        in_specs=[vmem],
        out_specs=(vmem,) * 5,
        scratch_shapes=[
            pltpu.VMEM((padded * rows, chunk * 2 * slots), jnp.bfloat16),
            pltpu.VMEM((cols, chunk * 2 * slots), jnp.bfloat16),
            pltpu.VMEM((cols // LANES, padded * rows, LANES), jnp.float32),
        ],
        compiler_params=params(),
        name="scatter",
    )(obs)


def sweep_kernel(starts, bounds, sigma_ref, be_ref, bn_ref, q_ref, r_ref, *refs):
    halo_refs = refs[:7]
    fine_ref, out_ref, source_ref, even_ref, odd_ref, turn_ref = refs[7:]
    rows, _, cols = halo_refs[0].shape
    total = rows + 2 * DEPTH
    group, tile = pl.program_id(0), pl.program_id(1)
    for k, start in enumerate(starts):

        @pl.when(tile == k)
        def _():
            for j in range(total):
                even_ref[j] = tile_row(j, start, halo_refs) * q_ref[0, 0, j]

    state, other = even_ref, odd_ref
    done = 0
    for step in range(STEPS):
        for j in range(done, total - done):
            root = r_ref[0, 0, j]
            source_ref[j] = state[j] * (root * root)
        for _sweep in range(SWEEPS):
            done += 1
            here = state[done]
            south = bn_ref[0, 0, done - 1] * state[done - 1]
            for j in range(done, total - done):
                north = state[j + 1]
                to_e = be_ref[0, 0, j]
                to_n = bn_ref[0, 0, j]
                new = source_ref[j] + south + to_n * north
                new = new + (to_e * roll_lanes(here, -1) + roll_lanes(to_e * here, 1))
                other[j] = new
                south = to_n * here
                here = north
            state, other = other, state

    sub = lax.broadcasted_iota(jnp.int32, (SUB, LANES), 0) + group * SUB
    spread = jnp.zeros((SUB, LANES), jnp.float32)
    for c in range(sigma_ref.shape[0]):
        spread = jnp.where(sub == c, sigma_ref[c], spread)
    for j in range(rows):
        state[j + DEPTH] = state[j + DEPTH] * (spread * r_ref[0, 0, j + DEPTH])
    for k, start in enumerate(starts):

        @pl.when(tile == k)
        def _():
            for m in range(cols // LANES):
                lo = max(bounds[k] - m * LANES, 0)
                hi = min(bounds[k + 1] - m * LANES, LANES)
                if lo >= hi:
                    continue
                lane = lane_iota((SUB, LANES))
                for j in range(rows):
                    piece = roll_lanes(state[j + DEPTH], start - m * LANES)
                    if lo > 0:
                        piece = jnp.where(lane >= lo, piece, fine_ref[j, :, m * LANES : (m + 1) * LANES])
                    fine_ref[j, :, m * LANES : (m + 1) * LANES] = piece

    @pl.when(tile == len(starts) - 1)
    def _():
        for m in range(cols // LANES):
            for j in range(rows):
                turn_ref[pl.ds(j, SUB, stride=rows), :] = fine_ref[j, :, m * LANES : (m + 1) * LANES]
            for s in range(SUB):
                out_ref[s, :, m * LANES : (m + 1) * LANES] = turn_ref[s * rows : (s + 1) * rows, :]


def sweeps(halo, weight, sigma, channels):
    own = halo[0]
    rows, padded, cols = own.shape
    starts, bounds = tile_starts(cols), tile_bounds(cols)
    total = rows + 2 * DEPTH
    groups = padded // SUB

    def side(x):
        return pl.BlockSpec((x.shape[0], SUB, x.shape[2]), lambda g, k: (0, g, 0))

    block = pl.BlockSpec((1, 1, total, SUB, LANES), lambda g, k: (k, g, 0, 0, 0))
    scratch = pltpu.VMEM((total, SUB, LANES), jnp.float32)
    return pl.pallas_call(
        functools.partial(sweep_kernel, starts, bounds),
        grid=(groups, len(starts)),
        out_shape=(
            jax.ShapeDtypeStruct((rows, padded, cols), jnp.float32),
            jax.ShapeDtypeStruct((channels, rows, cols), jnp.float32),
        ),
        in_specs=[pl.BlockSpec(memory_space=pltpu.SMEM)] + [block] * 4 + [side(x) for x in halo],
        out_specs=(
            pl.BlockSpec((rows, SUB, cols), lambda g, k: (0, g, 0)),
            pl.BlockSpec((SUB, rows, cols), lambda g, k: (g, 0, 0)),
        ),
        scratch_shapes=[scratch, scratch, scratch, pltpu.VMEM((SUB * rows, LANES), jnp.float32)],
        compiler_params=params(),
        name="sweeps",
    )(sigma, *weight, *halo)


def gather_kernel(channels, pair, fine_ref, obs_ref, out_ref, left_ref):
    senders, padded, slots = out_ref.shape
    rows, _, cols = fine_ref.shape
    high, low = split(fine_ref[...].reshape(rows * padded, cols))
    left_ref[:, :cols] = high
    left_ref[:, cols:] = low
    at_row, at_col = channels % SUB, (channels + 1) % SUB
    col_iota = lax.broadcasted_iota(jnp.int32, (cols, slots), 0).astype(jnp.float32)

    def body(step, carry):
        hots = []
        for s in range(pair):
            col = obs_ref[step * pair + s, at_col : at_col + 1, :]
            hots.append((col_iota == col).astype(jnp.bfloat16))
        hot = jnp.concatenate(hots, axis=1)
        found = jnp.dot(
            left_ref[...], jnp.concatenate([hot, hot], axis=0), preferred_element_type=jnp.float32
        )
        for s in range(pair):
            row = jnp.broadcast_to(obs_ref[step * pair + s, at_row : at_row + 1, :], (padded, slots))
            total = jnp.zeros((padded, slots), jnp.float32)
            for j in range(rows):
                piece = found[j * padded : (j + 1) * padded, s * slots : (s + 1) * slots]
                total = jnp.where(row == float(j), piece, total)
            out_ref[step * pair + s] = total
        return carry

    lax.fori_loop(0, senders // pair, body, 0)


def gather(fine, obs, channels):
    rows, padded, cols = fine.shape
    senders, _, slots = obs.shape
    pair = 2 if senders % 2 == 0 else 1
    where_group = channels // SUB
    vmem = pl.BlockSpec(memory_space=pltpu.VMEM)
    return pl.pallas_call(
        functools.partial(gather_kernel, channels, pair),
        grid=(1,),
        out_shape=jax.ShapeDtypeStruct((senders, padded, slots), jnp.float32),
        in_specs=[
            pl.BlockSpec((rows, padded, cols), lambda i: (0, 0, 0)),
            pl.BlockSpec((senders, SUB, slots), lambda i: (0, where_group, 0)),
        ],
        out_specs=pl.BlockSpec((senders, padded, slots), lambda i: (0, 0, 0)),
        scratch_shapes=[pltpu.VMEM((rows * padded, 2 * cols), jnp.bfloat16)],
        compiler_params=params(),
        name="gather",
    )(fine, obs)


def per_device(
    obs_value, obs_cell, obs_count, bottom_level, diffusivity, partner, length_scale, sigma
):
    _, channels, owners, slots = obs_value.shape
    rows, cols = bottom_level.shape
    n_lat, n_lon = lax.axis_size("lat"), lax.axis_size("lon")
    padded = -(-(channels + 2) // SUB) * SUB
    vmem = pl.BlockSpec(memory_space=pltpu.VMEM)
    smem = pl.BlockSpec(memory_space=pltpu.SMEM)

    outgoing = pl.pallas_call(
        functools.partial(pack_kernel, channels, padded, cols),
        out_shape=jax.ShapeDtypeStruct((owners * padded, slots), jnp.float32),
        in_specs=[smem, vmem, vmem],
        out_specs=vmem,
        compiler_params=params(),
        name="pack",
    )(obs_count, obs_value.reshape(channels * owners, slots), obs_cell[0])
    arrived = lax.all_to_all(
        outgoing.reshape(owners, padded, slots), ("lat", "lon"), split_axis=0, concat_axis=0, tiled=True
    )

    n_cols = cols * n_lon
    centre = lax.rem(partner[0] + lax.axis_index("lon") * cols, n_cols)
    centre_tile, centre_col = centre // cols, centre % cols
    is_top = (lax.axis_index("lat") == n_lat - 1).astype(jnp.int32)
    where = jnp.stack([is_top, centre_col])
    around = functools.partial(
        with_halo, centre_tile=centre_tile, where=where, n_lat=n_lat, n_lon=n_lon
    )

    coef = pl.pallas_call(
        coef_kernel,
        out_shape=(jax.ShapeDtypeStruct((rows, SUB, cols), jnp.float32),) + strip_shapes(rows, SUB, cols),
        in_specs=[vmem] * 2,
        out_specs=(vmem,) * 5,
        compiler_params=params(),
        name="coefficients",
    )(bottom_level, diffusivity)
    weight = weights(around(*coef), length_scale, sigma, padded // SUB)

    field = around(*scatter(arrived, channels, rows, cols))
    fine, diffused = sweeps(field, weight, sigma, channels)
    local_fit = gather(fine, arrived, channels)
    returned = lax.all_to_all(local_fit, ("lat", "lon"), split_axis=0, concat_axis=0, tiled=True)
    obs_fit = pl.pallas_call(
        functools.partial(unpack_kernel, channels, padded),
        out_shape=jax.ShapeDtypeStruct((channels, owners, slots), jnp.float32),
        in_specs=[vmem],
        out_specs=vmem,
        compiler_params=params(),
        name="unpack",
    )(returned.reshape(owners * padded, slots))
    return obs_fit[None], diffused


def solution(mesh):
    return jax.shard_map(
        per_device,
        mesh=mesh,
        in_specs=(
            P(("lat", "lon"), None, None, None),
            P(("lat", "lon"), None, None),
            P(("lat", "lon"), None),
            P("lat", "lon"),
            P(None, "lat", "lon"),
            P("lon"),
            P(),
            P(),
        ),
        out_specs=(P(("lat", "lon"), None, None, None), P(None, "lat", "lon")),
        check_vma=False,
    )
```

time: 472 us -> 152 us (0.32); the launches traced: 462 us -> 150 us
  other arithmetic: 183 us -> 0.07 us
  local copies, waits for them, and re-layouts: 87.2 us -> 5.24 us
  blocking collectives: 123 us -> 51.1 us
  Pallas kernels: 0 us -> 54.4 us
  between operations: 14.9 us -> 1.52 us
  starting transfers between devices: 39.6 us -> 27.9 us
    div x11 -> x0, other arithmetic: 119 us -> none  [per_device(): (trim_margin(source_wide, depth, inner) + trim_margin(w_east, depth, inne...]
    all_gather x2 -> x0, blocking collectives: 105 us -> none  [extend_deep(): lax.all_gather(block[:, tile_rows - depth:, :], 'lon', axis=2, tiled=True)]
    pallas_call x0 -> x9, Pallas kernels: none -> 54.4 us  [the longest x1 21.7 us: sweeps(): pl.pallas_call(functools.partial(sweep_kernel, starts, bounds), grid=(gro...]
    all_to_all x1 -> x2, blocking collectives: 18.2 us -> 51.1 us  [the longest x1 30.5 us: per_device(): lax.all_to_all(local_fit, ('lat', 'lon'), split_axis=0, concat_axis=0, ti...]
    gather x4 -> x0, local copies, waits for them, and re-layouts: 28.1 us -> none  [the longest x3 14.5 us: extend_deep(): ghost = jnp.take(top_rows, partner_wide, axis=2)[:, ::-1, :]]
    scatter-add x1 -> x0, other arithmetic: 25.4 us -> none  [per_device(): jnp.zeros((channels, tile_rows * tile_cols), jnp.float32).at[:, cell_ids]]
    all_gather x3 -> x0, local copies, waits for them, and re-layouts: 17.4 us -> none  [extend_deep(): lax.all_gather(block[:, tile_rows - depth:, :], 'lon', axis=2, tiled=True)]
    all_to_all x2 -> x0, waiting for transfers between devices: 12 us -> none  [the longest x1 12 us: per_device(): lax.all_to_all(outgoing, ('lat', 'lon'), split_axis=2, concat_axis=2, til...]
  transfers between devices with their start and end apart: 17 -> 16, of which waited for: 2 -> 2; matrix products, arithmetic and copies ran while one was open for 19% -> 1% of each run, Pallas kernels for 0% -> 11%
where the time goes in v1:
time: 152 us; the launch traced here: 150 us
  Pallas kernels  54.4 us (36%)
  blocking collectives  51.1 us (34%)
  starting transfers between devices  27.9 us (18%)
  waiting for transfers between devices  10.1 us (7%)
  local copies, waits for them, and re-layouts  5.24 us (3%)
  between operations  1.52 us (1%)
    all_to_all x1, blocking collectives, per_device(): lax.all_to_all(local_fit, ('lat', 'lon'), split_axis=0, concat_axis=0, ti...  30.5 us
    pallas_call x1, Pallas kernels, sweeps(): pl.pallas_call(functools.partial(sweep_kernel, starts, bounds), grid=(gro...  21.7 us
    all_to_all x1, blocking collectives, per_device(): lax.all_to_all(outgoing.reshape(owners, padded, slots), ('lat', 'lon'), s...  20.6 us
    pallas_call x1, Pallas kernels, weights(): pl.pallas_call(functools.partial(weight_kernel, starts, groups), grid=(le...  13.4 us
    ppermute x2, starting transfers between devices, with_halo(): east_halo = lax.ppermute(west, 'lon', to_west)  8.16 us
    pallas_call x1, Pallas kernels, scatter(): pl.pallas_call(functools.partial(scatter_kernel, channels, chunk), out_sh...  7.7 us
    pallas_call x1, Pallas kernels, gather(): pl.pallas_call(functools.partial(gather_kernel, channels, pair), grid=(1,...  7.67 us
    ppermute x2, waiting for transfers between devices, with_halo(): corner_w = lax.ppermute(corner_east, 'lon', to_east)  6.38 us
  transfers between devices with their start and end apart: 16, of which 2 were waited for; matrix products, arithmetic and copies ran while one was open for 1% of the time, Pallas kernels for 11%

profile of v1, /device:TPU:0, one launch (start us, length us, event | category | flops | bytes accessed | tf_op | source)
XLA Modules:
  0.0 150.4 jit_solution(5451289408002837645)
XLA Ops:
  0.6 0.0 copy-start.4
  0.6 0.0 copy-start.6
  0.7 0.0 copy-start
  0.7 1.0 copy-done
  1.6 0.0 copy-start.3
  1.6 0.7 copy-done.3
  2.4 0.0 copy-start.5
  2.4 0.7 copy-done.5
  3.0 0.6 pack.1
  3.6 20.6 %all_to_all.10.obs_ref = f32[32,24,128]{2,1,0:T(8,128)S(1)} all-to-all(f32[32,24,128]{2,1,0:T(8,128)S(1)} %bitcast.9), channel_id=1, replica_groups=mesh['lat'=4,'lon'=8] {'lat','lon'}, dimensions={0} | all-to-all | bytes 786432 | tf_op jit(solution)/shard_map/all_to_all | solution.py:539
  24.3 7.7 %scatter.1 = (f32[48,24,256]{2,1,0:T(8,128)S(1)}, f32[5,24,128]{2,1,0:T(8,128)S(1)}, f32[5,24,128]{2,1,0:T(8,128)S(1)}, f32[12,24,256]{2,1,0:T(8,128)}, f32[12,24,256]{2,1,0:T(8,128)S(1)}) custom-call(f32[32,24,128]{2,1,0:T(8,128)S(1)} %all_to_all.10.obs_ref), custom_call_target="tpu_custom_call" | custom-call | tf_op jit(solution)/shard_map/scatter/pallas_call | solution.py:360
  32.0 1.3 collective-permute-start.39
  33.3 3.0 %collective-permute-start.38 = (f32[12,24,256]{2,1,0:T(8,128)}, f32[12,24,256]{2,1,0:T(8,128)S(1)}, u32[]{:S(2)}, u32[]{:S(2)}) collective-permute-start(f32[12,24,256]{2,1,0:T(8,128)} %get-tuple-element.59), channel_id=1, source_target_pairs={{0,8},{8,16},{16,24},{1,9},{9,17},{17,25},{2,10},{10,18},{18,26},{... | collective-permute-start | bytes 884744 | tf_op jit(solution)/shard_map/ppermute | solution.py:141
  36.3 0.0 copy-start.1
  36.3 0.9 copy-done.1
  37.2 0.0 copy-start.2
  37.2 0.8 copy-done.2
  38.0 0.2 coefficients.1
  38.2 0.9 collective-permute-start.34
  39.1 1.2 slice.3
  41.0 2.6 %conditional.2 = (f32[12,8,256]{2,1,0:T(8,128)}, f32[12,8,256]{2,1,0:T(8,128)}) conditional(s32[]{:T(128)} %clamp.4, f32[12,8,256]{2,1,0:T(8,128)S(1)} %get-tuple-element.45, f32[12,8,256]{2,1,0:T(8,128)S(1)} %get-tuple-element.45, f32[12,8,256]{2,1,0:T(8,128)S(1)} %get-tuple-element.45, ...), branch_computations={%region_0.1_spmd, %region_1.2_spmd, %region_2.3_spmd, %region_3.4_... | conditional | bytes 786528 | solution.py:158
  41.0 1.3 collective-permute-start.11
  42.3 1.3 collective-permute-start.10
  43.6 0.0 collective-permute-done.11
  43.6 0.0 collective-permute-done.10
  43.6 2.8 %conditional.3 = (f32[12,24,256]{2,1,0:T(8,128)}, f32[12,24,256]{2,1,0:T(8,128)}) conditional(s32[]{:T(128)} %clamp.4, f32[12,24,256]{2,1,0:T(8,128)} %get-tuple-element.59, f32[12,24,256]{2,1,0:T(8,128)} %get-tuple-element.59, f32[12,24,256]{2,1,0:T(8,128)} %get-tuple-element.59, ...), branch_computations={%region_8.9_spmd, %region_9.10_spmd, %region_10.11_spmd, %region_1... | conditional | bytes 2359392 | solution.py:158
  43.6 1.4 collective-permute-start.27
  45.0 1.4 collective-permute-start.26
  46.4 0.0 collective-permute-done.27
  46.4 0.0 collective-permute-done.26
  46.4 3.0 %collective-permute-start.32 = (f32[12,8,256]{2,1,0:T(8,128)S(1)}, f32[12,8,256]{2,1,0:T(8,128)S(1)}, u32[]{:S(2)}, u32[]{:S(2)}) collective-permute-start(f32[12,8,256]{2,1,0:T(8,128)S(1)} %get-tuple-element.45), channel_id=1, source_target_pairs={{0,8},{8,16},{16,24},{1,9},{9,17},{17,25},{2,10},{10,18},{18,26},{... | collective-permute-start | bytes 294920 | tf_op jit(solution)/shard_map/ppermute | solution.py:141
  49.4 3.5 %collective-permute-start.35 = (f32[5,8,128]{2,1,0:T(8,128)S(1)}, f32[5,8,128]{2,1,0:T(8,128)S(1)}, u32[]{:S(2)}, u32[]{:S(2)}) collective-permute-start(f32[5,8,128]{2,1,0:T(8,128)S(1)} %get-tuple-element.51), channel_id=1, source_target_pairs={{1,0},{2,1},{3,2},{4,3},{5,4},{6,5},{7,6},{0,7},{9,8},{10,9},{11,1... | collective-permute-start | bytes 61448 | tf_op jit(solution)/shard_map/ppermute | solution.py:140
  52.8 0.0 collective-permute-done.34.refs_3_
  52.8 1.3 collective-permute-start.33
  54.1 0.0 collective-permute-done.39.north_ref
  54.1 0.1 collective-permute-start.40
  54.2 0.0 collective-permute-done.38.south_ref.refs_1_
  54.2 4.7 %collective-permute-start.41 = (f32[5,24,128]{2,1,0:T(8,128)S(1)}, f32[5,24,128]{2,1,0:T(8,128)S(1)}, u32[]{:S(2)}, u32[]{:S(2)}) collective-permute-start(f32[5,24,128]{2,1,0:T(8,128)S(1)} %get-tuple-element.65), channel_id=1, source_target_pairs={{1,0},{2,1},{3,2},{4,3},{5,4},{6,5},{7,6},{0,7},{9,8},{10,9},{11,1... | collective-permute-start | bytes 184328 | tf_op jit(solution)/shard_map/ppermute | solution.py:140
  58.9 0.1 pad_add_fusion.where_ref
  59.0 1.3 north_ghost.3
  60.3 0.0 collective-permute-done.33.north_ref
  60.3 0.1 collective-permute-start.42
  60.4 0.0 collective-permute-done.32.south_ref.refs_1_
  60.4 4.7 %collective-permute-start.43 = (f32[3,24,128]{2,1,0:T(8,128)S(1)}, f32[3,24,128]{2,1,0:T(8,128)S(1)}, u32[]{:S(2)}, u32[]{:S(2)}) collective-permute-start(f32[3,24,128]{2,1,0:T(8,128)S(1)} %get-tuple-element.67), channel_id=1, source_target_pairs={{1,0},{2,1},{3,2},{4,3},{5,4},{6,5},{7,6},{0,7},{9,8},{10,9},{11,1... | collective-permute-start | bytes 110600 | tf_op jit(solution)/shard_map/ppermute | solution.py:170
  65.1 1.1 north_ghost.2
  66.2 0.0 collective-permute-done.35.refs_4_
  66.2 0.1 collective-permute-start.36
  66.2 6.4 %collective-permute-done.36.refs_5_ = f32[3,8,128]{2,1,0:T(8,128)S(1)} collective-permute-done((f32[3,8,128]{2,1,0:T(8,128)S(1)}, f32[3,8,128]{2,1,0:T(8,128)S(1)}, u32[]{:S(2)}, u32[]{:S(2)}) %collective-permute-start.36) | collective-permute-done | bytes 12320 | tf_op jit(solution)/shard_map/ppermute | solution.py:169
  72.6 0.0 collective-permute-start.37
  72.6 3.7 %collective-permute-done.37.refs_6_ = f32[3,8,128]{2,1,0:T(8,128)S(1)} collective-permute-done((f32[3,8,128]{2,1,0:T(8,128)S(1)}, f32[3,8,128]{2,1,0:T(8,128)S(1)}, u32[]{:S(2)}, u32[]{:S(2)}) %collective-permute-start.37) | collective-permute-done | bytes 12320 | tf_op jit(solution)/shard_map/ppermute | solution.py:170
  76.3 0.0 copy-done.4
  76.3 0.0 copy-done.6
  76.3 13.4 %weights.1 = (f32[3,3,72,8,128]{4,3,2,1,0:T(8,128)S(1)}, f32[3,3,72,8,128]{4,3,2,1,0:T(8,128)S(1)}, f32[3,3,72,8,128]{4,3,2,1,0:T(8,128)S(1)}, f32[3,3,72,8,128]{4,3,2,1,0:T(8,128)S(1)}) custom-call(f32[21]{0:T(128)S(1)} %copy-done.6, f32[21]{0:T(128)S(1)} %copy-done.4, f32[48,8,256]{2,1,0:T(8,128)S(1)} %get-tuple-element.44.refs_0_, ...), custom_call_target="tpu_custom_call" | custom-call | flops 5898240 | bytes 7077888 | tf_op jit(solution)/shard_map/weights/pallas_call | solution.py:292
  89.7 0.0 collective-permute-done.40.refs_3_
  89.7 0.0 collective-permute-done.41.refs_4_
  89.7 0.0 collective-permute-done.42.refs_5_
  89.7 0.0 collective-permute-done.43.refs_6_
  89.7 21.7 %sweeps.1 = (f32[48,24,256]{2,1,0:T(8,128)S(1)}, f32[21,48,256]{2,1,0:T(8,128)}) custom-call(f32[21]{0:T(128)S(1)} %copy-done.4, f32[3,3,72,8,128]{4,3,2,1,0:T(8,128)S(1)} %get-tuple-element.54.be_ref, f32[3,3,72,8,128]{4,3,2,1,0:T(8,128)S(1)} %get-tuple-element.55.bn_ref, f32[3,3,72,8,128]{4,3,2,1,0:T(8,128)S(1)} %get-tuple-element.56.q_ref, ...), custom_call_target="tpu_custom_call" | custom-call | tf_op jit(solution)/shard_map/sweeps/pallas_call | solution.py:452
  111.4 7.7 %gather.1 = f32[32,24,128]{2,1,0:T(8,128)S(1)} custom-call(f32[48,24,256]{2,1,0:T(8,128)S(1)} %get-tuple-element.68.fine_ref, f32[32,24,128]{2,1,0:T(8,128)S(1)} %all_to_all.10.obs_ref), custom_call_target="tpu_custom_call" | custom-call | tf_op jit(solution)/shard_map/gather/pallas_call | solution.py:506
  119.1 30.5 %all_to_all.11 = f32[32,24,128]{2,1,0:T(8,128)S(1)} all-to-all(f32[32,24,128]{2,1,0:T(8,128)S(1)} %gather.1), channel_id=1, replica_groups=mesh['lat'=4,'lon'=8] {'lat','lon'}, dimensions={0} | all-to-all | bytes 786432 | tf_op jit(solution)/shard_map/all_to_all | solution.py:565
  149.6 0.8 unpack.1
Async XLA Ops:
  0.6 75.7 %copy-start.4 = (f32[21]{0:T(128)S(1)}, f32[21]{0:T(128)}, u32[]{:S(2)}) copy-start(f32[21]{0:T(128)} %sigma_ref.3) | copy-start | bytes 256
  0.6 75.7 %copy-start.6 = (f32[21]{0:T(128)S(1)}, f32[21]{0:T(128)}, u32[]{:S(2)}) copy-start(f32[21]{0:T(128)} %scale_ref.1) | copy-start | bytes 256
  0.7 1.0 copy-start
  1.6 0.7 copy-start.3
  2.4 0.7 copy-start.5
  32.0 22.1 %collective-permute-start.39 = (f32[12,24,256]{2,1,0:T(8,128)S(1)}, f32[12,24,256]{2,1,0:T(8,128)S(1)}, u32[]{:S(2)}, u32[]{:S(2)}) collective-permute-start(f32[12,24,256]{2,1,0:T(8,128)S(1)} %get-tuple-element.60), channel_id=1, source_target_pairs={{8,0},{16,8},{24,16},{9,1},{17,9},{25,17},{10,2},{18,10},{26,18},{... | collective-permute-start | bytes 884744 | tf_op jit(solution)/shard_map/ppermute | solution.py:142
  33.3 20.9 %collective-permute-start.38 = (f32[12,24,256]{2,1,0:T(8,128)}, f32[12,24,256]{2,1,0:T(8,128)S(1)}, u32[]{:S(2)}, u32[]{:S(2)}) collective-permute-start(f32[12,24,256]{2,1,0:T(8,128)} %get-tuple-element.59), channel_id=1, source_target_pairs={{0,8},{8,16},{16,24},{1,9},{9,17},{17,25},{2,10},{10,18},{18,26},{... | collective-permute-start | bytes 884744 | tf_op jit(solution)/shard_map/ppermute | solution.py:141
  36.3 0.9 copy-start.1
  37.2 0.8 copy-start.2
  38.2 14.6 %collective-permute-start.34 = (f32[5,8,128]{2,1,0:T(8,128)S(1)}, f32[5,8,128]{2,1,0:T(8,128)S(1)}, u32[]{:S(2)}, u32[]{:S(2)}) collective-permute-start(f32[5,8,128]{2,1,0:T(8,128)S(1)} %get-tuple-element.50), channel_id=1, source_target_pairs={{0,1},{1,2},{2,3},{3,4},{4,5},{5,6},{6,7},{7,0},{8,9},{9,10},{10,1... | collective-permute-start | bytes 61448 | tf_op jit(solution)/shard_map/ppermute | solution.py:139
  41.0 2.6 %collective-permute-start.11 = (f32[12,8,256]{2,1,0:T(8,128)S(1)}, f32[12,8,256]{2,1,0:T(8,128)}, u32[]{:S(2)}, u32[]{:S(2)}) collective-permute-start(f32[12,8,256]{2,1,0:T(8,128)S(1)} %param.5), channel_id=1, source_target_pairs={{24,28},{25,27},{26,26},{27,25},{28,24},{29,31},{30,30},{31,29}} | collective-permute-start | bytes 294920 | tf_op jit(solution)/shard_map/cond/branch_5_fun/ppermute | solution.py:148
  42.3 1.3 collective-permute-start.10
  43.6 2.8 %collective-permute-start.27 = (f32[12,24,256]{2,1,0:T(8,128)}, f32[12,24,256]{2,1,0:T(8,128)}, u32[]{:S(2)}, u32[]{:S(2)}) collective-permute-start(f32[12,24,256]{2,1,0:T(8,128)} %param.13), channel_id=1, source_target_pairs={{24,28},{25,27},{26,26},{27,25},{28,24},{29,31},{30,30},{31,29}} | collective-permute-start | bytes 884744 | tf_op jit(solution)/shard_map/cond/branch_5_fun/ppermute | solution.py:148
  45.0 1.4 collective-permute-start.26
  46.4 14.0 %collective-permute-start.32 = (f32[12,8,256]{2,1,0:T(8,128)S(1)}, f32[12,8,256]{2,1,0:T(8,128)S(1)}, u32[]{:S(2)}, u32[]{:S(2)}) collective-permute-start(f32[12,8,256]{2,1,0:T(8,128)S(1)} %get-tuple-element.45), channel_id=1, source_target_pairs={{0,8},{8,16},{16,24},{1,9},{9,17},{17,25},{2,10},{10,18},{18,26},{... | collective-permute-start | bytes 294920 | tf_op jit(solution)/shard_map/ppermute | solution.py:141
  49.4 16.8 %collective-permute-start.35 = (f32[5,8,128]{2,1,0:T(8,128)S(1)}, f32[5,8,128]{2,1,0:T(8,128)S(1)}, u32[]{:S(2)}, u32[]{:S(2)}) collective-permute-start(f32[5,8,128]{2,1,0:T(8,128)S(1)} %get-tuple-element.51), channel_id=1, source_target_pairs={{1,0},{2,1},{3,2},{4,3},{5,4},{6,5},{7,6},{0,7},{9,8},{10,9},{11,1... | collective-permute-start | bytes 61448 | tf_op jit(solution)/shard_map/ppermute | solution.py:140
  52.8 7.5 %collective-permute-start.33 = (f32[12,8,256]{2,1,0:T(8,128)S(1)}, f32[12,8,256]{2,1,0:T(8,128)S(1)}, u32[]{:S(2)}, u32[]{:S(2)}) collective-permute-start(f32[12,8,256]{2,1,0:T(8,128)S(1)} %get-tuple-element.46), channel_id=1, source_target_pairs={{8,0},{16,8},{24,16},{9,1},{17,9},{25,17},{10,2},{18,10},{26,18},{... | collective-permute-start | bytes 294920 | tf_op jit(solution)/shard_map/ppermute | solution.py:142
  54.1 35.6 %collective-permute-start.40 = (f32[5,24,128]{2,1,0:T(8,128)S(1)}, f32[5,24,128]{2,1,0:T(8,128)S(1)}, u32[]{:S(2)}, u32[]{:S(2)}) collective-permute-start(f32[5,24,128]{2,1,0:T(8,128)S(1)} %get-tuple-element.64), channel_id=1, source_target_pairs={{0,1},{1,2},{2,3},{3,4},{4,5},{5,6},{6,7},{7,0},{8,9},{9,10},{10,1... | collective-permute-start | bytes 184328 | tf_op jit(solution)/shard_map/ppermute | solution.py:139
  54.2 35.5 %collective-permute-start.41 = (f32[5,24,128]{2,1,0:T(8,128)S(1)}, f32[5,24,128]{2,1,0:T(8,128)S(1)}, u32[]{:S(2)}, u32[]{:S(2)}) collective-permute-start(f32[5,24,128]{2,1,0:T(8,128)S(1)} %get-tuple-element.65), channel_id=1, source_target_pairs={{1,0},{2,1},{3,2},{4,3},{5,4},{6,5},{7,6},{0,7},{9,8},{10,9},{11,1... | collective-permute-start | bytes 184328 | tf_op jit(solution)/shard_map/ppermute | solution.py:140
  60.3 29.4 %collective-permute-start.42 = (f32[3,24,128]{2,1,0:T(8,128)S(1)}, f32[3,24,128]{2,1,0:T(8,128)S(1)}, u32[]{:S(2)}, u32[]{:S(2)}) collective-permute-start(f32[3,24,128]{2,1,0:T(8,128)S(1)} %get-tuple-element.66), channel_id=1, source_target_pairs={{0,1},{1,2},{2,3},{3,4},{4,5},{5,6},{6,7},{7,0},{8,9},{9,10},{10,1... | collective-permute-start | bytes 110600 | tf_op jit(solution)/shard_map/ppermute | solution.py:169
  60.4 29.4 %collective-permute-start.43 = (f32[3,24,128]{2,1,0:T(8,128)S(1)}, f32[3,24,128]{2,1,0:T(8,128)S(1)}, u32[]{:S(2)}, u32[]{:S(2)}) collective-permute-start(f32[3,24,128]{2,1,0:T(8,128)S(1)} %get-tuple-element.67), channel_id=1, source_target_pairs={{1,0},{2,1},{3,2},{4,3},{5,4},{6,5},{7,6},{0,7},{9,8},{10,9},{11,1... | collective-permute-start | bytes 110600 | tf_op jit(solution)/shard_map/ppermute | solution.py:170
  66.2 6.4 %collective-permute-start.36 = (f32[3,8,128]{2,1,0:T(8,128)S(1)}, f32[3,8,128]{2,1,0:T(8,128)S(1)}, u32[]{:S(2)}, u32[]{:S(2)}) collective-permute-start(f32[3,8,128]{2,1,0:T(8,128)S(1)} %get-tuple-element.52), channel_id=1, source_target_pairs={{0,1},{1,2},{2,3},{3,4},{4,5},{5,6},{6,7},{7,0},{8,9},{9,10},{10,1... | collective-permute-start | bytes 36872 | tf_op jit(solution)/shard_map/ppermute | solution.py:169
  72.6 3.7 %collective-permute-start.37 = (f32[3,8,128]{2,1,0:T(8,128)S(1)}, f32[3,8,128]{2,1,0:T(8,128)S(1)}, u32[]{:S(2)}, u32[]{:S(2)}) collective-permute-start(f32[3,8,128]{2,1,0:T(8,128)S(1)} %get-tuple-element.53), channel_id=1, source_target_pairs={{1,0},{2,1},{3,2},{4,3},{5,4},{6,5},{7,6},{0,7},{9,8},{10,9},{11,1... | collective-permute-start | bytes 36872 | tf_op jit(solution)/shard_map/ppermute | solution.py:170

commit v2 on v0

v2 whole, which is shorter than its diff:
```python
import functools

import jax
import jax.numpy as jnp
from jax import lax
from jax.experimental import pallas as pl
from jax.experimental.pallas import tpu as pltpu
from jax.sharding import PartitionSpec as P

LEV = 10
STEPS = 2
SWEEPS = 6
DEPTH = STEPS * SWEEPS
LANES = 128
SUB = 8
PER = LANES // DEPTH
PHASES = 3
COEFS = 3
VMEM_LIMIT = 40 * 1024 * 1024


def params(limit=VMEM_LIMIT):
    return pltpu.CompilerParams(vmem_limit_bytes=limit)


def lane_iota(shape):
    return lax.broadcasted_iota(jnp.int32, shape, len(shape) - 1)


def roll_lanes(x, shift):
    shift = shift % LANES
    return x if shift == 0 else pltpu.roll(x, shift, x.ndim - 1)


def pack_kernel(channels, padded, cols, count_ref, value_ref, cell_ref, out_ref):
    owners, slots = cell_ref.shape
    for c in range(channels):
        out_ref[pl.ds(c, owners, stride=padded), :] = value_ref[pl.ds(c * owners, owners), :]
    owner = lax.broadcasted_iota(jnp.int32, (owners, slots), 0)
    count = jnp.zeros((owners, slots), jnp.int32)
    for d in range(owners):
        count = jnp.where(owner == d, count_ref[0, d], count)
    cell = cell_ref[...].astype(jnp.float32)
    row = jnp.floor((cell + 0.5) * (1.0 / cols))
    col = cell - row * cols
    row = jnp.where(lane_iota((owners, slots)) < count, row, -1.0)
    out_ref[pl.ds(channels, owners, stride=padded), :] = row
    out_ref[pl.ds(channels + 1, owners, stride=padded), :] = col
    for c in range(channels + 2, padded):
        out_ref[pl.ds(c, owners, stride=padded), :] = jnp.zeros((owners, slots), jnp.float32)


def unpack_kernel(channels, padded, in_ref, out_ref):
    owners = out_ref.shape[1]
    for c in range(channels):
        out_ref[c] = in_ref[pl.ds(c, owners, stride=padded), :]


def split(x):
    high = x.astype(jnp.bfloat16)
    low = (x - high.astype(jnp.float32)).astype(jnp.bfloat16)
    return high, low


def phase_matrix(cols, dtype):
    shape = (cols + LANES, PHASES * LANES)
    source = lax.broadcasted_iota(jnp.int32, shape, 0)
    target = lax.broadcasted_iota(jnp.int32, shape, 1)
    w = (target % LANES) * PHASES + target // LANES
    at = jnp.where(w < DEPTH, w + cols, jnp.where(w < DEPTH + cols, w - DEPTH, w))
    return jnp.where((source == at) & (w < cols + 2 * DEPTH), 1.0, 0.0).astype(dtype)


def plain_matrix(cols, dtype):
    shape = (PHASES * LANES, cols)
    source = lax.broadcasted_iota(jnp.int32, shape, 0)
    w = lax.broadcasted_iota(jnp.int32, shape, 1) + DEPTH
    return jnp.where(source == (w % PHASES) * LANES + w // PHASES, 1.0, 0.0).astype(dtype)


def moved(x, matrix, exact=False):
    dot = functools.partial(jnp.dot, preferred_element_type=jnp.float32)
    high, low = split(x)
    out = dot(high, matrix) + dot(low, matrix)
    if exact:
        rest = (x - high.astype(jnp.float32)) - low.astype(jnp.float32)
        out = out + dot(rest.astype(jnp.bfloat16), matrix)
    return out


def mirror_matrices(cols, centre_col):
    source = lax.broadcasted_iota(jnp.int32, (cols, cols), 0)
    target = lax.broadcasted_iota(jnp.int32, (cols, cols), 1)
    near = (source == centre_col - target).astype(jnp.float32).astype(jnp.bfloat16)
    far = (source == centre_col - target + cols).astype(jnp.float32).astype(jnp.bfloat16)
    return near, far


def strip_count(rows):
    return -(-rows // PER)


class Moves:
    def __init__(self, n_lat, n_lon, centre_tile):
        self.to_east = [(i, (i + 1) % n_lon) for i in range(n_lon)]
        self.to_west = [(b, a) for a, b in self.to_east]
        self.to_north = [(i, i + 1) for i in range(n_lat - 1)]
        self.to_south = [(b, a) for a, b in self.to_north]
        self.n_lon = n_lon
        self.first = (n_lat - 1) * n_lon
        self.centre_tile = centre_tile

    def east(self, x):
        return lax.ppermute(x, "lon", self.to_east)

    def west(self, x):
        return lax.ppermute(x, "lon", self.to_west)

    def north(self, x):
        return lax.ppermute(x, "lat", self.to_north)

    def south(self, x):
        return lax.ppermute(x, "lat", self.to_south)

    def fold(self, centre_half, slab, halves):
        def pairs(tile, part):
            return [
                (self.first + s, self.first + (tile - part - s) % self.n_lon) for s in range(self.n_lon)
            ]

        def branch(tile, half):
            def run(whole, left, right):
                return (
                    lax.ppermute(whole, ("lat", "lon"), pairs(tile, 1 - half)),
                    lax.ppermute((left, right)[half], ("lat", "lon"), pairs(tile, half)),
                )

            return run

        branches = [branch(t, h) for t in range(self.n_lon) for h in (0, 1)]
        return lax.switch(self.centre_tile * 2 + centre_half, branches, slab, *halves)


def scatter_kernel(channels, chunk, obs_ref, bottom_ref, kappa_ref, *refs):
    own_ref, top_ref, low_ref = refs[:3]
    half_refs, (left_ref, right_ref, sum_ref) = refs[3:-3], refs[-3:]
    senders, padded, slots = obs_ref.shape
    rows, _, cols = own_ref.shape
    row_iota = lax.broadcasted_iota(jnp.int32, (rows, slots), 0).astype(jnp.float32)
    col_iota = lax.broadcasted_iota(jnp.int32, (cols, slots), 0).astype(jnp.float32)

    def body(step, carry):
        for s in range(chunk):
            x = obs_ref[step * chunk + s]
            high, low = split(x)
            on_row = (row_iota == x[channels : channels + 1, :]).astype(jnp.bfloat16)
            on_col = (col_iota == x[channels + 1 : channels + 2, :]).astype(jnp.bfloat16)
            at = s * 2 * slots
            right_ref[:, at : at + slots] = on_col
            right_ref[:, at + slots : at + 2 * slots] = on_col
            for c in range(channels):
                left_ref[c * rows : (c + 1) * rows, at : at + slots] = on_row * high[c : c + 1, :]
                left_ref[c * rows : (c + 1) * rows, at + slots : at + 2 * slots] = on_row * low[c : c + 1, :]
        part = lax.dot_general(
            left_ref[...], right_ref[...], (((1,), (1,)), ((), ())), preferred_element_type=jnp.float32
        )
        for m in range(cols // LANES):
            piece = part[:, m * LANES : (m + 1) * LANES]

            @pl.when(step == 0)
            def _():
                sum_ref[m, : channels * rows] = piece

            @pl.when(step > 0)
            def _():
                sum_ref[m, : channels * rows] += piece

        return carry

    lax.fori_loop(0, senders // chunk, body, 0)
    coefs = [bottom_ref[...].astype(jnp.float32), kappa_ref[0], kappa_ref[1]]
    for m in range(cols // LANES):
        at = slice(m * LANES, (m + 1) * LANES)
        for i, coef in enumerate(coefs):
            sum_ref[m, (channels + i) * rows : (channels + i + 1) * rows] = coef[:, at]
        for g in range(padded // SUB):
            for j in range(rows):
                own_ref[j, g * SUB : (g + 1) * SUB, at] = sum_ref[
                    m, pl.ds(g * SUB * rows + j, SUB, stride=rows), :
                ]
        top_ref[m] = own_ref[rows - DEPTH :, :, at]
        half_refs[m][...] = own_ref[rows - DEPTH :, :, at]
        low_ref[m] = own_ref[:DEPTH, :, at]


def scatter(obs, bottom_level, diffusivity, channels):
    senders, padded, slots = obs.shape
    rows, cols = bottom_level.shape
    tiles = cols // LANES
    chunk = 8 if senders % 8 == 0 else 1
    vmem = pl.BlockSpec(memory_space=pltpu.VMEM)
    half = jax.ShapeDtypeStruct((DEPTH, padded, LANES), jnp.float32)
    slab = jax.ShapeDtypeStruct((tiles, DEPTH, padded, LANES), jnp.float32)
    shapes = [jax.ShapeDtypeStruct((rows, padded, cols), jnp.float32), slab, slab] + [half] * tiles
    return pl.pallas_call(
        functools.partial(scatter_kernel, channels, chunk),
        out_shape=tuple(shapes),
        in_specs=[vmem] * 3,
        out_specs=(vmem,) * len(shapes),
        scratch_shapes=[
            pltpu.VMEM((channels * rows, chunk * 2 * slots), jnp.bfloat16),
            pltpu.VMEM((cols, chunk * 2 * slots), jnp.bfloat16),
            pltpu.VMEM((tiles, padded * rows, LANES), jnp.float32),
        ],
        compiler_params=params(),
        cost_estimate=pl.CostEstimate(
            flops=4 * senders * slots * padded * rows * cols, bytes_accessed=0, transcendentals=0
        ),
        name="scatter",
    )(obs, bottom_level, diffusivity)


def pack_strip(read, count, east, out_ref):
    for v in range(out_ref.shape[0]):
        total = None
        for s in range(min(PER, count - v * PER)):
            x = roll_lanes(read(v * PER + s), s * DEPTH + (DEPTH if east else 0))
            total = x if total is None else jnp.where(lane_iota(x.shape) >= s * DEPTH, x, total)
        out_ref[v] = total


def ghost_kernel(where_ref, south_ref, own_ref, north_ref, whole_ref, part_ref, ghost_ref, west_ref, east_ref):
    tiles, depth, width, _ = ghost_ref.shape
    cols = tiles * LANES

    for half in (0, 1):

        @pl.when((where_ref[0] == 1) & (where_ref[1] // LANES == half))
        def _():
            near, far = mirror_matrices(cols, where_ref[1])
            whole = [whole_ref[m].reshape(depth * width, LANES) for m in range(tiles)]
            part = part_ref[...].reshape(depth * width, LANES)
            if half == 0:
                x, matrix = [part] + whole, jnp.concatenate([near[:LANES], far], axis=0)
            else:
                x, matrix = whole + [part], jnp.concatenate([near, far[LANES:]], axis=0)
            mirrored = moved(jnp.concatenate(x, axis=1), matrix, exact=True)
            for m in range(tiles):
                block = mirrored[:, m * LANES : (m + 1) * LANES].reshape(depth, width, LANES)
                for j in range(depth):
                    ghost_ref[m, j] = block[depth - 1 - j]

    @pl.when(where_ref[0] == 0)
    def _():
        ghost_ref[...] = north_ref[...]

    rows = own_ref.shape[0]

    def read(m):
        def at(j):
            if j < depth:
                return south_ref[m, j]
            if j >= depth + rows:
                return ghost_ref[m, j - depth - rows]
            return own_ref[j - depth, :, m * LANES : (m + 1) * LANES]

        return at

    pack_strip(read(0), rows + 2 * depth, False, west_ref)
    pack_strip(read(tiles - 1), rows + 2 * depth, True, east_ref)


def field_ghosts(where, south, own, north, whole, part):
    width = own.shape[1]
    count = own.shape[0] + 2 * DEPTH
    strip = jax.ShapeDtypeStruct((strip_count(count), width, LANES), jnp.float32)
    vmem = pl.BlockSpec(memory_space=pltpu.VMEM)
    return pl.pallas_call(
        ghost_kernel,
        out_shape=(jax.ShapeDtypeStruct(south.shape, jnp.float32), strip, strip),
        in_specs=[pl.BlockSpec(memory_space=pltpu.SMEM)] + [vmem] * 5,
        out_specs=(vmem,) * 3,
        compiler_params=params(),
        name="field_ghosts",
    )(where, south, own, north, whole, part)


def east_of(xs, m):
    return xs[m + 1] if m + 1 < PHASES else roll_lanes(xs[0], -1)


def west_of(xs, m):
    return xs[m - 1] if m > 0 else roll_lanes(xs[PHASES - 1], 1)


def cell_terms(first, wide_ref, cell_ref):
    total = wide_ref.shape[1] // SUB

    def coef(i, m, skip=0):
        return wide_ref[m, pl.ds(first + i + skip * SUB, total - skip, stride=SUB), :]

    lon = [coef(1, m) for m in range(PHASES)]
    bottom = [coef(0, m) for m in range(PHASES)]
    for m in range(PHASES):
        cell_ref[0, m] = bottom[m]
        cell_ref[1, m] = jnp.minimum(bottom[m], east_of(bottom, m))
        cell_ref[2, m] = 0.5 * (lon[m] + east_of(lon, m))
        cell_ref[3, m, : total - 1] = jnp.minimum(bottom[m][: total - 1], coef(0, m, 1))
        cell_ref[4, m, : total - 1] = 0.5 * (coef(2, m)[: total - 1] + coef(2, m, 1))
        cell_ref[3, m, total - 1 :] = jnp.zeros((1, LANES), jnp.float32)
        cell_ref[4, m, total - 1 :] = jnp.zeros((1, LANES), jnp.float32)


def make_weights(level, scale, sigma, cell_ref, wide_ref, be_ref, bn_ref, root_ref, state_ref):
    total = be_ref.shape[0]
    zero = jnp.zeros((SUB, LANES), jnp.float32)
    below, root_below = [zero] * PHASES, [zero] * PHASES
    for j in range(total):

        def spread(i, m):
            return jnp.broadcast_to(cell_ref[i, m, j : j + 1, :], (SUB, LANES))

        a_e = [jnp.where(level < spread(1, m), scale * spread(2, m), 0.0) for m in range(PHASES)]
        a_n = [jnp.where(level < spread(3, m), scale * spread(4, m), 0.0) for m in range(PHASES)]
        root = []
        for m in range(PHASES):
            d = 1.0 + a_e[m] + west_of(a_e, m) + a_n[m] + below[m]
            x = lax.rsqrt(d)
            x = x * (1.5 - 0.5 * d * x * x)
            root.append(x)
            root_ref[j, m] = x
            start = jnp.where(level < spread(0, m), sigma * (d * x), 0.0)
            state_ref[j, m] = wide_ref[m, j * SUB : (j + 1) * SUB, :] * start
        for m in range(PHASES):
            be_ref[j, m] = a_e[m] * root[m] * east_of(root, m)
            if j > 0:
                bn_ref[j - 1, m] = below[m] * root_below[m] * root[m]
        below, root_below = a_n, root
    for m in range(PHASES):
        bn_ref[total - 1, m] = zero


def sweep_kernel(coef_at, scale_ref, sigma_ref, south_ref, own_ref, north_ref, west_ref, east_ref, *refs):
    fine_ref, out_ref, window_ref, wide_ref, to_phase_ref, to_plain_ref, cell_ref = refs[:7]
    be_ref, bn_ref, root_ref, source_ref, even_ref, odd_ref, turn_ref = refs[7:]
    rows, _, cols = own_ref.shape
    tiles = cols // LANES
    total = rows + 2 * DEPTH
    every = range(PHASES)
    step = pl.program_id(0)
    group = pl.num_programs(0) - 1 - step

    @pl.when(step == 0)
    def _():
        to_phase_ref[...] = phase_matrix(cols, jnp.float32).astype(jnp.bfloat16)
        to_plain_ref[...] = plain_matrix(cols, jnp.float32).astype(jnp.bfloat16)

    lane = lane_iota((SUB, LANES))
    for j in range(total):
        at = slice(j * SUB, (j + 1) * SUB)
        if DEPTH <= j < DEPTH + rows:
            window_ref[at, :cols] = own_ref[j - DEPTH]
        else:
            ref, i = (south_ref, j) if j < DEPTH else (north_ref, j - DEPTH - rows)
            for m in range(tiles):
                window_ref[at, m * LANES : (m + 1) * LANES] = ref[m, i]
        west = roll_lanes(west_ref[j // PER], -(j % PER) * DEPTH)
        east = roll_lanes(east_ref[j // PER], DEPTH - (j % PER) * DEPTH)
        side = jnp.where(lane < DEPTH, west, east)
        window_ref[at, cols:] = jnp.where(lane < 2 * DEPTH, side, 0.0)

    @pl.when(step == 0)
    def _():
        wide = moved(window_ref[...], to_phase_ref[...], exact=True)
        for m in every:
            wide_ref[m] = wide[:, m * LANES : (m + 1) * LANES]
        cell_terms(coef_at, wide_ref, cell_ref)

    @pl.when(step > 0)
    def _():
        wide = moved(window_ref[...], to_phase_ref[...])
        for m in every:
            wide_ref[m] = wide[:, m * LANES : (m + 1) * LANES]

    c = lax.broadcasted_iota(jnp.int32, (SUB, LANES), 0) + group * SUB
    level = jnp.where(c < LEV, c, jnp.where(c < 2 * LEV, c - LEV, jnp.where(c == 2 * LEV, 0, LEV)))
    scale, sigma = (jnp.zeros((SUB, LANES), jnp.float32) for _ in range(2))
    for i in range(sigma_ref.shape[0]):
        scale = jnp.where(c == i, scale_ref[i], scale)
        sigma = jnp.where(c == i, sigma_ref[i], sigma)
    make_weights(
        level.astype(jnp.float32), scale, sigma, cell_ref, wide_ref, be_ref, bn_ref, root_ref, even_ref
    )

    state, other = even_ref, odd_ref
    done = 0
    for _step in range(STEPS):
        for j in range(done, total - done):
            for m in every:
                root = root_ref[j, m]
                source_ref[j, m] = state[j, m] * (root * root)
        for _sweep in range(SWEEPS):
            done += 1
            here = [state[done, m] for m in every]
            south = [bn_ref[done - 1, m] * state[done - 1, m] for m in every]
            for j in range(done, total - done):
                north = [state[j + 1, m] for m in every]
                to_e = [be_ref[j, m] for m in every]
                to_n = [bn_ref[j, m] for m in every]
                flow = [to_e[m] * here[m] for m in every]
                for m in every:
                    new = source_ref[j, m] + south[m] + to_n[m] * north[m]
                    other[j, m] = new + (to_e[m] * east_of(here, m) + west_of(flow, m))
                south = [to_n[m] * here[m] for m in every]
                here = north
            state, other = other, state

    for j in range(rows):
        for m in every:
            window_ref[j * SUB : (j + 1) * SUB, m * LANES : (m + 1) * LANES] = state[j + DEPTH, m] * (
                sigma * root_ref[j + DEPTH, m]
            )
    plain = moved(window_ref[: rows * SUB], to_plain_ref[...])
    fine_ref[...] = plain.reshape(rows, SUB, cols)
    for m in range(tiles):
        for j in range(rows):
            turn_ref[pl.ds(j, SUB, stride=rows), :] = fine_ref[j, :, m * LANES : (m + 1) * LANES]
        for s in range(SUB):
            out_ref[s, :, m * LANES : (m + 1) * LANES] = turn_ref[s * rows : (s + 1) * rows, :]


def sweeps(south, own, north, west, east, length_scale, sigma, channels):
    rows, padded, cols = own.shape
    total = rows + 2 * DEPTH
    groups = padded // SUB
    last = groups - 1
    smem = pl.BlockSpec(memory_space=pltpu.SMEM)

    def body(x):
        return pl.BlockSpec((x.shape[0], SUB, x.shape[2]), lambda g: (0, last - g, 0))

    def slab(x):
        return pl.BlockSpec((x.shape[0], x.shape[1], SUB, LANES), lambda g: (0, 0, last - g, 0))

    plane = pltpu.VMEM((total, PHASES, SUB, LANES), jnp.float32)
    return pl.pallas_call(
        functools.partial(sweep_kernel, channels % SUB),
        grid=(groups,),
        out_shape=(
            jax.ShapeDtypeStruct((rows, padded, cols), jnp.float32),
            jax.ShapeDtypeStruct((channels, rows, cols), jnp.float32),
        ),
        in_specs=[smem, smem, slab(south), body(own), slab(north), body(west), body(east)],
        out_specs=(
            pl.BlockSpec((rows, SUB, cols), lambda g: (0, last - g, 0)),
            pl.BlockSpec((SUB, rows, cols), lambda g: (last - g, 0, 0)),
        ),
        scratch_shapes=[
            pltpu.VMEM((total * SUB, cols + LANES), jnp.float32),
            pltpu.VMEM((PHASES, total * SUB, LANES), jnp.float32),
            pltpu.VMEM((cols + LANES, PHASES * LANES), jnp.bfloat16),
            pltpu.VMEM((PHASES * LANES, cols), jnp.bfloat16),
            pltpu.VMEM((5, PHASES, total, LANES), jnp.float32),
        ]
        + [plane] * 6
        + [pltpu.VMEM((SUB * rows, LANES), jnp.float32)],
        compiler_params=params(),
        name="sweeps",
    )(length_scale, sigma, south, own, north, west, east)


def gather_kernel(channels, pair, fine_ref, obs_ref, out_ref, left_ref):
    senders, padded, slots = out_ref.shape
    rows, _, cols = fine_ref.shape
    high, low = split(fine_ref[...].reshape(rows * padded, cols))
    left_ref[:, :cols] = high
    left_ref[:, cols:] = low
    at_row, at_col = channels % SUB, (channels + 1) % SUB
    col_iota = lax.broadcasted_iota(jnp.int32, (cols, slots), 0).astype(jnp.float32)

    def body(step, carry):
        hots = []
        for s in range(pair):
            col = obs_ref[step * pair + s, at_col : at_col + 1, :]
            hots.append((col_iota == col).astype(jnp.bfloat16))
        hot = jnp.concatenate(hots, axis=1)
        found = jnp.dot(
            left_ref[...], jnp.concatenate([hot, hot], axis=0), preferred_element_type=jnp.float32
        )
        for s in range(pair):
            row = jnp.broadcast_to(obs_ref[step * pair + s, at_row : at_row + 1, :], (padded, slots))
            total = jnp.zeros((padded, slots), jnp.float32)
            for j in range(rows):
                piece = found[j * padded : (j + 1) * padded, s * slots : (s + 1) * slots]
                total = jnp.where(row == float(j), piece, total)
            out_ref[step * pair + s] = total
        return carry

    lax.fori_loop(0, senders // pair, body, 0)


def gather(fine, obs, channels):
    rows, padded, cols = fine.shape
    senders, _, slots = obs.shape
    pair = 2 if senders % 2 == 0 else 1
    where_group = channels // SUB
    vmem = pl.BlockSpec(memory_space=pltpu.VMEM)
    return pl.pallas_call(
        functools.partial(gather_kernel, channels, pair),
        grid=(1,),
        out_shape=jax.ShapeDtypeStruct((senders, padded, slots), jnp.float32),
        in_specs=[
            pl.BlockSpec((rows, padded, cols), lambda i: (0, 0, 0)),
            pl.BlockSpec((senders, SUB, slots), lambda i: (0, where_group, 0)),
        ],
        out_specs=pl.BlockSpec((senders, padded, slots), lambda i: (0, 0, 0)),
        scratch_shapes=[pltpu.VMEM((rows * padded, 2 * cols), jnp.bfloat16)],
        compiler_params=params(),
        name="gather",
    )(fine, obs)


def per_device(
    obs_value, obs_cell, obs_count, bottom_level, diffusivity, partner, length_scale, sigma
):
    _, channels, owners, slots = obs_value.shape
    rows, cols = bottom_level.shape
    n_lat, n_lon = lax.axis_size("lat"), lax.axis_size("lon")
    padded = -(-(channels + COEFS) // SUB) * SUB
    vmem = pl.BlockSpec(memory_space=pltpu.VMEM)
    smem = pl.BlockSpec(memory_space=pltpu.SMEM)

    outgoing = pl.pallas_call(
        functools.partial(pack_kernel, channels, padded, cols),
        grid=(1,),
        out_shape=jax.ShapeDtypeStruct((owners * padded, slots), jnp.float32),
        in_specs=[
            smem,
            pl.BlockSpec((channels * owners, slots), lambda i: (0, 0)),
            pl.BlockSpec((owners, slots), lambda i: (0, 0)),
        ],
        out_specs=vmem,
        compiler_params=params(60 * 1024 * 1024),
        name="pack",
    )(obs_count, obs_value.reshape(channels * owners, slots), obs_cell[0])
    arrived = lax.all_to_all(
        outgoing.reshape(owners, padded, slots), ("lat", "lon"), split_axis=0, concat_axis=0, tiled=True
    )

    centre = lax.rem(partner[0] + lax.axis_index("lon") * cols, cols * n_lon)
    centre_col = centre % cols
    is_top = (lax.axis_index("lat") == n_lat - 1).astype(jnp.int32)
    where = jnp.stack([is_top, centre_col])
    moves = Moves(n_lat, n_lon, centre // cols)

    own, top, low, *halves = scatter(arrived, bottom_level, diffusivity, channels)
    south, north = moves.north(top), moves.south(low)
    whole, part = moves.fold(centre_col // LANES, top, halves)
    ghost, west, east = field_ghosts(where, south, own, north, whole, part)
    fine, diffused = sweeps(
        south, own, ghost, moves.east(east), moves.west(west), length_scale, sigma, channels
    )
    local_fit = gather(fine, arrived, channels)
    returned = lax.all_to_all(local_fit, ("lat", "lon"), split_axis=0, concat_axis=0, tiled=True)
    obs_fit = pl.pallas_call(
        functools.partial(unpack_kernel, channels, padded),
        out_shape=jax.ShapeDtypeStruct((channels, owners, slots), jnp.float32),
        in_specs=[vmem],
        out_specs=vmem,
        compiler_params=params(),
        name="unpack",
    )(returned.reshape(owners * padded, slots))
    return obs_fit[None], diffused


def solution(mesh):
    return jax.shard_map(
        per_device,
        mesh=mesh,
        in_specs=(
            P(("lat", "lon"), None, None, None),
            P(("lat", "lon"), None, None),
            P(("lat", "lon"), None),
            P("lat", "lon"),
            P(None, "lat", "lon"),
            P("lon"),
            P(),
            P(),
        ),
        out_specs=(P(("lat", "lon"), None, None, None), P(None, "lat", "lon")),
        check_vma=False,
    )
```

time: 472 us -> 98.5 us (0.21); the launches traced: 462 us -> 98.1 us
  other arithmetic: 183 us -> 0.08 us
  local copies, waits for them, and re-layouts: 87.2 us -> 0.54 us
  blocking collectives: 123 us -> 45.5 us
  Pallas kernels: 0 us -> 34.9 us
  starting transfers between devices: 39.6 us -> 11.8 us
  between operations: 14.9 us -> 1.44 us
  waiting for transfers between devices: 14.4 us -> 3.86 us
    div x11 -> x0, other arithmetic: 119 us -> none  [per_device(): (trim_margin(source_wide, depth, inner) + trim_margin(w_east, depth, inne...]
    all_gather x2 -> x0, blocking collectives: 105 us -> none  [extend_deep(): lax.all_gather(block[:, tile_rows - depth:, :], 'lon', axis=2, tiled=True)]
    pallas_call x0 -> x6, Pallas kernels: none -> 34.9 us  [the longest x1 16 us: sweeps(): pl.pallas_call(functools.partial(sweep_kernel, channels % SUB), grid=(gro...]
    gather x4 -> x0, local copies, waits for them, and re-layouts: 28.1 us -> none  [the longest x3 14.5 us: extend_deep(): ghost = jnp.take(top_rows, partner_wide, axis=2)[:, ::-1, :]]
    all_to_all x1 -> x2, blocking collectives: 18.2 us -> 45.5 us  [the longest x1 24.7 us: per_device(): lax.all_to_all(local_fit, ('lat', 'lon'), split_axis=0, concat_axis=0, ti...]
    scatter-add x1 -> x0, other arithmetic: 25.4 us -> none  [per_device(): jnp.zeros((channels, tile_rows * tile_cols), jnp.float32).at[:, cell_ids]]
    all_gather x3 -> x0, local copies, waits for them, and re-layouts: 17.4 us -> none  [extend_deep(): lax.all_gather(block[:, tile_rows - depth:, :], 'lon', axis=2, tiled=True)]
    ppermute x14 -> x6, starting transfers between devices: 28.6 us -> 11.8 us  [the longest x1 3.84 us: west(): return lax.ppermute(x, 'lon', self.to_west)]
  transfers between devices with their start and end apart: 17 -> 6, of which waited for: 2 -> 2; matrix products, arithmetic and copies ran while one was open for 19% -> 1% of each run, Pallas kernels for 0% -> 0%
where the time goes in v2:
time: 98.5 us; the launch traced here: 98.1 us
  blocking collectives  45.5 us (46%)
  Pallas kernels  34.9 us (35%)
  starting transfers between devices  11.8 us (12%)
  waiting for transfers between devices  3.86 us (4%)
  between operations  1.44 us (1%)
    all_to_all x1, blocking collectives, per_device(): lax.all_to_all(local_fit, ('lat', 'lon'), split_axis=0, concat_axis=0, ti...  24.7 us
    all_to_all x1, blocking collectives, per_device(): lax.all_to_all(outgoing.reshape(owners, padded, slots), ('lat', 'lon'), s...  20.8 us
    pallas_call x1, Pallas kernels, sweeps(): pl.pallas_call(functools.partial(sweep_kernel, channels % SUB), grid=(gro...  16 us
    pallas_call x1, Pallas kernels, gather(): pl.pallas_call(functools.partial(gather_kernel, channels, pair), grid=(1,...  7.65 us
    pallas_call x1, Pallas kernels, scatter(): pl.pallas_call(functools.partial(scatter_kernel, channels, chunk), out_sh...  7.03 us
    ppermute x1, starting transfers between devices, west(): return lax.ppermute(x, 'lon', self.to_west)  3.84 us
    ppermute x1, waiting for transfers between devices, east(): return lax.ppermute(x, 'lon', self.to_east)  3.68 us
    ppermute x1, starting transfers between devices, north(): return lax.ppermute(x, 'lat', self.to_north)  3.05 us
  transfers between devices with their start and end apart: 6, of which 2 were waited for; matrix products, arithmetic and copies ran while one was open for 1% of the time, Pallas kernels for 0%

profile of v2, /device:TPU:0, one launch (start us, length us, event | category | flops | bytes accessed | tf_op | source)
XLA Modules:
  0.0 98.1 jit_solution(3114728085753008077)
XLA Ops:
  0.6 0.0 copy-start.2
  0.6 0.0 copy-start.3
  0.7 1.8 %pack.1 = f32[768,128]{1,0:T(8,128)} custom-call(s32[1,32]{1,0:T(1,128)} %count_ref.1, f32[672,128]{1,0:T(8,128)} %bitcast.10, s32[32,128]{1,0:T(8,128)} %bitcast.12), custom_call_target="tpu_custom_call" | custom-call | tf_op jit(solution)/shard_map/pack/pallas_call | solution.py:533
  2.5 20.8 %all_to_all.10.obs_ref = f32[32,24,128]{2,1,0:T(8,128)S(1)} all-to-all(f32[32,24,128]{2,1,0:T(8,128)} %bitcast.9), channel_id=1, replica_groups=mesh['lat'=4,'lon'=8] {'lat','lon'}, dimensions={0} | all-to-all | bytes 786432 | tf_op jit(solution)/shard_map/all_to_all | solution.py:546
  23.3 0.0 copy-done.2
  23.3 0.0 copy-done.3
  23.3 0.0 copy-start.4
  23.3 7.0 %scatter.1 = (f32[48,24,256]{2,1,0:T(8,128)S(1)}, f32[2,12,24,128]{3,2,1,0:T(8,128)}, f32[2,12,24,128]{3,2,1,0:T(8,128)S(1)}, f32[12,24,128]{2,1,0:T(8,128)S(1)}, f32[12,24,128]{2,1,0:T(8,128)S(1)}) custom-call(f32[32,24,128]{2,1,0:T(8,128)S(1)} %all_to_all.10.obs_ref, s32[48,256]{1,0:T(8,128)S(1)} %copy-done.3, f32[2,48,256]{2,1,0:T(8,128)S(1)} %copy-done.2), custom_call_target="tpu_custom_call" | custom-call | flops 4831838208 | tf_op jit(solution)/shard_map/scatter/pallas_call | solution.py:205
  30.4 1.3 %collective-permute-start.33 = (f32[2,12,24,128]{3,2,1,0:T(8,128)S(1)}, f32[2,12,24,128]{3,2,1,0:T(8,128)S(1)}, u32[]{:S(2)}, u32[]{:S(2)}) collective-permute-start(f32[2,12,24,128]{3,2,1,0:T(8,128)S(1)} %get-tuple-element.112), channel_id=1, source_target_pairs={{8,0},{16,8},{24,16},{9,1},{17,9},{25,17},{10,2},{18,10},{26,18},{... | collective-permute-start | bytes 884744 | tf_op jit(solution)/shard_map/ppermute | solution.py:123
  31.7 3.0 %collective-permute-start.32 = (f32[2,12,24,128]{3,2,1,0:T(8,128)}, f32[2,12,24,128]{3,2,1,0:T(8,128)S(1)}, u32[]{:S(2)}, u32[]{:S(2)}) collective-permute-start(f32[2,12,24,128]{3,2,1,0:T(8,128)} %get-tuple-element.110), channel_id=1, source_target_pairs={{0,8},{8,16},{16,24},{1,9},{9,17},{17,25},{2,10},{10,18},{18,26},{... | collective-permute-start | bytes 884744 | tf_op jit(solution)/shard_map/ppermute | solution.py:120
  34.7 0.0 copy-done.4
  34.7 0.5 slice.3
  35.9 0.0 copy-start
  36.0 0.0 copy-start.1
  36.0 0.1 pad_add_fusion.where_ref
  36.1 2.7 %conditional.1 = (f32[2,12,24,128]{3,2,1,0:T(8,128)}, f32[12,24,128]{2,1,0:T(8,128)}) conditional(s32[]{:T(128)} %clamp.3, (f32[2,12,24,128]{3,2,1,0:T(8,128)}, f32[12,24,128]{2,1,0:T(8,128)S(1)}) %tuple.72, (f32[2,12,24,128]{3,2,1,0:T(8,128)}, f32[12,24,128]{2,1,0:T(8,128)S(1)}) %tuple.73, ...), branch_computations={%region_0.1_spmd, %region_1.2_spmd, %region_2.3_spmd, %region_3.4_... | conditional | bytes 1769568 | solution.py:141
  36.1 1.4 %collective-permute-start.28 = (f32[2,12,24,128]{3,2,1,0:T(8,128)}, f32[2,12,24,128]{3,2,1,0:T(8,128)}, u32[]{:S(2)}, u32[]{:S(2)}) collective-permute-start(f32[2,12,24,128]{3,2,1,0:T(8,128)} %get-tuple-element.92), channel_id=1, source_target_pairs={{24,30},{25,29},{26,28},{27,27},{28,26},{29,25},{30,24},{31,31}} | collective-permute-start | bytes 884744 | tf_op jit(solution)/shard_map/cond/branch_14_fun/ppermute | solution.py:134
  37.4 1.3 %collective-permute-start.29 = (f32[12,24,128]{2,1,0:T(8,128)S(1)}, f32[12,24,128]{2,1,0:T(8,128)}, u32[]{:S(2)}, u32[]{:S(2)}) collective-permute-start(f32[12,24,128]{2,1,0:T(8,128)S(1)} %get-tuple-element.93), channel_id=1, source_target_pairs={{24,31},{25,30},{26,29},{27,28},{28,27},{29,26},{30,25},{31,24}} | collective-permute-start | bytes 442376 | tf_op jit(solution)/shard_map/cond/branch_14_fun/ppermute | solution.py:135
  38.7 0.0 collective-permute-done.29
  38.7 0.0 collective-permute-done.28
  38.7 0.0 collective-permute-done.33.north_ref
  38.8 0.0 collective-permute-done.32.south_ref
  38.8 1.6 %field_ghosts.1 = (f32[2,12,24,128]{3,2,1,0:T(8,128)S(1)}, f32[8,24,128]{2,1,0:T(8,128)S(1)}, f32[8,24,128]{2,1,0:T(8,128)S(1)}) custom-call(s32[2]{0:T(128)S(1)} %pad_add_fusion.where_ref, f32[2,12,24,128]{3,2,1,0:T(8,128)S(1)} %collective-permute-done.32.south_ref, f32[48,24,256]{2,1,0:T(8,128)S(1)} %get-tuple-element.111.own_ref, ...), custom_call_target="tpu_custom_call" | custom-call | tf_op jit(solution)/shard_map/field_ghosts/pallas_call | solution.py:278
  40.3 0.9 collective-permute-start.34
  41.3 3.8 %collective-permute-start.35 = (f32[8,24,128]{2,1,0:T(8,128)S(1)}, f32[8,24,128]{2,1,0:T(8,128)S(1)}, u32[]{:S(2)}, u32[]{:S(2)}) collective-permute-start(f32[8,24,128]{2,1,0:T(8,128)S(1)} %get-tuple-element.119), channel_id=1, source_target_pairs={{1,0},{2,1},{3,2},{4,3},{5,4},{6,5},{7,6},{0,7},{9,8},{10,9},{11,1... | collective-permute-start | bytes 294920 | tf_op jit(solution)/shard_map/ppermute | solution.py:117
  45.1 3.7 %collective-permute-done.34.west_ref = f32[8,24,128]{2,1,0:T(8,128)S(1)} collective-permute-done((f32[8,24,128]{2,1,0:T(8,128)S(1)}, f32[8,24,128]{2,1,0:T(8,128)S(1)}, u32[]{:S(2)}, u32[]{:S(2)}) %collective-permute-start.34) | collective-permute-done | bytes 98336 | tf_op jit(solution)/shard_map/ppermute | solution.py:114
  48.8 0.2 collective-permute-done.35.east_ref
  48.9 0.0 copy-done
  49.0 0.0 copy-done.1
  49.0 16.0 %sweeps.1 = (f32[48,24,256]{2,1,0:T(8,128)S(1)}, f32[21,48,256]{2,1,0:T(8,128)}) custom-call(f32[21]{0:T(128)S(1)} %copy-done, f32[21]{0:T(128)S(1)} %copy-done.1, f32[2,12,24,128]{3,2,1,0:T(8,128)S(1)} %collective-permute-done.32.south_ref, f32[48,24,256]{2,1,0:T(8,128)S(1)} %get-tuple-element.111.own_ref, ...), custom_call_target="tpu_custom_call" | custom-call | tf_op jit(solution)/shard_map/sweeps/pallas_call | solution.py:446
  65.0 7.6 %gather.1 = f32[32,24,128]{2,1,0:T(8,128)S(1)} custom-call(f32[48,24,256]{2,1,0:T(8,128)S(1)} %get-tuple-element.120.fine_ref, f32[32,24,128]{2,1,0:T(8,128)S(1)} %all_to_all.10.obs_ref), custom_call_target="tpu_custom_call" | custom-call | tf_op jit(solution)/shard_map/gather/pallas_call | solution.py:508
  72.6 24.7 %all_to_all.11 = f32[32,24,128]{2,1,0:T(8,128)S(1)} all-to-all(f32[32,24,128]{2,1,0:T(8,128)S(1)} %gather.1), channel_id=1, replica_groups=mesh['lat'=4,'lon'=8] {'lat','lon'}, dimensions={0} | all-to-all | bytes 786432 | tf_op jit(solution)/shard_map/all_to_all | solution.py:564
  97.3 0.8 unpack.1
Async XLA Ops:
  0.6 22.7 %copy-start.2 = (f32[2,48,256]{2,1,0:T(8,128)S(1)}, f32[2,48,256]{2,1,0:T(8,128)}, u32[]{:S(2)}) copy-start(f32[2,48,256]{2,1,0:T(8,128)} %kappa_ref.1) | copy-start | bytes 294916
  0.6 22.7 %copy-start.3 = (s32[48,256]{1,0:T(8,128)S(1)}, s32[48,256]{1,0:T(8,128)}, u32[]{:S(2)}) copy-start(s32[48,256]{1,0:T(8,128)} %bottom_ref.1) | copy-start | bytes 147460
  23.3 11.4 %copy-start.4 = (s32[256]{0:T(256)S(1)}, s32[256]{0:T(256)}, u32[]{:S(2)}) copy-start(s32[256]{0:T(256)} %param.29) | copy-start | bytes 3076
  30.4 8.4 %collective-permute-start.33 = (f32[2,12,24,128]{3,2,1,0:T(8,128)S(1)}, f32[2,12,24,128]{3,2,1,0:T(8,128)S(1)}, u32[]{:S(2)}, u32[]{:S(2)}) collective-permute-start(f32[2,12,24,128]{3,2,1,0:T(8,128)S(1)} %get-tuple-element.112), channel_id=1, source_target_pairs={{8,0},{16,8},{24,16},{9,1},{17,9},{25,17},{10,2},{18,10},{26,18},{... | collective-permute-start | bytes 884744 | tf_op jit(solution)/shard_map/ppermute | solution.py:123
  31.7 7.1 %collective-permute-start.32 = (f32[2,12,24,128]{3,2,1,0:T(8,128)}, f32[2,12,24,128]{3,2,1,0:T(8,128)S(1)}, u32[]{:S(2)}, u32[]{:S(2)}) collective-permute-start(f32[2,12,24,128]{3,2,1,0:T(8,128)} %get-tuple-element.110), channel_id=1, source_target_pairs={{0,8},{8,16},{16,24},{1,9},{9,17},{17,25},{2,10},{10,18},{18,26},{... | collective-permute-start | bytes 884744 | tf_op jit(solution)/shard_map/ppermute | solution.py:120
  35.9 13.0 %copy-start = (f32[21]{0:T(128)S(1)}, f32[21]{0:T(128)}, u32[]{:S(2)}) copy-start(f32[21]{0:T(128)} %scale_ref.1) | copy-start | bytes 256
  36.0 13.0 %copy-start.1 = (f32[21]{0:T(128)S(1)}, f32[21]{0:T(128)}, u32[]{:S(2)}) copy-start(f32[21]{0:T(128)} %sigma_ref.1) | copy-start | bytes 256
  36.1 2.7 %collective-permute-start.28 = (f32[2,12,24,128]{3,2,1,0:T(8,128)}, f32[2,12,24,128]{3,2,1,0:T(8,128)}, u32[]{:S(2)}, u32[]{:S(2)}) collective-permute-start(f32[2,12,24,128]{3,2,1,0:T(8,128)} %get-tuple-element.92), channel_id=1, source_target_pairs={{24,30},{25,29},{26,28},{27,27},{28,26},{29,25},{30,24},{31,31}} | collective-permute-start | bytes 884744 | tf_op jit(solution)/shard_map/cond/branch_14_fun/ppermute | solution.py:134
  37.4 1.3 %collective-permute-start.29 = (f32[12,24,128]{2,1,0:T(8,128)S(1)}, f32[12,24,128]{2,1,0:T(8,128)}, u32[]{:S(2)}, u32[]{:S(2)}) collective-permute-start(f32[12,24,128]{2,1,0:T(8,128)S(1)} %get-tuple-element.93), channel_id=1, source_target_pairs={{24,31},{25,30},{26,29},{27,28},{28,27},{29,26},{30,25},{31,24}} | collective-permute-start | bytes 442376 | tf_op jit(solution)/shard_map/cond/branch_14_fun/ppermute | solution.py:135
  40.3 8.5 %collective-permute-start.34 = (f32[8,24,128]{2,1,0:T(8,128)S(1)}, f32[8,24,128]{2,1,0:T(8,128)S(1)}, u32[]{:S(2)}, u32[]{:S(2)}) collective-permute-start(f32[8,24,128]{2,1,0:T(8,128)S(1)} %get-tuple-element.118), channel_id=1, source_target_pairs={{0,1},{1,2},{2,3},{3,4},{4,5},{5,6},{6,7},{7,0},{8,9},{9,10},{10,1... | collective-permute-start | bytes 294920 | tf_op jit(solution)/shard_map/ppermute | solution.py:114
  41.3 7.7 %collective-permute-start.35 = (f32[8,24,128]{2,1,0:T(8,128)S(1)}, f32[8,24,128]{2,1,0:T(8,128)S(1)}, u32[]{:S(2)}, u32[]{:S(2)}) collective-permute-start(f32[8,24,128]{2,1,0:T(8,128)S(1)} %get-tuple-element.119), channel_id=1, source_target_pairs={{1,0},{2,1},{3,2},{4,3},{5,4},{6,5},{7,6},{0,7},{9,8},{10,9},{11,1... | collective-permute-start | bytes 294920 | tf_op jit(solution)/shard_map/ppermute | solution.py:117

commit v3 on v2

v3 whole, which is shorter than its diff:
```python
import functools

import jax
import jax.numpy as jnp
from jax import lax
from jax.experimental import pallas as pl
from jax.experimental.pallas import tpu as pltpu
from jax.sharding import PartitionSpec as P

LEV = 10
STEPS = 2
SWEEPS = 6
DEPTH = STEPS * SWEEPS
LANES = 128
SUB = 8
PER = LANES // DEPTH
MARGIN = -(-DEPTH // SUB) * SUB
COEFS = 3
MEGA = 1024 * 1024


def params(limit=8):
    return pltpu.CompilerParams(vmem_limit_bytes=limit * MEGA)


def lane_iota(shape):
    return lax.broadcasted_iota(jnp.int32, shape, len(shape) - 1)


def roll_lanes(x, shift):
    shift = shift % LANES
    return x if shift == 0 else pltpu.roll(x, shift, x.ndim - 1)


def pack_kernel(channels, padded, cols, count_ref, value_ref, cell_ref, out_ref):
    owners, slots = cell_ref.shape
    for c in range(channels):
        out_ref[pl.ds(c, owners, stride=padded), :] = value_ref[pl.ds(c * owners, owners), :]
    owner = lax.broadcasted_iota(jnp.int32, (owners, slots), 0)
    count = jnp.zeros((owners, slots), jnp.int32)
    for d in range(owners):
        count = jnp.where(owner == d, count_ref[0, d], count)
    cell = cell_ref[...].astype(jnp.float32)
    row = jnp.floor((cell + 0.5) * (1.0 / cols))
    col = cell - row * cols
    row = jnp.where(lane_iota((owners, slots)) < count, row, -1.0)
    out_ref[pl.ds(channels, owners, stride=padded), :] = row
    out_ref[pl.ds(channels + 1, owners, stride=padded), :] = col
    for c in range(channels + 2, padded):
        out_ref[pl.ds(c, owners, stride=padded), :] = jnp.zeros((owners, slots), jnp.float32)


def unpack_kernel(channels, padded, in_ref, out_ref):
    owners = out_ref.shape[1]
    for c in range(channels):
        out_ref[c] = in_ref[pl.ds(c, owners, stride=padded), :]


def layout(cols, groups):
    window = cols + 2 * DEPTH
    phases = -(-window // (LANES // groups))
    return phases, -(-window // phases), -(-phases // groups)


def split(x):
    high = x.astype(jnp.bfloat16)
    low = (x - high.astype(jnp.float32)).astype(jnp.bfloat16)
    return high, low


def turned_window(cols, groups, group, n):
    phases, part, _ = layout(cols, groups)
    block = n // LANES
    lane = lax.rem(n - block * LANES + (LANES - group * part % LANES), LANES)
    i = lane // part
    phase = block * groups + i
    return jnp.where((i < groups) & (phase < phases), (lane - i * part) * phases + phase, -1)


def window_source(cols, w):
    at = jnp.where(w < DEPTH, w + cols, jnp.where(w < DEPTH + cols, w - DEPTH, w))
    return jnp.where((w >= 0) & (w < cols + 2 * DEPTH), at, -1)


def moved(x, matrix, exact=False):
    dot = functools.partial(jnp.dot, preferred_element_type=jnp.float32)
    high, low = split(x)
    parts = [high, low]
    if exact:
        rest = (x - high.astype(jnp.float32)) - low.astype(jnp.float32)
        parts.append(rest.astype(jnp.bfloat16))
    return dot(jnp.concatenate(parts, axis=1), jnp.concatenate([matrix] * len(parts), axis=0))


def part_starts(cols):
    return DEPTH, cols - DEPTH - LANES


def mirror_source(cols, centre_col, kind, w):
    column = centre_col + DEPTH - w
    left, right = part_starts(cols)
    in_part = jnp.where(kind == 0, column - left, column + cols - right)
    in_whole = jnp.where(kind == 0, column + cols, column)
    at_whole = jnp.where(in_whole < 0, cols + DEPTH + in_whole, in_whole + jnp.where(in_whole < cols, 0, DEPTH))
    from_whole = (in_whole >= -DEPTH) & (in_whole < cols + DEPTH)
    at = jnp.where(from_whole, at_whole, cols + LANES + in_part)
    return jnp.where((w >= 0) & (w < cols + 2 * DEPTH), at, -1)


def fill_tables(cols, where_ref, phase_ref, plain_ref, mirror_ref):
    is_top, centre_col, kind = where_ref[0], where_ref[1], where_ref[2]
    groups = phase_ref.shape[0]
    phases, part, _ = layout(cols, groups)

    def lanes_of(ref):
        return lax.broadcasted_iota(jnp.int32, (1, ref.shape[-1]), 1)

    def hot(ref, at):
        source = lax.broadcasted_iota(jnp.int32, ref.shape[-2:], 0)
        return jnp.where(source == at, 1.0, 0.0).astype(jnp.bfloat16)

    for g in range(groups):
        w = turned_window(cols, groups, g, lanes_of(phase_ref))
        phase_ref[g] = hot(phase_ref, window_source(cols, w))
        w = lanes_of(plain_ref) + DEPTH
        phase, lane = w % phases, w // phases
        at = ((phase % groups + g) * part + lane) % LANES
        plain_ref[g] = hot(plain_ref, phase // groups * LANES + at)

    @pl.when(is_top == 1)
    def _():
        for g in range(groups):
            w = turned_window(cols, groups, g, lanes_of(mirror_ref))
            mirror_ref[g] = hot(mirror_ref, mirror_source(cols, centre_col, kind, w))


def strip_count(rows, width=DEPTH):
    return -(-rows // (LANES // width))


def pack_strip(read, count, first, out_ref):
    for v in range(out_ref.shape[0]):
        total = None
        for s in range(min(PER, count - v * PER)):
            x = roll_lanes(read(v * PER + s), s * DEPTH - first)
            total = x if total is None else jnp.where(lane_iota(x.shape) >= s * DEPTH, x, total)
        out_ref[v] = total


def halo_lanes(west, at_west, east, at_east, at=0):
    split_at = lane_iota(west.shape) < at + DEPTH
    return jnp.where(split_at, roll_lanes(west, at - at_west), roll_lanes(east, at + DEPTH - at_east))


def slab_kernel(own_ref, west_ref, east_ref, top_ref, low_ref):
    rows, _, cols = own_ref.shape
    tiles, per = cols // LANES, PER // 2
    for ref, first in ((top_ref, rows - DEPTH), (low_ref, 0)):
        for m in range(tiles):
            ref[m * DEPTH : (m + 1) * DEPTH] = own_ref[first : first + DEPTH, :, m * LANES : (m + 1) * LANES]
        for v in range(ref.shape[0] - tiles * DEPTH):
            total = None
            for s in range(min(per, DEPTH - v * per)):
                i, at = divmod(first + v * per + s, PER)
                x = halo_lanes(west_ref[i], at * DEPTH, east_ref[i], at * DEPTH, s * 2 * DEPTH)
                total = x if s == 0 else jnp.where(lane_iota(x.shape) >= s * 2 * DEPTH, x, total)
            ref[tiles * DEPTH + v] = total


def slabs(own, west, east):
    _, width, cols = own.shape
    count = cols // LANES * DEPTH + strip_count(DEPTH, 2 * DEPTH)
    vmem = pl.BlockSpec(memory_space=pltpu.VMEM)
    return pl.pallas_call(
        slab_kernel,
        out_shape=(jax.ShapeDtypeStruct((count, width, LANES), jnp.float32),) * 2,
        in_specs=[vmem] * 3,
        out_specs=(vmem,) * 2,
        compiler_params=params(),
        name="slabs",
    )(own, west, east)


class Moves:
    def __init__(self, n_lat, n_lon, centre_tile):
        self.to_east = [(i, (i + 1) % n_lon) for i in range(n_lon)]
        self.to_west = [(b, a) for a, b in self.to_east]
        self.to_north = [(i, i + 1) for i in range(n_lat - 1)]
        self.to_south = [(b, a) for a, b in self.to_north]
        self.n_lon = n_lon
        self.first = (n_lat - 1) * n_lon
        self.centre_tile = centre_tile

    def east(self, x):
        return lax.ppermute(x, "lon", self.to_east)

    def west(self, x):
        return lax.ppermute(x, "lon", self.to_west)

    def north(self, x):
        return lax.ppermute(x, "lat", self.to_north)

    def south(self, x):
        return lax.ppermute(x, "lat", self.to_south)

    def slabs(self, kind, top, low, parts):
        def pairs(tile, part):
            return [
                (self.first + s, self.first + (tile - part - s) % self.n_lon) for s in range(self.n_lon)
            ]

        def branch(tile, kind):
            def run(top, low, parts):
                part = lax.ppermute(parts[kind], ("lat", "lon"), pairs(tile, kind))
                part, slab = lax.optimization_barrier((part, top))
                whole = lax.ppermute(slab, ("lat", "lon"), pairs(tile, 1 - kind))
                return self.north(top), self.south(low), whole, part

            return run

        branches = [branch(t, k) for t in range(self.n_lon) for k in (0, 1)]
        return lax.switch(self.centre_tile * 2 + kind, branches, top, low, parts)


def scatter_kernel(channels, chunk, obs_ref, bottom_ref, kappa_ref, *refs):
    own_ref, west_ref, east_ref = refs[:3]
    part_refs, (left_ref, right_ref, sum_ref) = refs[3:5], refs[5:]
    senders, padded, slots = obs_ref.shape
    rows, _, cols = own_ref.shape
    row_iota = lax.broadcasted_iota(jnp.int32, (rows, slots), 0).astype(jnp.float32)
    col_iota = lax.broadcasted_iota(jnp.int32, (cols, slots), 0).astype(jnp.float32)

    def body(step, carry):
        for s in range(chunk):
            x = obs_ref[step * chunk + s]
            high, low = split(x)
            on_row = (row_iota == x[channels : channels + 1, :]).astype(jnp.bfloat16)
            on_col = (col_iota == x[channels + 1 : channels + 2, :]).astype(jnp.bfloat16)
            at = s * 2 * slots
            right_ref[:, at : at + slots] = on_col
            right_ref[:, at + slots : at + 2 * slots] = on_col
            for c in range(channels):
                left_ref[c * rows : (c + 1) * rows, at : at + slots] = on_row * high[c : c + 1, :]
                left_ref[c * rows : (c + 1) * rows, at + slots : at + 2 * slots] = on_row * low[c : c + 1, :]
        part = lax.dot_general(
            left_ref[...], right_ref[...], (((1,), (1,)), ((), ())), preferred_element_type=jnp.float32
        )
        for m in range(cols // LANES):
            piece = part[:, m * LANES : (m + 1) * LANES]

            @pl.when(step == 0)
            def _():
                sum_ref[m, : channels * rows] = piece

            @pl.when(step > 0)
            def _():
                sum_ref[m, : channels * rows] += piece

        return carry

    lax.fori_loop(0, senders // chunk, body, 0)
    coefs = [bottom_ref[...].astype(jnp.float32), kappa_ref[0], kappa_ref[1]]
    for m in range(cols // LANES):
        at = slice(m * LANES, (m + 1) * LANES)
        for i, coef in enumerate(coefs):
            sum_ref[m, (channels + i) * rows : (channels + i + 1) * rows] = coef[:, at]
        for g in range(padded // SUB):
            for j in range(rows):
                own_ref[j, g * SUB : (g + 1) * SUB, at] = sum_ref[
                    m, pl.ds(g * SUB * rows + j, SUB, stride=rows), :
                ]
    pack_strip(lambda j: own_ref[j, :, :LANES], rows, 0, west_ref)
    pack_strip(lambda j: own_ref[j, :, cols - LANES :], rows, LANES - DEPTH, east_ref)
    for ref, start in zip(part_refs, part_starts(cols)):
        m, shift = divmod(start, LANES)
        for j in range(DEPTH):
            x = own_ref[rows - DEPTH + j, :, m * LANES : (m + 1) * LANES]
            y = own_ref[rows - DEPTH + j, :, (m + 1) * LANES : (m + 2) * LANES]
            here = lane_iota(x.shape) < LANES - shift
            ref[j] = jnp.where(here, roll_lanes(x, -shift), roll_lanes(y, -shift))


def scatter(obs, bottom_level, diffusivity, channels):
    senders, padded, slots = obs.shape
    rows, cols = bottom_level.shape
    tiles = cols // LANES
    chunk = 8 if senders % 8 == 0 else 1
    vmem = pl.BlockSpec(memory_space=pltpu.VMEM)
    side = (strip_count(rows), padded, LANES)
    part = (DEPTH, padded, LANES)
    shapes = [(rows, padded, cols), side, side, part, part]
    shapes = [jax.ShapeDtypeStruct(shape, jnp.float32) for shape in shapes]
    return pl.pallas_call(
        functools.partial(scatter_kernel, channels, chunk),
        out_shape=tuple(shapes),
        in_specs=[vmem] * 3,
        out_specs=(vmem,) * len(shapes),
        scratch_shapes=[
            pltpu.VMEM((channels * rows, chunk * 2 * slots), jnp.bfloat16),
            pltpu.VMEM((cols, chunk * 2 * slots), jnp.bfloat16),
            pltpu.VMEM((tiles, padded * rows, LANES), jnp.float32),
        ],
        compiler_params=params(14),
        cost_estimate=pl.CostEstimate(
            flops=4 * senders * slots * padded * rows * cols, bytes_accessed=0, transcendentals=0
        ),
        name="scatter",
    )(obs, bottom_level, diffusivity)


def east_of(xs, m):
    return xs[m + 1] if m + 1 < len(xs) else roll_lanes(xs[0], -1)


def west_of(xs, m):
    return xs[m - 1] if m > 0 else roll_lanes(xs[-1], 1)


def slab_row(ref, j, cols):
    tiles, per = cols // LANES, PER // 2
    side = roll_lanes(ref[tiles * DEPTH + j // per], -(j % per) * 2 * DEPTH)
    side = jnp.where(lane_iota(side.shape) < 2 * DEPTH, side, 0.0)
    return [ref[m * DEPTH + j] for m in range(tiles)] + [side]


def part_of_lane(first, part, shape):
    return lax.rem(lane_iota(shape) + (LANES - first % LANES), LANES) // part


def cell_terms(coef_at, part, wide_ref, coef_ref, cell_ref):
    groups = wide_ref.shape[0]
    _, count, total, _ = cell_ref.shape
    which = part_of_lane(0, part, (total, LANES))
    for i in range(COEFS):
        for m in range(count):
            block, turn = divmod(m, groups)
            x = wide_ref[groups - 1, block, pl.ds(coef_at + i, total, stride=SUB), :]
            first = (groups - 1 + turn) * part
            out = jnp.zeros_like(x)
            for g in range(groups):
                out = jnp.where(which == g, roll_lanes(x, g * part - first), out)
            coef_ref[i, m, :total] = out
            coef_ref[i, m, total:] = jnp.zeros((SUB, LANES), jnp.float32)
    bottom = [coef_ref[0, m, :total] for m in range(count)]
    lon = [coef_ref[1, m, :total] for m in range(count)]
    for m in range(count):
        cell_ref[0, m] = bottom[m]
        cell_ref[1, m] = jnp.minimum(bottom[m], east_of(bottom, m))
        cell_ref[2, m] = 0.5 * (lon[m] + east_of(lon, m))
        cell_ref[3, m] = jnp.minimum(bottom[m], coef_ref[0, m, 1 : total + 1])
        cell_ref[4, m] = 0.5 * (coef_ref[2, m, :total] + coef_ref[2, m, 1 : total + 1])


def gathered_phases(wide_ref, j, count, part):
    groups = wide_ref.shape[0]
    at = slice(j * SUB, (j + 1) * SUB)
    out = []
    for m in range(count):
        block, i = divmod(m, groups)
        which = part_of_lane(i * part, part, (SUB, LANES))
        x = wide_ref[groups - 1, block, at, :]
        for g in range(groups - 1):
            x = jnp.where(which == g, wide_ref[g, block, at, :], x)
        out.append(roll_lanes(x, -i * part))
    return out


def scattered_phases(xs, groups, part):
    out = [[] for _ in range(groups)]
    for first in range(0, len(xs), groups):
        turned = [roll_lanes(x, i * part) for i, x in enumerate(xs[first : first + groups])]
        for g in range(groups):
            which = part_of_lane(g * part, part, (SUB, LANES))
            x = turned[0]
            for i in range(1, len(turned)):
                x = jnp.where(which == i, turned[i], x)
            out[g].append(x)
    return out


def make_weights(part, level, scale, sigma, cell_ref, wide_ref, be_ref, bn_ref, root_ref, state_ref):
    total, count = be_ref.shape[:2]
    zero = jnp.zeros((SUB, LANES), jnp.float32)
    below, root_below = [zero] * count, [zero] * count
    skip = MARGIN - DEPTH
    for j in range(skip, total - skip):

        def spread(i, m):
            return jnp.broadcast_to(cell_ref[i, m, j : j + 1, :], (SUB, LANES))

        a_e = [jnp.where(level < spread(1, m), scale * spread(2, m), 0.0) for m in range(count)]
        a_n = [jnp.where(level < spread(3, m), scale * spread(4, m), 0.0) for m in range(count)]
        start = gathered_phases(wide_ref, j, count, part)
        root = []
        for m in range(count):
            d = 1.0 + a_e[m] + west_of(a_e, m) + a_n[m] + below[m]
            x = lax.rsqrt(d)
            x = x * (1.5 - 0.5 * d * x * x)
            root.append(x)
            root_ref[j, m] = x
            state_ref[j, m] = start[m] * jnp.where(level < spread(0, m), sigma * (d * x), 0.0)
        for m in range(count):
            be_ref[j, m] = a_e[m] * root[m] * east_of(root, m)
            bn_ref[j - 1, m] = below[m] * root_below[m] * root[m]
        below, root_below = a_n, root


def run_sweeps(first, last, count, be_ref, bn_ref, source_ref, state_ref):
    every = range(be_ref.shape[1])

    def sweep(_, carry):
        here = [state_ref[first, m] for m in every]
        south = [bn_ref[first - 1, m] * state_ref[first - 1, m] for m in every]
        for j in range(first, last):
            north = [state_ref[j + 1, m] for m in every]
            to_e = [be_ref[j, m] for m in every]
            to_n = [bn_ref[j, m] for m in every]
            flow = [to_e[m] * here[m] for m in every]
            for m in every:
                new = source_ref[j, m] + south[m] + to_n[m] * north[m]
                state_ref[j, m] = new + (to_e[m] * east_of(here, m) + west_of(flow, m))
            south = [to_n[m] * here[m] for m in every]
            here = north
        return carry

    lax.fori_loop(0, count, sweep, 0)


def sweep_kernel(coef_at, where_ref, scale_ref, sigma_ref, *refs):
    own_ref, west_ref, east_ref, south_ref, north_ref, whole_ref, part_ref = refs[:7]
    fine_ref, out_ref, window_ref, ghost_ref, wide_ref, coef_ref, cell_ref = refs[7:14]
    be_ref, bn_ref, root_ref, source_ref, state_ref, turn_ref = refs[14:20]
    phase_ref, plain_ref, mirror_ref = refs[20:]
    rows, padded, cols = own_ref.shape
    tiles, groups = cols // LANES, padded // SUB
    total, count = be_ref.shape[:2]
    part = layout(cols, groups)[1]
    body = MARGIN + rows
    skip = MARGIN - DEPTH
    is_top = where_ref[0]
    fill_tables(cols, where_ref, phase_ref, plain_ref, mirror_ref)

    def put(ref, j, pieces):
        for m, piece in enumerate(pieces):
            for g in range(groups):
                ref[g, m, j * SUB : (j + 1) * SUB] = piece[g * SUB : (g + 1) * SUB]

    def clear(ref, first, last):
        for j in range(first, last):
            put(ref, j, [jnp.zeros((padded, LANES), jnp.float32)] * ref.shape[1])

    clear(window_ref, 0, skip)
    for j in range(DEPTH):
        put(window_ref, skip + j, slab_row(south_ref, j, cols))
    lane = lane_iota((padded, LANES))
    for j in range(rows):
        v, s = divmod(j, PER)
        side = halo_lanes(west_ref[v], s * DEPTH, east_ref[v], s * DEPTH)
        side = jnp.where(lane < 2 * DEPTH, side, 0.0)
        put(
            window_ref,
            MARGIN + j,
            [own_ref[j, :, m * LANES : (m + 1) * LANES] for m in range(tiles)] + [side],
        )
    clear(ghost_ref, DEPTH, MARGIN)

    def widen(ref, used, matrix_ref, first):
        for g in range(groups):
            x = jnp.concatenate([ref[g, t] for t in range(used)], axis=1)
            wide = moved(x, matrix_ref[g], exact=g == groups - 1)
            for k in range(wide_ref.shape[1]):
                wide_ref[g, k, first : first + x.shape[0]] = wide[:, k * LANES : (k + 1) * LANES]

    @pl.when(is_top == 1)
    def _():
        for j in range(DEPTH):
            i = DEPTH - 1 - j
            put(ghost_ref, j, slab_row(whole_ref, i, cols) + [part_ref[i]])
        widen(ghost_ref, tiles + 2, mirror_ref, body * SUB)

    @pl.when(is_top == 0)
    def _():
        for j in range(DEPTH):
            put(ghost_ref, j, slab_row(north_ref, j, cols))
        widen(ghost_ref, tiles + 1, phase_ref, body * SUB)

    widen(window_ref, tiles + 1, phase_ref, 0)
    cell_terms(coef_at, part, wide_ref, coef_ref, cell_ref)

    c = lax.broadcasted_iota(jnp.int32, (SUB, LANES), 0) + lane_iota((SUB, LANES)) // part * SUB
    level = jnp.where(c < LEV, c, jnp.where(c < 2 * LEV, c - LEV, jnp.where(c == 2 * LEV, 0, LEV)))
    scale, sigma = (jnp.zeros((SUB, LANES), jnp.float32) for _ in range(2))
    for i in range(sigma_ref.shape[0]):
        scale = jnp.where(c == i, scale_ref[i], scale)
        sigma = jnp.where(c == i, sigma_ref[i], sigma)
    make_weights(
        part, level.astype(jnp.float32), scale, sigma, cell_ref, wide_ref, be_ref, bn_ref, root_ref, state_ref
    )

    done = 0
    for _step in range(STEPS):

        def make_source(j, carry):
            for m in range(count):
                root = root_ref[j, m]
                source_ref[j, m] = state_ref[j, m] * (root * root)
            return carry

        lax.fori_loop(skip + done, total - skip - done, make_source, 0, unroll=4)
        for some in (SWEEPS - SWEEPS // 2, SWEEPS // 2):
            if some > 0:
                run_sweeps(
                    skip + done + 1, total - skip - done - 1, some, be_ref, bn_ref, source_ref, state_ref
                )
            done += some

    for j in range(rows):
        at = MARGIN + j
        scaled = [state_ref[at, m] * (sigma * root_ref[at, m]) for m in range(count)]
        for g, pieces in enumerate(scattered_phases(scaled, groups, part)):
            for k, piece in enumerate(pieces):
                window_ref[g, k, j * SUB : (j + 1) * SUB] = piece
    for g in range(groups):
        x = jnp.concatenate(
            [window_ref[g, k, : rows * SUB] for k in range(wide_ref.shape[1])], axis=1
        )
        plain = moved(x, plain_ref[g]).reshape(rows, SUB, cols)
        fine_ref[:, g * SUB : (g + 1) * SUB, :] = plain
        for m in range(tiles):
            for j in range(rows):
                turn_ref[pl.ds(j, SUB, stride=rows), :] = plain[j, :, m * LANES : (m + 1) * LANES]
            for s in range(SUB):
                if g * SUB + s < out_ref.shape[0]:
                    out_ref[g * SUB + s, :, m * LANES : (m + 1) * LANES] = turn_ref[
                        s * rows : (s + 1) * rows, :
                    ]


def sweeps(where, own, around, length_scale, sigma, channels):
    rows, padded, cols = own.shape
    total = rows + 2 * MARGIN
    groups = padded // SUB
    count, _, blocks = layout(cols, groups)
    smem = pl.BlockSpec(memory_space=pltpu.SMEM)
    vmem = pl.BlockSpec(memory_space=pltpu.VMEM)
    plane = pltpu.VMEM((total, count, SUB, LANES), jnp.float32)
    tiles = max(cols // LANES + 1, blocks)
    return pl.pallas_call(
        functools.partial(sweep_kernel, channels % SUB),
        out_shape=(
            jax.ShapeDtypeStruct((rows, padded, cols), jnp.float32),
            jax.ShapeDtypeStruct((channels, rows, cols), jnp.float32),
        ),
        in_specs=[smem] * 3 + [vmem] * (1 + len(around)),
        out_specs=(vmem, vmem),
        scratch_shapes=[
            pltpu.VMEM((groups, tiles, (MARGIN + rows) * SUB, LANES), jnp.float32),
            pltpu.VMEM((groups, cols // LANES + 2, MARGIN * SUB, LANES), jnp.float32),
            pltpu.VMEM((groups, blocks, total * SUB, LANES), jnp.float32),
            pltpu.VMEM((COEFS, count, total + SUB, LANES), jnp.float32),
            pltpu.VMEM((5, count, total, LANES), jnp.float32),
        ]
        + [plane] * 5
        + [pltpu.VMEM((SUB * rows, LANES), jnp.float32)]
        + [
            pltpu.VMEM((groups, cols + LANES, blocks * LANES), jnp.bfloat16),
            pltpu.VMEM((groups, blocks * LANES, cols), jnp.bfloat16),
            pltpu.VMEM((groups, cols + 2 * LANES, blocks * LANES), jnp.bfloat16),
        ],
        compiler_params=params(28),
        name="sweeps",
    )(where, length_scale, sigma, own, *around)


def gather_kernel(channels, pair, fine_ref, obs_ref, out_ref, left_ref):
    senders, padded, slots = out_ref.shape
    rows, _, cols = fine_ref.shape
    high, low = split(fine_ref[...].reshape(rows * padded, cols))
    left_ref[:, :cols] = high
    left_ref[:, cols:] = low
    at_row, at_col = channels % SUB, (channels + 1) % SUB
    col_iota = lax.broadcasted_iota(jnp.int32, (cols, slots), 0).astype(jnp.float32)

    def body(step, carry):
        hots = []
        for s in range(pair):
            col = obs_ref[step * pair + s, at_col : at_col + 1, :]
            hots.append((col_iota == col).astype(jnp.bfloat16))
        hot = jnp.concatenate(hots, axis=1)
        found = jnp.dot(
            left_ref[...], jnp.concatenate([hot, hot], axis=0), preferred_element_type=jnp.float32
        )
        for s in range(pair):
            row = jnp.broadcast_to(obs_ref[step * pair + s, at_row : at_row + 1, :], (padded, slots))
            total = jnp.zeros((padded, slots), jnp.float32)
            for j in range(rows):
                piece = found[j * padded : (j + 1) * padded, s * slots : (s + 1) * slots]
                total = jnp.where(row == float(j), piece, total)
            out_ref[step * pair + s] = total
        return carry

    lax.fori_loop(0, senders // pair, body, 0)


def gather(fine, obs, channels):
    rows, padded, cols = fine.shape
    senders, _, slots = obs.shape
    pair = 2 if senders % 2 == 0 else 1
    where_group = channels // SUB
    vmem = pl.BlockSpec(memory_space=pltpu.VMEM)
    return pl.pallas_call(
        functools.partial(gather_kernel, channels, pair),
        grid=(1,),
        out_shape=jax.ShapeDtypeStruct((senders, padded, slots), jnp.float32),
        in_specs=[
            pl.BlockSpec((rows, padded, cols), lambda i: (0, 0, 0)),
            pl.BlockSpec((senders, SUB, slots), lambda i: (0, where_group, 0)),
        ],
        out_specs=pl.BlockSpec((senders, padded, slots), lambda i: (0, 0, 0)),
        scratch_shapes=[pltpu.VMEM((rows * padded, 2 * cols), jnp.bfloat16)],
        compiler_params=params(12),
        name="gather",
    )(fine, obs)


def per_device(
    obs_value, obs_cell, obs_count, bottom_level, diffusivity, partner, length_scale, sigma
):
    _, channels, owners, slots = obs_value.shape
    rows, cols = bottom_level.shape
    n_lat, n_lon = lax.axis_size("lat"), lax.axis_size("lon")
    padded = -(-(channels + COEFS) // SUB) * SUB
    vmem = pl.BlockSpec(memory_space=pltpu.VMEM)
    smem = pl.BlockSpec(memory_space=pltpu.SMEM)

    outgoing = pl.pallas_call(
        functools.partial(pack_kernel, channels, padded, cols),
        grid=(1,),
        out_shape=jax.ShapeDtypeStruct((owners * padded, slots), jnp.float32),
        in_specs=[
            smem,
            pl.BlockSpec((channels * owners, slots), lambda i: (0, 0)),
            pl.BlockSpec((owners, slots), lambda i: (0, 0)),
        ],
        out_specs=vmem,
        compiler_params=params(60),
        name="pack",
    )(obs_count, obs_value.reshape(channels * owners, slots), obs_cell[0])
    arrived = lax.all_to_all(
        outgoing.reshape(owners, padded, slots), ("lat", "lon"), split_axis=0, concat_axis=0, tiled=True
    )

    centre = lax.rem(partner[0] + lax.axis_index("lon") * cols, cols * n_lon)
    centre_col = centre % cols
    is_top = (lax.axis_index("lat") == n_lat - 1).astype(jnp.int32)
    kind = (centre_col >= cols // 2).astype(jnp.int32)
    where = jnp.stack([is_top, centre_col, kind])
    moves = Moves(n_lat, n_lon, centre // cols)

    own, west, east, *parts = scatter(arrived, bottom_level, diffusivity, channels)
    west, east = moves.east(east), moves.west(west)
    top, low = slabs(own, west, east)
    around = (west, east, *moves.slabs(kind, top, low, parts))
    fine, diffused = sweeps(where, own, around, length_scale, sigma, channels)
    local_fit = gather(fine, arrived, channels)
    returned = lax.all_to_all(local_fit, ("lat", "lon"), split_axis=0, concat_axis=0, tiled=True)
    obs_fit = pl.pallas_call(
        functools.partial(unpack_kernel, channels, padded),
        out_shape=jax.ShapeDtypeStruct((channels, owners, slots), jnp.float32),
        in_specs=[vmem],
        out_specs=vmem,
        compiler_params=params(),
        name="unpack",
    )(returned.reshape(owners * padded, slots))
    return obs_fit[None], diffused


def solution(mesh):
    return jax.shard_map(
        per_device,
        mesh=mesh,
        in_specs=(
            P(("lat", "lon"), None, None, None),
            P(("lat", "lon"), None, None),
            P(("lat", "lon"), None),
            P("lat", "lon"),
            P(None, "lat", "lon"),
            P("lon"),
            P(),
            P(),
        ),
        out_specs=(P(("lat", "lon"), None, None, None), P(None, "lat", "lon")),
        check_vma=False,
    )
```

time: 98.5 us -> 93.5 us (0.949)
  blocking collectives: 45.5 us -> 24.8 us
  waiting for transfers between devices: 3.86 us -> 14.5 us
  starting transfers between devices: 11.8 us -> 19.9 us
  Pallas kernels: 34.9 us -> 32.2 us
    all_to_all x1 -> x0, blocking collectives: 20.8 us -> none  [per_device(): lax.all_to_all(outgoing.reshape(owners, padded, slots), ('lat', 'lon'), s...]
    all_to_all x0 -> x1, waiting for transfers between devices: none -> 12.3 us  [per_device(): lax.all_to_all(outgoing.reshape(owners, padded, slots), ('lat', 'lon'), s...]
    all_to_all x0 -> x1, starting transfers between devices: none -> 7.3 us  [per_device(): lax.all_to_all(outgoing.reshape(owners, padded, slots), ('lat', 'lon'), s...]
    pallas_call x2, Pallas kernels: 17.6 us -> 15.4 us  [the longest x1 15.2 us: sweeps(): pl.pallas_call(functools.partial(sweep_kernel, channels % SUB), out_shape...]
    ppermute x1, waiting for transfers between devices: 3.68 us -> 2.12 us  [east(): return lax.ppermute(x, 'lon', self.to_east)]
  transfers between devices with their start and end apart: 6 -> 7, of which waited for: 2 -> 2; matrix products, arithmetic and copies ran while one was open for 1% -> 1% of each run, Pallas kernels for 0% -> 0%
where the time goes in v3:
time: 93.5 us; the launch traced here: 93.4 us
  Pallas kernels  32.2 us (34%)
  blocking collectives  24.8 us (27%)
  starting transfers between devices  19.9 us (21%)
  waiting for transfers between devices  14.5 us (16%)
  between operations  1.44 us (2%)
    all_to_all x1, blocking collectives, per_device(): lax.all_to_all(local_fit, ('lat', 'lon'), split_axis=0, concat_axis=0, ti...  24.8 us
    pallas_call x1, Pallas kernels, sweeps(): pl.pallas_call(functools.partial(sweep_kernel, channels % SUB), out_shape...  15.2 us
    all_to_all x1, waiting for transfers between devices, per_device(): lax.all_to_all(outgoing.reshape(owners, padded, slots), ('lat', 'lon'), s...  12.3 us
    pallas_call x1, Pallas kernels, gather(): pl.pallas_call(functools.partial(gather_kernel, channels, pair), grid=(1,...  7.65 us
    all_to_all x1, starting transfers between devices, per_device(): lax.all_to_all(outgoing.reshape(owners, padded, slots), ('lat', 'lon'), s...  7.3 us
    pallas_call x1, Pallas kernels, scatter(): pl.pallas_call(functools.partial(scatter_kernel, channels, chunk), out_sh...  6.48 us
    ppermute x1, starting transfers between devices, west(): return lax.ppermute(x, 'lon', self.to_west)  3.84 us
    ppermute x1, starting transfers between devices, north(): return lax.ppermute(x, 'lat', self.to_north)  3.78 us
  transfers between devices with their start and end apart: 7, of which 2 were waited for; matrix products, arithmetic and copies ran while one was open for 1% of the time, Pallas kernels for 0%

profile of v3, /device:TPU:0, one launch (start us, length us, event | category | flops | bytes accessed | tf_op | source)
XLA Modules:
  0.0 93.4 jit_solution(4900749538271591477)
XLA Ops:
  0.6 0.0 copy-start.4
  0.6 0.0 copy-start.2
  0.7 0.0 copy-start.3
  0.7 1.8 %pack.1 = f32[768,128]{1,0:T(8,128)} custom-call(s32[1,32]{1,0:T(1,128)} %count_ref.1, f32[672,128]{1,0:T(8,128)} %bitcast.11, s32[32,128]{1,0:T(8,128)} %bitcast.13), custom_call_target="tpu_custom_call" | custom-call | tf_op jit(solution)/shard_map/pack/pallas_call | solution.py:636
  2.5 7.3 %all-to-all-start = ((f32[32,24,128]{2,1,0:T(8,128)}), f32[32,24,128]{2,1,0:T(8,128)S(1)}, u32[]{:S(2)}, u32[]{:S(2)}) async-start(f32[32,24,128]{2,1,0:T(8,128)} %bitcast.10), calls=%async_computation | async-start | bytes 786432 | tf_op jit(solution)/shard_map/all_to_all | solution.py:649
  9.8 0.0 copy-done.4
  9.8 0.5 slice.3
  11.0 12.3 %all-to-all-done.obs_ref = f32[32,24,128]{2,1,0:T(8,128)S(1)} async-done(((f32[32,24,128]{2,1,0:T(8,128)}), f32[32,24,128]{2,1,0:T(8,128)S(1)}, u32[]{:S(2)}, u32[]{:S(2)}) %all-to-all-start) | async-done | bytes 393248 | tf_op jit(solution)/shard_map/all_to_all | solution.py:649
  23.4 0.0 copy-done.2
  23.4 0.0 copy-done.3
  23.4 6.5 %scatter.1 = (f32[48,24,256]{2,1,0:T(8,128)S(1)}, f32[5,24,128]{2,1,0:T(8,128)S(1)}, f32[5,24,128]{2,1,0:T(8,128)S(1)}, f32[12,24,128]{2,1,0:T(8,128)S(1)}, f32[12,24,128]{2,1,0:T(8,128)S(1)}) custom-call(f32[32,24,128]{2,1,0:T(8,128)S(1)} %all-to-all-done.obs_ref, s32[48,256]{1,0:T(8,128)S(1)} %copy-done.3, f32[2,48,256]{2,1,0:T(8,128)S(1)} %copy-done.2), custom_call_target="tpu_custom_call" | custom-call | flops 4831838208 | tf_op jit(solution)/shard_map/scatter/pallas_call | solution.py:293
  29.9 0.0 copy-start
  29.9 0.0 copy-start.1
  29.9 0.9 collective-permute-start.64
  30.8 3.8 %collective-permute-start.65 = (f32[5,24,128]{2,1,0:T(8,128)S(1)}, f32[5,24,128]{2,1,0:T(8,128)S(1)}, u32[]{:S(2)}, u32[]{:S(2)}) collective-permute-start(f32[5,24,128]{2,1,0:T(8,128)S(1)} %get-tuple-element.193), channel_id=1, source_target_pairs={{1,0},{2,1},{3,2},{4,3},{5,4},{6,5},{7,6},{0,7},{9,8},{10,9},{11,1... | collective-permute-start | bytes 184328 | tf_op jit(solution)/shard_map/ppermute | solution.py:198
  34.7 0.1 pad_add_fusion.where_ref
  34.7 2.1 %collective-permute-done.64.west_ref.refs_1_ = f32[5,24,128]{2,1,0:T(8,128)S(1)} collective-permute-done((f32[5,24,128]{2,1,0:T(8,128)S(1)}, f32[5,24,128]{2,1,0:T(8,128)S(1)}, u32[]{:S(2)}, u32[]{:S(2)}) %collective-permute-start.64) | collective-permute-done | bytes 61472 | tf_op jit(solution)/shard_map/ppermute | solution.py:195
  36.8 0.0 collective-permute-done.65.east_ref.refs_2_
  36.9 0.2 slabs.1
  37.1 7.8 %conditional.1 = (f32[27,24,128]{2,1,0:T(8,128)}, f32[27,24,128]{2,1,0:T(8,128)}, f32[27,24,128]{2,1,0:T(8,128)}, f32[12,24,128]{2,1,0:T(8,128)}) conditional(s32[]{:T(128)} %clamp.3, (f32[27,24,128]{2,1,0:T(8,128)S(1)}, f32[27,24,128]{2,1,0:T(8,128)S(1)}, f32[12,24,128]{2,1,0:T(8,128)S(1)}) %tuple.88, ...), branch_computations={%region_0.1_spmd, %region_1.2_spmd, %region_2.3_spmd, %region_3.4_... | conditional | bytes 4571328 | solution.py:222
  37.1 1.3 %collective-permute-start.54 = (f32[12,24,128]{2,1,0:T(8,128)S(1)}, f32[12,24,128]{2,1,0:T(8,128)}, u32[]{:S(2)}, u32[]{:S(2)}) collective-permute-start(f32[12,24,128]{2,1,0:T(8,128)S(1)} %get-tuple-element.163), channel_id=1, source_target_pairs={{24,29},{25,28},{26,27},{27,26},{28,25},{29,24},{30,31},{31,30}} | collective-permute-start | bytes 442376 | tf_op jit(solution)/shard_map/cond/branch_13_fun/ppermute | solution.py:214
  38.4 1.3 %collective-permute-start.53 = (f32[27,24,128]{2,1,0:T(8,128)S(1)}, f32[27,24,128]{2,1,0:T(8,128)}, u32[]{:S(2)}, u32[]{:S(2)}) collective-permute-start(f32[27,24,128]{2,1,0:T(8,128)S(1)} %get-tuple-element.162), channel_id=1, source_target_pairs={{8,0},{16,8},{24,16},{9,1},{17,9},{25,17},{10,2},{18,10},{26,18},{... | collective-permute-start | bytes 995336 | tf_op jit(solution)/shard_map/cond/branch_13_fun/ppermute | solution.py:204
  39.7 3.8 %collective-permute-start.52 = (f32[27,24,128]{2,1,0:T(8,128)S(1)}, f32[27,24,128]{2,1,0:T(8,128)}, u32[]{:S(2)}, u32[]{:S(2)}) collective-permute-start(f32[27,24,128]{2,1,0:T(8,128)S(1)} %get-tuple-element.164), channel_id=1, source_target_pairs={{0,8},{8,16},{16,24},{1,9},{9,17},{17,25},{2,10},{10,18},{18,26},{... | collective-permute-start | bytes 995336 | tf_op jit(solution)/shard_map/cond/branch_13_fun/ppermute | solution.py:201
  43.5 0.0 collective-permute-done.54
  43.5 1.4 %collective-permute-start.55 = (f32[27,24,128]{2,1,0:T(8,128)S(1)}, f32[27,24,128]{2,1,0:T(8,128)}, u32[]{:S(2)}, u32[]{:S(2)}) collective-permute-start(f32[27,24,128]{2,1,0:T(8,128)S(1)} %get-tuple-element.164), channel_id=1, source_target_pairs={{24,30},{25,29},{26,28},{27,27},{28,26},{29,25},{30,24},{31,31}} | collective-permute-start | bytes 995336 | tf_op jit(solution)/shard_map/cond/branch_13_fun/ppermute | solution.py:216
  44.9 0.0 collective-permute-done.53
  44.9 0.0 collective-permute-done.52
  44.9 0.0 collective-permute-done.55
  44.9 0.0 copy-done
  44.9 0.0 copy-done.1
  44.9 15.2 %sweeps.1 = (f32[48,24,256]{2,1,0:T(8,128)S(1)}, f32[21,48,256]{2,1,0:T(8,128)}) custom-call(s32[3]{0:T(128)S(1)} %pad_add_fusion.where_ref, f32[21]{0:T(128)S(1)} %copy-done, f32[21]{0:T(128)S(1)} %copy-done.1, f32[48,24,256]{2,1,0:T(8,128)S(1)} %get-tuple-element.191.own_ref.refs_0_, f32[5,24,128]{2,1,0:T(8,128)S(1)} %collective-permute-done.64.west_ref.refs_1_, ...), custom_call_target="tpu_custom_call" | custom-call | tf_op jit(solution)/shard_map/sweeps/pallas_call | solution.py:548
  60.2 7.6 %gather.1 = f32[32,24,128]{2,1,0:T(8,128)S(1)} custom-call(f32[48,24,256]{2,1,0:T(8,128)S(1)} %get-tuple-element.202.fine_ref, f32[32,24,128]{2,1,0:T(8,128)S(1)} %all-to-all-done.obs_ref), custom_call_target="tpu_custom_call" | custom-call | tf_op jit(solution)/shard_map/gather/pallas_call | solution.py:611
  67.8 24.8 %all_to_all.10 = f32[32,24,128]{2,1,0:T(8,128)S(1)} all-to-all(f32[32,24,128]{2,1,0:T(8,128)S(1)} %gather.1), channel_id=1, replica_groups=mesh['lat'=4,'lon'=8] {'lat','lon'}, dimensions={0} | all-to-all | bytes 786432 | tf_op jit(solution)/shard_map/all_to_all | solution.py:666
  92.6 0.8 unpack.1
Async XLA Ops:
  0.6 9.2 %copy-start.4 = (s32[256]{0:T(256)S(1)}, s32[256]{0:T(256)}, u32[]{:S(2)}) copy-start(s32[256]{0:T(256)} %param.29) | copy-start | bytes 3076
  0.6 22.7 %copy-start.2 = (f32[2,48,256]{2,1,0:T(8,128)S(1)}, f32[2,48,256]{2,1,0:T(8,128)}, u32[]{:S(2)}) copy-start(f32[2,48,256]{2,1,0:T(8,128)} %kappa_ref.1) | copy-start | bytes 294916
  0.7 22.7 %copy-start.3 = (s32[48,256]{1,0:T(8,128)S(1)}, s32[48,256]{1,0:T(8,128)}, u32[]{:S(2)}) copy-start(s32[48,256]{1,0:T(8,128)} %bottom_ref.1) | copy-start | bytes 147460
  2.5 20.8 %all-to-all-start = ((f32[32,24,128]{2,1,0:T(8,128)}), f32[32,24,128]{2,1,0:T(8,128)S(1)}, u32[]{:S(2)}, u32[]{:S(2)}) async-start(f32[32,24,128]{2,1,0:T(8,128)} %bitcast.10), calls=%async_computation | async-start | bytes 786432 | tf_op jit(solution)/shard_map/all_to_all | solution.py:649
  29.9 15.1 %copy-start = (f32[21]{0:T(128)S(1)}, f32[21]{0:T(128)}, u32[]{:S(2)}) copy-start(f32[21]{0:T(128)} %scale_ref.1) | copy-start | bytes 256
  29.9 15.1 %copy-start.1 = (f32[21]{0:T(128)S(1)}, f32[21]{0:T(128)}, u32[]{:S(2)}) copy-start(f32[21]{0:T(128)} %sigma_ref.1) | copy-start | bytes 256
  29.9 7.0 %collective-permute-start.64 = (f32[5,24,128]{2,1,0:T(8,128)S(1)}, f32[5,24,128]{2,1,0:T(8,128)S(1)}, u32[]{:S(2)}, u32[]{:S(2)}) collective-permute-start(f32[5,24,128]{2,1,0:T(8,128)S(1)} %get-tuple-element.192), channel_id=1, source_target_pairs={{0,1},{1,2},{2,3},{3,4},{4,5},{5,6},{6,7},{7,0},{8,9},{9,10},{10,1... | collective-permute-start | bytes 184328 | tf_op jit(solution)/shard_map/ppermute | solution.py:195
  30.8 6.0 %collective-permute-start.65 = (f32[5,24,128]{2,1,0:T(8,128)S(1)}, f32[5,24,128]{2,1,0:T(8,128)S(1)}, u32[]{:S(2)}, u32[]{:S(2)}) collective-permute-start(f32[5,24,128]{2,1,0:T(8,128)S(1)} %get-tuple-element.193), channel_id=1, source_target_pairs={{1,0},{2,1},{3,2},{4,3},{5,4},{6,5},{7,6},{0,7},{9,8},{10,9},{11,1... | collective-permute-start | bytes 184328 | tf_op jit(solution)/shard_map/ppermute | solution.py:198
  37.1 6.4 %collective-permute-start.54 = (f32[12,24,128]{2,1,0:T(8,128)S(1)}, f32[12,24,128]{2,1,0:T(8,128)}, u32[]{:S(2)}, u32[]{:S(2)}) collective-permute-start(f32[12,24,128]{2,1,0:T(8,128)S(1)} %get-tuple-element.163), channel_id=1, source_target_pairs={{24,29},{25,28},{26,27},{27,26},{28,25},{29,24},{30,31},{31,30}} | collective-permute-start | bytes 442376 | tf_op jit(solution)/shard_map/cond/branch_13_fun/ppermute | solution.py:214
  38.4 6.5 %collective-permute-start.53 = (f32[27,24,128]{2,1,0:T(8,128)S(1)}, f32[27,24,128]{2,1,0:T(8,128)}, u32[]{:S(2)}, u32[]{:S(2)}) collective-permute-start(f32[27,24,128]{2,1,0:T(8,128)S(1)} %get-tuple-element.162), channel_id=1, source_target_pairs={{8,0},{16,8},{24,16},{9,1},{17,9},{25,17},{10,2},{18,10},{26,18},{... | collective-permute-start | bytes 995336 | tf_op jit(solution)/shard_map/cond/branch_13_fun/ppermute | solution.py:204
  39.7 5.2 %collective-permute-start.52 = (f32[27,24,128]{2,1,0:T(8,128)S(1)}, f32[27,24,128]{2,1,0:T(8,128)}, u32[]{:S(2)}, u32[]{:S(2)}) collective-permute-start(f32[27,24,128]{2,1,0:T(8,128)S(1)} %get-tuple-element.164), channel_id=1, source_target_pairs={{0,8},{8,16},{16,24},{1,9},{9,17},{17,25},{2,10},{10,18},{18,26},{... | collective-permute-start | bytes 995336 | tf_op jit(solution)/shard_map/cond/branch_13_fun/ppermute | solution.py:201
  43.5 1.4 %collective-permute-start.55 = (f32[27,24,128]{2,1,0:T(8,128)S(1)}, f32[27,24,128]{2,1,0:T(8,128)}, u32[]{:S(2)}, u32[]{:S(2)}) collective-permute-start(f32[27,24,128]{2,1,0:T(8,128)S(1)} %get-tuple-element.164), channel_id=1, source_target_pairs={{24,30},{25,29},{26,28},{27,27},{28,26},{29,25},{30,24},{31,31}} | collective-permute-start | bytes 995336 | tf_op jit(solution)/shard_map/cond/branch_13_fun/ppermute | solution.py:216

commit v4 on v3

--- a/solution.py
+++ b/solution.py
@@ -236,17 +236,17 @@
             high, low = split(x)
             on_row = (row_iota == x[channels : channels + 1, :]).astype(jnp.bfloat16)
             on_col = (col_iota == x[channels + 1 : channels + 2, :]).astype(jnp.bfloat16)
-            at = s * 2 * slots
-            right_ref[:, at : at + slots] = on_col
-            right_ref[:, at + slots : at + 2 * slots] = on_col
+            at = slice(s * slots, (s + 1) * slots)
+            right_ref[:, at] = on_col
             for c in range(channels):
-                left_ref[c * rows : (c + 1) * rows, at : at + slots] = on_row * high[c : c + 1, :]
-                left_ref[c * rows : (c + 1) * rows, at + slots : at + 2 * slots] = on_row * low[c : c + 1, :]
+                left_ref[c * rows : (c + 1) * rows, at] = on_row * high[c : c + 1, :]
+                left_ref[(channels + c) * rows : (channels + c + 1) * rows, at] = on_row * low[c : c + 1, :]
         part = lax.dot_general(
             left_ref[...], right_ref[...], (((1,), (1,)), ((), ())), preferred_element_type=jnp.float32
         )
         for m in range(cols // LANES):
             piece = part[:, m * LANES : (m + 1) * LANES]
+            piece = piece[: channels * rows] + piece[channels * rows :]
 
             @pl.when(step == 0)
             def _():
@@ -284,7 +284,7 @@
     senders, padded, slots = obs.shape
     rows, cols = bottom_level.shape
     tiles = cols // LANES
-    chunk = 8 if senders % 8 == 0 else 1
+    chunk = 16 if senders % 16 == 0 else 1
     vmem = pl.BlockSpec(memory_space=pltpu.VMEM)
     side = (strip_count(rows), padded, LANES)
     part = (DEPTH, padded, LANES)
@@ -296,11 +296,11 @@
         in_specs=[vmem] * 3,
         out_specs=(vmem,) * len(shapes),
         scratch_shapes=[
-            pltpu.VMEM((channels * rows, chunk * 2 * slots), jnp.bfloat16),
-            pltpu.VMEM((cols, chunk * 2 * slots), jnp.bfloat16),
+            pltpu.VMEM((2 * channels * rows, chunk * slots), jnp.bfloat16),
+            pltpu.VMEM((cols, chunk * slots), jnp.bfloat16),
             pltpu.VMEM((tiles, padded * rows, LANES), jnp.float32),
         ],
-        compiler_params=params(14),
+        compiler_params=params(28),
         cost_estimate=pl.CostEstimate(
             flops=4 * senders * slots * padded * rows * cols, bytes_accessed=0, transcendentals=0
         ),
@@ -427,10 +427,17 @@
 
 
 def sweep_kernel(coef_at, where_ref, scale_ref, sigma_ref, *refs):
-    own_ref, west_ref, east_ref, south_ref, north_ref, whole_ref, part_ref = refs[:7]
+    own_ref, west_ref, east_ref = refs[:3]
     fine_ref, out_ref, window_ref, ghost_ref, wide_ref, coef_ref, cell_ref = refs[7:14]
     be_ref, bn_ref, root_ref, source_ref, state_ref, turn_ref = refs[14:20]
-    phase_ref, plain_ref, mirror_ref = refs[20:]
+    phase_ref, plain_ref, mirror_ref = refs[20:23]
+    south_ref, north_ref, whole_ref, part_ref = refs[23:27]
+    copies = [
+        pltpu.make_async_copy(source, target, refs[27].at[i])
+        for i, (source, target) in enumerate(zip(refs[3:7], refs[23:27]))
+    ]
+    for copy in copies:
+        copy.start()
     rows, padded, cols = own_ref.shape
     tiles, groups = cols // LANES, padded // SUB
     total, count = be_ref.shape[:2]
@@ -450,8 +457,6 @@
             put(ref, j, [jnp.zeros((padded, LANES), jnp.float32)] * ref.shape[1])
 
     clear(window_ref, 0, skip)
-    for j in range(DEPTH):
-        put(window_ref, skip + j, slab_row(south_ref, j, cols))
     lane = lane_iota((padded, LANES))
     for j in range(rows):
         v, s = divmod(j, PER)
@@ -463,6 +468,10 @@
             [own_ref[j, :, m * LANES : (m + 1) * LANES] for m in range(tiles)] + [side],
         )
     clear(ghost_ref, DEPTH, MARGIN)
+    for copy in copies:
+        copy.wait()
+    for j in range(DEPTH):
+        put(window_ref, skip + j, slab_row(south_ref, j, cols))
 
     def widen(ref, used, matrix_ref, first):
         for g in range(groups):
@@ -543,7 +552,9 @@
     count, _, blocks = layout(cols, groups)
     smem = pl.BlockSpec(memory_space=pltpu.SMEM)
     vmem = pl.BlockSpec(memory_space=pltpu.VMEM)
+    somewhere = pl.BlockSpec(memory_space=pl.ANY)
     plane = pltpu.VMEM((total, count, SUB, LANES), jnp.float32)
+    late = around[2:]
     tiles = max(cols // LANES + 1, blocks)
     return pl.pallas_call(
         functools.partial(sweep_kernel, channels % SUB),
@@ -551,7 +562,7 @@
             jax.ShapeDtypeStruct((rows, padded, cols), jnp.float32),
             jax.ShapeDtypeStruct((channels, rows, cols), jnp.float32),
         ),
-        in_specs=[smem] * 3 + [vmem] * (1 + len(around)),
+        in_specs=[smem] * 3 + [vmem] * 3 + [somewhere] * len(late),
         out_specs=(vmem, vmem),
         scratch_shapes=[
             pltpu.VMEM((groups, tiles, (MARGIN + rows) * SUB, LANES), jnp.float32),
@@ -566,19 +577,23 @@
             pltpu.VMEM((groups, cols + LANES, blocks * LANES), jnp.bfloat16),
             pltpu.VMEM((groups, blocks * LANES, cols), jnp.bfloat16),
             pltpu.VMEM((groups, cols + 2 * LANES, blocks * LANES), jnp.bfloat16),
-        ],
+        ]
+        + [pltpu.VMEM(x.shape, jnp.float32) for x in late]
+        + [pltpu.SemaphoreType.DMA((len(late),))],
         compiler_params=params(28),
         name="sweeps",
     )(where, length_scale, sigma, own, *around)
 
 
-def gather_kernel(channels, pair, fine_ref, obs_ref, out_ref, left_ref):
+def gather_kernel(channels, pair, fine_ref, field_ref, obs_ref, out_ref, field_out_ref, left_ref, done_ref):
+    copy = pltpu.make_async_copy(field_ref, field_out_ref, done_ref)
+    copy.start()
     senders, padded, slots = out_ref.shape
     rows, _, cols = fine_ref.shape
     high, low = split(fine_ref[...].reshape(rows * padded, cols))
     left_ref[:, :cols] = high
     left_ref[:, cols:] = low
-    at_row, at_col = channels % SUB, (channels + 1) % SUB
+    at_row, at_col = channels, channels + 1
     col_iota = lax.broadcasted_iota(jnp.int32, (cols, slots), 0).astype(jnp.float32)
 
     def body(step, carry):
@@ -591,36 +606,39 @@
             left_ref[...], jnp.concatenate([hot, hot], axis=0), preferred_element_type=jnp.float32
         )
         for s in range(pair):
-            row = jnp.broadcast_to(obs_ref[step * pair + s, at_row : at_row + 1, :], (padded, slots))
-            total = jnp.zeros((padded, slots), jnp.float32)
+            row = jnp.broadcast_to(obs_ref[step * pair + s, at_row : at_row + 1, :], (SUB, slots))
+            total = [jnp.zeros((SUB, slots), jnp.float32)] * (padded // SUB)
             for j in range(rows):
-                piece = found[j * padded : (j + 1) * padded, s * slots : (s + 1) * slots]
-                total = jnp.where(row == float(j), piece, total)
-            out_ref[step * pair + s] = total
+                here = row == float(j)
+                for g in range(padded // SUB):
+                    at = j * padded + g * SUB
+                    piece = found[at : at + SUB, s * slots : (s + 1) * slots]
+                    total[g] = jnp.where(here, piece, total[g])
+            for g in range(padded // SUB):
+                out_ref[step * pair + s, g * SUB : (g + 1) * SUB] = total[g]
         return carry
 
     lax.fori_loop(0, senders // pair, body, 0)
-
-
-def gather(fine, obs, channels):
+    copy.wait()
+
+
+def gather(fine, field, obs, channels):
     rows, padded, cols = fine.shape
     senders, _, slots = obs.shape
-    pair = 2 if senders % 2 == 0 else 1
-    where_group = channels // SUB
+    pair = 16 if senders % 16 == 0 else 1
     vmem = pl.BlockSpec(memory_space=pltpu.VMEM)
     return pl.pallas_call(
         functools.partial(gather_kernel, channels, pair),
-        grid=(1,),
-        out_shape=jax.ShapeDtypeStruct((senders, padded, slots), jnp.float32),
-        in_specs=[
-            pl.BlockSpec((rows, padded, cols), lambda i: (0, 0, 0)),
-            pl.BlockSpec((senders, SUB, slots), lambda i: (0, where_group, 0)),
-        ],
-        out_specs=pl.BlockSpec((senders, padded, slots), lambda i: (0, 0, 0)),
-        scratch_shapes=[pltpu.VMEM((rows * padded, 2 * cols), jnp.bfloat16)],
-        compiler_params=params(12),
+        out_shape=(
+            jax.ShapeDtypeStruct((senders, padded, slots), jnp.float32),
+            jax.ShapeDtypeStruct(field.shape, jnp.float32),
+        ),
+        in_specs=[vmem] * 3,
+        out_specs=(vmem, pl.BlockSpec(memory_space=pl.ANY)),
+        scratch_shapes=[pltpu.VMEM((rows * padded, 2 * cols), jnp.bfloat16), pltpu.SemaphoreType.DMA],
+        compiler_params=params(28),
         name="gather",
-    )(fine, obs)
+    )(fine, field, obs)
 
 
 def per_device(
@@ -661,8 +679,8 @@
     west, east = moves.east(east), moves.west(west)
     top, low = slabs(own, west, east)
     around = (west, east, *moves.slabs(kind, top, low, parts))
-    fine, diffused = sweeps(where, own, around, length_scale, sigma, channels)
-    local_fit = gather(fine, arrived, channels)
+    fine, field = sweeps(where, own, around, length_scale, sigma, channels)
+    local_fit, diffused = gather(fine, field, arrived, channels)
     returned = lax.all_to_all(local_fit, ("lat", "lon"), split_axis=0, concat_axis=0, tiled=True)
     obs_fit = pl.pallas_call(
         functools.partial(unpack_kernel, channels, padded),

time: 93.5 us -> 89.6 us (0.958)
  Pallas kernels: 32.2 us -> 28.3 us
    pallas_call x1, Pallas kernels: 7.65 us -> 5.44 us  [gather(): pl.pallas_call(functools.partial(gather_kernel, channels, pair), out_shap...]
    pallas_call x1, Pallas kernels: 15.2 us -> 14.2 us  [sweeps(): pl.pallas_call(functools.partial(sweep_kernel, channels % SUB), out_shape...]
where the time goes in v4:
time: 89.6 us; the launch traced here: 88.8 us
  Pallas kernels  28.3 us (32%)
  blocking collectives  24 us (27%)
  starting transfers between devices  19.9 us (22%)
  waiting for transfers between devices  14.5 us (16%)
  between operations  1.45 us (2%)
    all_to_all x1, blocking collectives, per_device(): lax.all_to_all(local_fit, ('lat', 'lon'), split_axis=0, concat_axis=0, ti...  24 us
    pallas_call x1, Pallas kernels, sweeps(): pl.pallas_call(functools.partial(sweep_kernel, channels % SUB), out_shape...  14.2 us
    all_to_all x1, waiting for transfers between devices, per_device(): lax.all_to_all(outgoing.reshape(owners, padded, slots), ('lat', 'lon'), s...  12.3 us
    all_to_all x1, starting transfers between devices, per_device(): lax.all_to_all(outgoing.reshape(owners, padded, slots), ('lat', 'lon'), s...  7.3 us
    pallas_call x1, Pallas kernels, scatter(): pl.pallas_call(functools.partial(scatter_kernel, channels, chunk), out_sh...  5.9 us
    pallas_call x1, Pallas kernels, gather(): pl.pallas_call(functools.partial(gather_kernel, channels, pair), out_shap...  5.44 us
    ppermute x1, starting transfers between devices, west(): return lax.ppermute(x, 'lon', self.to_west)  3.84 us
    ppermute x1, starting transfers between devices, north(): return lax.ppermute(x, 'lat', self.to_north)  3.79 us
  transfers between devices with their start and end apart: 7, of which 2 were waited for; matrix products, arithmetic and copies ran while one was open for 1% of the time, Pallas kernels for 0%

profile of v4, /device:TPU:0, one launch (start us, length us, event | category | flops | bytes accessed | tf_op | source)
XLA Modules:
  0.0 88.8 jit_solution(10783615422198197307)
XLA Ops:
  0.6 0.0 copy-start.4
  0.6 0.0 copy-start.2
  0.7 0.0 copy-start.3
  0.7 1.8 %pack.1 = f32[768,128]{1,0:T(8,128)} custom-call(s32[1,32]{1,0:T(1,128)} %count_ref.1, f32[672,128]{1,0:T(8,128)} %bitcast.11, s32[32,128]{1,0:T(8,128)} %bitcast.13), custom_call_target="tpu_custom_call" | custom-call | tf_op jit(solution)/shard_map/pack/pallas_call | solution.py:654
  2.5 7.3 %all-to-all-start = ((f32[32,24,128]{2,1,0:T(8,128)}), f32[32,24,128]{2,1,0:T(8,128)S(1)}, u32[]{:S(2)}, u32[]{:S(2)}) async-start(f32[32,24,128]{2,1,0:T(8,128)} %bitcast.10), calls=%async_computation | async-start | bytes 786432 | tf_op jit(solution)/shard_map/all_to_all | solution.py:667
  9.8 0.0 copy-done.4
  9.8 0.5 slice.3
  11.0 12.3 %all-to-all-done.obs_ref = f32[32,24,128]{2,1,0:T(8,128)S(1)} async-done(((f32[32,24,128]{2,1,0:T(8,128)}), f32[32,24,128]{2,1,0:T(8,128)S(1)}, u32[]{:S(2)}, u32[]{:S(2)}) %all-to-all-start) | async-done | bytes 393248 | tf_op jit(solution)/shard_map/all_to_all | solution.py:667
  23.4 0.0 copy-done.2
  23.4 0.0 copy-done.3
  23.4 5.9 %scatter.1 = (f32[48,24,256]{2,1,0:T(8,128)S(1)}, f32[5,24,128]{2,1,0:T(8,128)S(1)}, f32[5,24,128]{2,1,0:T(8,128)S(1)}, f32[12,24,128]{2,1,0:T(8,128)S(1)}, f32[12,24,128]{2,1,0:T(8,128)S(1)}) custom-call(f32[32,24,128]{2,1,0:T(8,128)S(1)} %all-to-all-done.obs_ref, s32[48,256]{1,0:T(8,128)S(1)} %copy-done.3, f32[2,48,256]{2,1,0:T(8,128)S(1)} %copy-done.2), custom_call_target="tpu_custom_call" | custom-call | flops 4831838208 | tf_op jit(solution)/shard_map/scatter/pallas_call | solution.py:293
  29.3 0.0 copy-start
  29.3 0.0 copy-start.1
  29.3 0.9 %collective-permute-start.64 = (f32[5,24,128]{2,1,0:T(8,128)S(1)}, f32[5,24,128]{2,1,0:T(8,128)S(1)}, u32[]{:S(2)}, u32[]{:S(2)}) collective-permute-start(f32[5,24,128]{2,1,0:T(8,128)S(1)} %get-tuple-element.194), channel_id=1, source_target_pairs={{0,1},{1,2},{2,3},{3,4},{4,5},{5,6},{6,7},{7,0},{8,9},{9,10},{10,1... | collective-permute-start | bytes 184328 | tf_op jit(solution)/shard_map/ppermute | solution.py:195
  30.2 3.8 %collective-permute-start.65 = (f32[5,24,128]{2,1,0:T(8,128)S(1)}, f32[5,24,128]{2,1,0:T(8,128)S(1)}, u32[]{:S(2)}, u32[]{:S(2)}) collective-permute-start(f32[5,24,128]{2,1,0:T(8,128)S(1)} %get-tuple-element.195), channel_id=1, source_target_pairs={{1,0},{2,1},{3,2},{4,3},{5,4},{6,5},{7,6},{0,7},{9,8},{10,9},{11,1... | collective-permute-start | bytes 184328 | tf_op jit(solution)/shard_map/ppermute | solution.py:198
  34.1 0.1 pad_add_fusion.where_ref
  34.1 2.1 %collective-permute-done.64.west_ref.refs_1_ = f32[5,24,128]{2,1,0:T(8,128)S(1)} collective-permute-done((f32[5,24,128]{2,1,0:T(8,128)S(1)}, f32[5,24,128]{2,1,0:T(8,128)S(1)}, u32[]{:S(2)}, u32[]{:S(2)}) %collective-permute-start.64) | collective-permute-done | bytes 61472 | tf_op jit(solution)/shard_map/ppermute | solution.py:195
  36.3 0.0 collective-permute-done.65.east_ref.refs_2_
  36.3 0.2 slabs.1
  36.5 7.8 %conditional.1 = (f32[27,24,128]{2,1,0:T(8,128)}, f32[27,24,128]{2,1,0:T(8,128)}, f32[27,24,128]{2,1,0:T(8,128)}, f32[12,24,128]{2,1,0:T(8,128)}) conditional(s32[]{:T(128)} %clamp.3, (f32[27,24,128]{2,1,0:T(8,128)S(1)}, f32[27,24,128]{2,1,0:T(8,128)S(1)}, f32[12,24,128]{2,1,0:T(8,128)S(1)}) %tuple.88, ...), branch_computations={%region_0.1_spmd, %region_1.2_spmd, %region_2.3_spmd, %region_3.4_... | conditional | bytes 4571328 | solution.py:222
  36.5 1.3 %collective-permute-start.42 = (f32[12,24,128]{2,1,0:T(8,128)S(1)}, f32[12,24,128]{2,1,0:T(8,128)}, u32[]{:S(2)}, u32[]{:S(2)}) collective-permute-start(f32[12,24,128]{2,1,0:T(8,128)S(1)} %get-tuple-element.148), channel_id=1, source_target_pairs={{24,29},{25,28},{26,27},{27,26},{28,25},{29,24},{30,31},{31,30}} | collective-permute-start | bytes 442376 | tf_op jit(solution)/shard_map/cond/branch_10_fun/ppermute | solution.py:214
  37.8 1.3 %collective-permute-start.41 = (f32[27,24,128]{2,1,0:T(8,128)S(1)}, f32[27,24,128]{2,1,0:T(8,128)}, u32[]{:S(2)}, u32[]{:S(2)}) collective-permute-start(f32[27,24,128]{2,1,0:T(8,128)S(1)} %get-tuple-element.147), channel_id=1, source_target_pairs={{8,0},{16,8},{24,16},{9,1},{17,9},{25,17},{10,2},{18,10},{26,18},{... | collective-permute-start | bytes 995336 | tf_op jit(solution)/shard_map/cond/branch_10_fun/ppermute | solution.py:204
  39.1 3.8 %collective-permute-start.40 = (f32[27,24,128]{2,1,0:T(8,128)S(1)}, f32[27,24,128]{2,1,0:T(8,128)}, u32[]{:S(2)}, u32[]{:S(2)}) collective-permute-start(f32[27,24,128]{2,1,0:T(8,128)S(1)} %get-tuple-element.149), channel_id=1, source_target_pairs={{0,8},{8,16},{16,24},{1,9},{9,17},{17,25},{2,10},{10,18},{18,26},{... | collective-permute-start | bytes 995336 | tf_op jit(solution)/shard_map/cond/branch_10_fun/ppermute | solution.py:201
  42.9 0.0 collective-permute-done.42
  42.9 1.4 %collective-permute-start.43 = (f32[27,24,128]{2,1,0:T(8,128)S(1)}, f32[27,24,128]{2,1,0:T(8,128)}, u32[]{:S(2)}, u32[]{:S(2)}) collective-permute-start(f32[27,24,128]{2,1,0:T(8,128)S(1)} %get-tuple-element.149), channel_id=1, source_target_pairs={{24,28},{25,27},{26,26},{27,25},{28,24},{29,31},{30,30},{31,29}} | collective-permute-start | bytes 995336 | tf_op jit(solution)/shard_map/cond/branch_10_fun/ppermute | solution.py:216
  44.3 0.0 collective-permute-done.41
  44.3 0.0 collective-permute-done.40
  44.3 0.0 collective-permute-done.43
  44.3 0.0 copy-done
  44.3 0.0 copy-done.1
  44.3 14.2 %sweeps.1 = (f32[48,24,256]{2,1,0:T(8,128)S(1)}, f32[21,48,256]{2,1,0:T(8,128)S(1)}) custom-call(s32[3]{0:T(128)S(1)} %pad_add_fusion.where_ref, f32[21]{0:T(128)S(1)} %copy-done, f32[21]{0:T(128)S(1)} %copy-done.1, f32[48,24,256]{2,1,0:T(8,128)S(1)} %get-tuple-element.193.own_ref.refs_0_, f32[5,24,128]{2,1,0:T(8,128)S(1)} %collective-permute-done.64.west_ref.refs_1_, ...), custom_call_target="tpu_custom_call" | custom-call | tf_op jit(solution)/shard_map/sweeps/pallas_call | solution.py:559
  58.5 5.4 %gather.1 = (f32[32,24,128]{2,1,0:T(8,128)S(1)}, f32[21,48,256]{2,1,0:T(8,128)}) custom-call(f32[48,24,256]{2,1,0:T(8,128)S(1)} %get-tuple-element.204.fine_ref, f32[21,48,256]{2,1,0:T(8,128)S(1)} %get-tuple-element.205.field_ref, f32[32,24,128]{2,1,0:T(8,128)S(1)} %all-to-all-done.obs_ref), custom_call_target="tpu_custom_call" | custom-call | tf_op jit(solution)/shard_map/gather/pallas_call | solution.py:630
  64.0 24.0 %all_to_all.10 = f32[32,24,128]{2,1,0:T(8,128)S(1)} all-to-all(f32[32,24,128]{2,1,0:T(8,128)S(1)} %get-tuple-element.206), channel_id=1, replica_groups=mesh['lat'=4,'lon'=8] {'lat','lon'}, dimensions={0} | all-to-all | bytes 786432 | tf_op jit(solution)/shard_map/all_to_all | solution.py:684
  88.0 0.8 unpack.1
Async XLA Ops:
  0.6 9.2 %copy-start.4 = (s32[256]{0:T(256)S(1)}, s32[256]{0:T(256)}, u32[]{:S(2)}) copy-start(s32[256]{0:T(256)} %param.29) | copy-start | bytes 3076
  0.6 22.7 %copy-start.2 = (f32[2,48,256]{2,1,0:T(8,128)S(1)}, f32[2,48,256]{2,1,0:T(8,128)}, u32[]{:S(2)}) copy-start(f32[2,48,256]{2,1,0:T(8,128)} %kappa_ref.1) | copy-start | bytes 294916
  0.7 22.7 %copy-start.3 = (s32[48,256]{1,0:T(8,128)S(1)}, s32[48,256]{1,0:T(8,128)}, u32[]{:S(2)}) copy-start(s32[48,256]{1,0:T(8,128)} %bottom_ref.1) | copy-start | bytes 147460
  2.5 20.8 %all-to-all-start = ((f32[32,24,128]{2,1,0:T(8,128)}), f32[32,24,128]{2,1,0:T(8,128)S(1)}, u32[]{:S(2)}, u32[]{:S(2)}) async-start(f32[32,24,128]{2,1,0:T(8,128)} %bitcast.10), calls=%async_computation | async-start | bytes 786432 | tf_op jit(solution)/shard_map/all_to_all | solution.py:667
  29.3 15.1 %copy-start = (f32[21]{0:T(128)S(1)}, f32[21]{0:T(128)}, u32[]{:S(2)}) copy-start(f32[21]{0:T(128)} %scale_ref.1) | copy-start | bytes 256
  29.3 15.1 %copy-start.1 = (f32[21]{0:T(128)S(1)}, f32[21]{0:T(128)}, u32[]{:S(2)}) copy-start(f32[21]{0:T(128)} %sigma_ref.1) | copy-start | bytes 256
  29.3 7.0 %collective-permute-start.64 = (f32[5,24,128]{2,1,0:T(8,128)S(1)}, f32[5,24,128]{2,1,0:T(8,128)S(1)}, u32[]{:S(2)}, u32[]{:S(2)}) collective-permute-start(f32[5,24,128]{2,1,0:T(8,128)S(1)} %get-tuple-element.194), channel_id=1, source_target_pairs={{0,1},{1,2},{2,3},{3,4},{4,5},{5,6},{6,7},{7,0},{8,9},{9,10},{10,1... | collective-permute-start | bytes 184328 | tf_op jit(solution)/shard_map/ppermute | solution.py:195
  30.2 6.0 %collective-permute-start.65 = (f32[5,24,128]{2,1,0:T(8,128)S(1)}, f32[5,24,128]{2,1,0:T(8,128)S(1)}, u32[]{:S(2)}, u32[]{:S(2)}) collective-permute-start(f32[5,24,128]{2,1,0:T(8,128)S(1)} %get-tuple-element.195), channel_id=1, source_target_pairs={{1,0},{2,1},{3,2},{4,3},{5,4},{6,5},{7,6},{0,7},{9,8},{10,9},{11,1... | collective-permute-start | bytes 184328 | tf_op jit(solution)/shard_map/ppermute | solution.py:198
  36.5 6.4 %collective-permute-start.42 = (f32[12,24,128]{2,1,0:T(8,128)S(1)}, f32[12,24,128]{2,1,0:T(8,128)}, u32[]{:S(2)}, u32[]{:S(2)}) collective-permute-start(f32[12,24,128]{2,1,0:T(8,128)S(1)} %get-tuple-element.148), channel_id=1, source_target_pairs={{24,29},{25,28},{26,27},{27,26},{28,25},{29,24},{30,31},{31,30}} | collective-permute-start | bytes 442376 | tf_op jit(solution)/shard_map/cond/branch_10_fun/ppermute | solution.py:214
  37.8 6.5 %collective-permute-start.41 = (f32[27,24,128]{2,1,0:T(8,128)S(1)}, f32[27,24,128]{2,1,0:T(8,128)}, u32[]{:S(2)}, u32[]{:S(2)}) collective-permute-start(f32[27,24,128]{2,1,0:T(8,128)S(1)} %get-tuple-element.147), channel_id=1, source_target_pairs={{8,0},{16,8},{24,16},{9,1},{17,9},{25,17},{10,2},{18,10},{26,18},{... | collective-permute-start | bytes 995336 | tf_op jit(solution)/shard_map/cond/branch_10_fun/ppermute | solution.py:204
  39.1 5.2 %collective-permute-start.40 = (f32[27,24,128]{2,1,0:T(8,128)S(1)}, f32[27,24,128]{2,1,0:T(8,128)}, u32[]{:S(2)}, u32[]{:S(2)}) collective-permute-start(f32[27,24,128]{2,1,0:T(8,128)S(1)} %get-tuple-element.149), channel_id=1, source_target_pairs={{0,8},{8,16},{16,24},{1,9},{9,17},{17,25},{2,10},{10,18},{18,26},{... | collective-permute-start | bytes 995336 | tf_op jit(solution)/shard_map/cond/branch_10_fun/ppermute | solution.py:201
  42.9 1.4 %collective-permute-start.43 = (f32[27,24,128]{2,1,0:T(8,128)S(1)}, f32[27,24,128]{2,1,0:T(8,128)}, u32[]{:S(2)}, u32[]{:S(2)}) collective-permute-start(f32[27,24,128]{2,1,0:T(8,128)S(1)} %get-tuple-element.149), channel_id=1, source_target_pairs={{24,28},{25,27},{26,26},{27,25},{28,24},{29,31},{30,30},{31,29}} | collective-permute-start | bytes 995336 | tf_op jit(solution)/shard_map/cond/branch_10_fun/ppermute | solution.py:216

commit v5 on v4

--- a/solution.py
+++ b/solution.py
@@ -32,10 +32,10 @@
     return x if shift == 0 else pltpu.roll(x, shift, x.ndim - 1)
 
 
-def pack_kernel(channels, padded, cols, count_ref, value_ref, cell_ref, out_ref):
+def pack_kernel(channels, width, cols, count_ref, value_ref, cell_ref, out_ref):
     owners, slots = cell_ref.shape
     for c in range(channels):
-        out_ref[pl.ds(c, owners, stride=padded), :] = value_ref[pl.ds(c * owners, owners), :]
+        out_ref[pl.ds(c, owners, stride=width), :] = value_ref[pl.ds(c * owners, owners), :]
     owner = lax.broadcasted_iota(jnp.int32, (owners, slots), 0)
     count = jnp.zeros((owners, slots), jnp.int32)
     for d in range(owners):
@@ -44,16 +44,21 @@
     row = jnp.floor((cell + 0.5) * (1.0 / cols))
     col = cell - row * cols
     row = jnp.where(lane_iota((owners, slots)) < count, row, -1.0)
-    out_ref[pl.ds(channels, owners, stride=padded), :] = row
-    out_ref[pl.ds(channels + 1, owners, stride=padded), :] = col
-    for c in range(channels + 2, padded):
-        out_ref[pl.ds(c, owners, stride=padded), :] = jnp.zeros((owners, slots), jnp.float32)
-
-
-def unpack_kernel(channels, padded, in_ref, out_ref):
-    owners = out_ref.shape[1]
+    out_ref[pl.ds(channels, owners, stride=width), :] = row
+    out_ref[pl.ds(channels + 1, owners, stride=width), :] = col
+
+
+def unpack_kernel(in_ref, out_ref):
+    channels, owners, _ = out_ref.shape
     for c in range(channels):
-        out_ref[c] = in_ref[pl.ds(c, owners, stride=padded), :]
+        out_ref[c] = in_ref[pl.ds(c, owners, stride=channels), :]
+
+
+def exchange(x, owners):
+    rows, slots = x.shape
+    x = x.reshape(owners, 1, rows // owners * slots)
+    x = lax.all_to_all(x, ("lat", "lon"), split_axis=0, concat_axis=0, tiled=True)
+    return x.reshape(rows, slots)
 
 
 def layout(cols, groups):
@@ -203,36 +208,32 @@
     def south(self, x):
         return lax.ppermute(x, "lat", self.to_south)
 
-    def slabs(self, kind, top, low, parts):
-        def pairs(tile, part):
-            return [
-                (self.first + s, self.first + (tile - part - s) % self.n_lon) for s in range(self.n_lon)
-            ]
-
-        def branch(tile, kind):
-            def run(top, low, parts):
-                part = lax.ppermute(parts[kind], ("lat", "lon"), pairs(tile, kind))
-                part, slab = lax.optimization_barrier((part, top))
-                whole = lax.ppermute(slab, ("lat", "lon"), pairs(tile, 1 - kind))
-                return self.north(top), self.south(low), whole, part
-
-            return run
-
-        branches = [branch(t, k) for t in range(self.n_lon) for k in (0, 1)]
-        return lax.switch(self.centre_tile * 2 + kind, branches, top, low, parts)
-
-
-def scatter_kernel(channels, chunk, obs_ref, bottom_ref, kappa_ref, *refs):
+    def fold(self, part, send, *operands):
+        first, n = self.first, self.n_lon
+
+        def branch(tile):
+            pairs = [(first + s, first + (tile - s) % n) for s in range(n)]
+            return lambda *xs: send(lambda x: lax.ppermute(x, ("lat", "lon"), pairs), *xs)
+
+        tile = lax.rem(self.centre_tile + n - part, n)
+        return lax.switch(tile, [branch(t) for t in range(n)], *operands)
+
+
+def scatter_kernel(channels, chunk, where_ref, obs_ref, bottom_ref, kappa_ref, *refs):
     own_ref, west_ref, east_ref = refs[:3]
-    part_refs, (left_ref, right_ref, sum_ref) = refs[3:5], refs[5:]
-    senders, padded, slots = obs_ref.shape
-    rows, _, cols = own_ref.shape
+    part_ref, left_ref, right_ref, sum_ref, blocks_ref = refs[3:]
+    rows, padded, cols = own_ref.shape
+    slots = obs_ref.shape[1]
+    senders = blocks_ref.shape[0] // padded
+    for c in range(channels + 2):
+        blocks_ref[pl.ds(c, senders, stride=padded), :] = obs_ref[pl.ds(c, senders, stride=channels + 2), :]
     row_iota = lax.broadcasted_iota(jnp.int32, (rows, slots), 0).astype(jnp.float32)
     col_iota = lax.broadcasted_iota(jnp.int32, (cols, slots), 0).astype(jnp.float32)
 
     def body(step, carry):
         for s in range(chunk):
-            x = obs_ref[step * chunk + s]
+            at = pl.multiple_of((step * chunk + s) * padded, SUB)
+            x = blocks_ref[pl.ds(at, padded), :]
             high, low = split(x)
             on_row = (row_iota == x[channels : channels + 1, :]).astype(jnp.bfloat16)
             on_col = (col_iota == x[channels + 1 : channels + 2, :]).astype(jnp.bfloat16)
@@ -271,41 +272,46 @@
                 ]
     pack_strip(lambda j: own_ref[j, :, :LANES], rows, 0, west_ref)
     pack_strip(lambda j: own_ref[j, :, cols - LANES :], rows, LANES - DEPTH, east_ref)
-    for ref, start in zip(part_refs, part_starts(cols)):
-        m, shift = divmod(start, LANES)
-        for j in range(DEPTH):
-            x = own_ref[rows - DEPTH + j, :, m * LANES : (m + 1) * LANES]
-            y = own_ref[rows - DEPTH + j, :, (m + 1) * LANES : (m + 2) * LANES]
-            here = lane_iota(x.shape) < LANES - shift
-            ref[j] = jnp.where(here, roll_lanes(x, -shift), roll_lanes(y, -shift))
-
-
-def scatter(obs, bottom_level, diffusivity, channels):
-    senders, padded, slots = obs.shape
+    for kind, start in enumerate(part_starts(cols)):
+
+        @pl.when(where_ref[2] == kind)
+        def _():
+            m, shift = divmod(start, LANES)
+            for j in range(DEPTH):
+                x = own_ref[rows - DEPTH + j, :, m * LANES : (m + 1) * LANES]
+                y = own_ref[rows - DEPTH + j, :, (m + 1) * LANES : (m + 2) * LANES]
+                here = lane_iota(x.shape) < LANES - shift
+                part_ref[j] = jnp.where(here, roll_lanes(x, -shift), roll_lanes(y, -shift))
+
+
+def scatter(where, obs, bottom_level, diffusivity, channels, padded):
+    slots = obs.shape[1]
+    senders = obs.shape[0] // (channels + 2)
     rows, cols = bottom_level.shape
     tiles = cols // LANES
     chunk = 16 if senders % 16 == 0 else 1
     vmem = pl.BlockSpec(memory_space=pltpu.VMEM)
     side = (strip_count(rows), padded, LANES)
     part = (DEPTH, padded, LANES)
-    shapes = [(rows, padded, cols), side, side, part, part]
+    shapes = [(rows, padded, cols), side, side, part]
     shapes = [jax.ShapeDtypeStruct(shape, jnp.float32) for shape in shapes]
     return pl.pallas_call(
         functools.partial(scatter_kernel, channels, chunk),
         out_shape=tuple(shapes),
-        in_specs=[vmem] * 3,
+        in_specs=[pl.BlockSpec(memory_space=pltpu.SMEM)] + [vmem] * 3,
         out_specs=(vmem,) * len(shapes),
         scratch_shapes=[
             pltpu.VMEM((2 * channels * rows, chunk * slots), jnp.bfloat16),
             pltpu.VMEM((cols, chunk * slots), jnp.bfloat16),
             pltpu.VMEM((tiles, padded * rows, LANES), jnp.float32),
+            pltpu.VMEM((senders * padded, slots), jnp.float32),
         ],
         compiler_params=params(28),
         cost_estimate=pl.CostEstimate(
             flops=4 * senders * slots * padded * rows * cols, bytes_accessed=0, transcendentals=0
         ),
         name="scatter",
-    )(obs, bottom_level, diffusivity)
+    )(where, obs, bottom_level, diffusivity)
 
 
 def east_of(xs, m):
@@ -585,28 +591,34 @@
     )(where, length_scale, sigma, own, *around)
 
 
-def gather_kernel(channels, pair, fine_ref, field_ref, obs_ref, out_ref, field_out_ref, left_ref, done_ref):
+def gather_kernel(channels, pair, fine_ref, field_ref, obs_ref, out_ref, field_out_ref, *scratch):
+    left_ref, cells_ref, blocks_ref, done_ref = scratch
     copy = pltpu.make_async_copy(field_ref, field_out_ref, done_ref)
     copy.start()
-    senders, padded, slots = out_ref.shape
-    rows, _, cols = fine_ref.shape
+    rows, padded, cols = fine_ref.shape
+    slots = obs_ref.shape[1]
+    senders = blocks_ref.shape[0] // padded
+    for i in (0, 1):
+        cells_ref[pl.ds(i, senders, stride=SUB), :] = obs_ref[
+            pl.ds(channels + i, senders, stride=channels + 2), :
+        ]
     high, low = split(fine_ref[...].reshape(rows * padded, cols))
     left_ref[:, :cols] = high
     left_ref[:, cols:] = low
-    at_row, at_col = channels, channels + 1
     col_iota = lax.broadcasted_iota(jnp.int32, (cols, slots), 0).astype(jnp.float32)
 
     def body(step, carry):
         hots = []
         for s in range(pair):
-            col = obs_ref[step * pair + s, at_col : at_col + 1, :]
+            col = cells_ref[pl.ds(pl.multiple_of((step * pair + s) * SUB, SUB), SUB), :][1:2, :]
             hots.append((col_iota == col).astype(jnp.bfloat16))
         hot = jnp.concatenate(hots, axis=1)
         found = jnp.dot(
             left_ref[...], jnp.concatenate([hot, hot], axis=0), preferred_element_type=jnp.float32
         )
         for s in range(pair):
-            row = jnp.broadcast_to(obs_ref[step * pair + s, at_row : at_row + 1, :], (SUB, slots))
+            row = cells_ref[pl.ds(pl.multiple_of((step * pair + s) * SUB, SUB), SUB), :][:1, :]
+            row = jnp.broadcast_to(row, (SUB, slots))
             total = [jnp.zeros((SUB, slots), jnp.float32)] * (padded // SUB)
             for j in range(rows):
                 here = row == float(j)
@@ -615,27 +627,36 @@
                     piece = found[at : at + SUB, s * slots : (s + 1) * slots]
                     total[g] = jnp.where(here, piece, total[g])
             for g in range(padded // SUB):
-                out_ref[step * pair + s, g * SUB : (g + 1) * SUB] = total[g]
+                at = pl.multiple_of((step * pair + s) * padded + g * SUB, SUB)
+                blocks_ref[pl.ds(at, SUB), :] = total[g]
         return carry
 
     lax.fori_loop(0, senders // pair, body, 0)
+    for c in range(channels):
+        out_ref[pl.ds(c, senders, stride=channels), :] = blocks_ref[pl.ds(c, senders, stride=padded), :]
     copy.wait()
 
 
 def gather(fine, field, obs, channels):
     rows, padded, cols = fine.shape
-    senders, _, slots = obs.shape
+    slots = obs.shape[1]
+    senders = obs.shape[0] // (channels + 2)
     pair = 16 if senders % 16 == 0 else 1
     vmem = pl.BlockSpec(memory_space=pltpu.VMEM)
     return pl.pallas_call(
         functools.partial(gather_kernel, channels, pair),
         out_shape=(
-            jax.ShapeDtypeStruct((senders, padded, slots), jnp.float32),
+            jax.ShapeDtypeStruct((senders * channels, slots), jnp.float32),
             jax.ShapeDtypeStruct(field.shape, jnp.float32),
         ),
         in_specs=[vmem] * 3,
         out_specs=(vmem, pl.BlockSpec(memory_space=pl.ANY)),
-        scratch_shapes=[pltpu.VMEM((rows * padded, 2 * cols), jnp.bfloat16), pltpu.SemaphoreType.DMA],
+        scratch_shapes=[
+            pltpu.VMEM((rows * padded, 2 * cols), jnp.bfloat16),
+            pltpu.VMEM((senders * SUB, slots), jnp.float32),
+            pltpu.VMEM((senders * padded, slots), jnp.float32),
+            pltpu.SemaphoreType.DMA,
+        ],
         compiler_params=params(28),
         name="gather",
     )(fine, field, obs)
@@ -652,9 +673,9 @@
     smem = pl.BlockSpec(memory_space=pltpu.SMEM)
 
     outgoing = pl.pallas_call(
-        functools.partial(pack_kernel, channels, padded, cols),
+        functools.partial(pack_kernel, channels, channels + 2, cols),
         grid=(1,),
-        out_shape=jax.ShapeDtypeStruct((owners * padded, slots), jnp.float32),
+        out_shape=jax.ShapeDtypeStruct((owners * (channels + 2), slots), jnp.float32),
         in_specs=[
             smem,
             pl.BlockSpec((channels * owners, slots), lambda i: (0, 0)),
@@ -664,9 +685,7 @@
         compiler_params=params(60),
         name="pack",
     )(obs_count, obs_value.reshape(channels * owners, slots), obs_cell[0])
-    arrived = lax.all_to_all(
-        outgoing.reshape(owners, padded, slots), ("lat", "lon"), split_axis=0, concat_axis=0, tiled=True
-    )
+    arrived = exchange(outgoing, owners)
 
     centre = lax.rem(partner[0] + lax.axis_index("lon") * cols, cols * n_lon)
     centre_col = centre % cols
@@ -675,21 +694,26 @@
     where = jnp.stack([is_top, centre_col, kind])
     moves = Moves(n_lat, n_lon, centre // cols)
 
-    own, west, east, *parts = scatter(arrived, bottom_level, diffusivity, channels)
+    own, west, east, part = scatter(where, arrived, bottom_level, diffusivity, channels, padded)
     west, east = moves.east(east), moves.west(west)
+    part = moves.fold(kind, lambda fold, x: fold(x), part)
     top, low = slabs(own, west, east)
-    around = (west, east, *moves.slabs(kind, top, low, parts))
+
+    def send(fold, top, low):
+        return moves.north(top), moves.south(low), fold(top)
+
+    around = (west, east, *moves.fold(1 - kind, send, top, low), part)
     fine, field = sweeps(where, own, around, length_scale, sigma, channels)
     local_fit, diffused = gather(fine, field, arrived, channels)
-    returned = lax.all_to_all(local_fit, ("lat", "lon"), split_axis=0, concat_axis=0, tiled=True)
+    returned = exchange(local_fit, owners)
     obs_fit = pl.pallas_call(
-        functools.partial(unpack_kernel, channels, padded),
+        unpack_kernel,
         out_shape=jax.ShapeDtypeStruct((channels, owners, slots), jnp.float32),
         in_specs=[vmem],
         out_specs=vmem,
         compiler_params=params(),
         name="unpack",
-    )(returned.reshape(owners * padded, slots))
+    )(returned)
     return obs_fit[None], diffused
 
 

time: 89.6 us -> 88.4 us (0.987)
  waiting for transfers between devices: 14.5 us -> 13.4 us
    ppermute x1, waiting for transfers between devices: 2.12 us -> 0.88 us  [east(): return lax.ppermute(x, 'lon', self.to_east)]
  transfers between devices with their start and end apart: 7 -> 7, of which waited for: 2 -> 3; matrix products, arithmetic and copies ran while one was open for 1% -> 1% of each run, Pallas kernels for 0% -> 0%
where the time goes in v5:
time: 88.4 us; the launch traced here: 88.1 us
  Pallas kernels  28.9 us (33%)
  blocking collectives  23.9 us (27%)
  starting transfers between devices  19.8 us (22%)
  waiting for transfers between devices  13.4 us (15%)
  between operations  1.41 us (2%)
    all_to_all x1, blocking collectives, exchange(): lax.all_to_all(x, ('lat', 'lon'), split_axis=0, concat_axis=0, tiled=True)  23.9 us
    pallas_call x1, Pallas kernels, sweeps(): pl.pallas_call(functools.partial(sweep_kernel, channels % SUB), out_shape...  14.1 us
    all_to_all x1, waiting for transfers between devices, exchange(): lax.all_to_all(x, ('lat', 'lon'), split_axis=0, concat_axis=0, tiled=True)  11.9 us
    all_to_all x1, starting transfers between devices, exchange(): lax.all_to_all(x, ('lat', 'lon'), split_axis=0, concat_axis=0, tiled=True)  7.3 us
    pallas_call x1, Pallas kernels, scatter(): pl.pallas_call(functools.partial(scatter_kernel, channels, chunk), out_sh...  6.49 us
    pallas_call x1, Pallas kernels, gather(): pl.pallas_call(functools.partial(gather_kernel, channels, pair), out_shap...  5.52 us
    ppermute x1, starting transfers between devices, west(): return lax.ppermute(x, 'lon', self.to_west)  3.84 us
    ppermute x1, starting transfers between devices, north(): return lax.ppermute(x, 'lat', self.to_north)  3.74 us
  transfers between devices with their start and end apart: 7, of which 3 were waited for; matrix products, arithmetic and copies ran while one was open for 1% of the time, Pallas kernels for 0%

profile of v5, /device:TPU:0, one launch (start us, length us, event | category | flops | bytes accessed | tf_op | source)
XLA Modules:
  0.0 88.1 jit_solution(5309120552158890882)
XLA Ops:
  0.6 0.0 copy-start.4
  0.6 0.0 copy-start.2
  0.7 0.0 copy-start.3
  0.7 1.8 %pack.1 = f32[736,128]{1,0:T(8,128)} custom-call(s32[1,32]{1,0:T(1,128)} %count_ref.1, f32[672,128]{1,0:T(8,128)} %bitcast.16, s32[32,128]{1,0:T(8,128)} %bitcast.18), custom_call_target="tpu_custom_call" | custom-call | tf_op jit(solution)/shard_map/pack/pallas_call | solution.py:675
  2.5 7.3 %all-to-all-start = ((f32[32,1,2944]{2,1,0:T(1,128)}), f32[32,1,2944]{2,1,0:T(1,128)S(1)}, u32[]{:S(2)}, u32[]{:S(2)}) async-start(f32[32,1,2944]{2,1,0:T(1,128)} %bitcast.15), calls=%async_computation | async-start | bytes 753664 | tf_op jit(solution)/shard_map/all_to_all | solution.py:60
  9.8 0.0 copy-done.4
  9.8 0.5 slice.3
  11.0 0.1 pad_add_fusion.where_ref
  11.1 11.9 %all-to-all-done = f32[32,1,2944]{2,1,0:T(1,128)S(1)} async-done(((f32[32,1,2944]{2,1,0:T(1,128)}), f32[32,1,2944]{2,1,0:T(1,128)S(1)}, u32[]{:S(2)}, u32[]{:S(2)}) %all-to-all-start) | async-done | bytes 376864 | tf_op jit(solution)/shard_map/all_to_all | solution.py:60
  23.0 0.0 copy-done.2
  23.0 0.0 copy-done.3
  23.0 6.5 %scatter.1 = (f32[48,24,256]{2,1,0:T(8,128)S(1)}, f32[5,24,128]{2,1,0:T(8,128)S(1)}, f32[5,24,128]{2,1,0:T(8,128)S(1)}, f32[12,24,128]{2,1,0:T(8,128)S(1)}) custom-call(s32[3]{0:T(128)S(1)} %pad_add_fusion.where_ref, f32[736,128]{1,0:T(8,128)S(1)} %bitcast.11, s32[48,256]{1,0:T(8,128)S(1)} %copy-done.3, f32[2,48,256]{2,1,0:T(8,128)S(1)} %copy-done.2), custom_call_target="tpu_custom_call" | custom-call | flops 4831838208 | tf_op jit(solution)/shard_map/scatter/pallas_call | solution.py:298
  29.5 0.0 copy-start
  29.5 0.0 copy-start.1
  29.5 0.9 %collective-permute-start.32 = (f32[5,24,128]{2,1,0:T(8,128)S(1)}, f32[5,24,128]{2,1,0:T(8,128)S(1)}, u32[]{:S(2)}, u32[]{:S(2)}) collective-permute-start(f32[5,24,128]{2,1,0:T(8,128)S(1)} %get-tuple-element.79), channel_id=1, source_target_pairs={{0,1},{1,2},{2,3},{3,4},{4,5},{5,6},{6,7},{7,0},{8,9},{9,10},{10,1... | collective-permute-start | bytes 184328 | tf_op jit(solution)/shard_map/ppermute | solution.py:200
  30.4 3.8 %collective-permute-start.33 = (f32[5,24,128]{2,1,0:T(8,128)S(1)}, f32[5,24,128]{2,1,0:T(8,128)S(1)}, u32[]{:S(2)}, u32[]{:S(2)}) collective-permute-start(f32[5,24,128]{2,1,0:T(8,128)S(1)} %get-tuple-element.80), channel_id=1, source_target_pairs={{1,0},{2,1},{3,2},{4,3},{5,4},{6,5},{7,6},{0,7},{9,8},{10,9},{11,1... | collective-permute-start | bytes 184328 | tf_op jit(solution)/shard_map/ppermute | solution.py:203
  34.3 1.3 %conditional.3 = (f32[12,24,128]{2,1,0:T(8,128)}) conditional(s32[]{:T(128)} %clamp.7, f32[12,24,128]{2,1,0:T(8,128)S(1)} %get-tuple-element.84, f32[12,24,128]{2,1,0:T(8,128)S(1)} %get-tuple-element.84, f32[12,24,128]{2,1,0:T(8,128)S(1)} %get-tuple-element.84, f32[12,24,128]{2,1,0:T(8,128)S(1)} %get-tuple-element.84, ...), branch_computations={%region_8.9_spmd, %region_9.10_spmd, %region_10.11_spmd, %region_1... | conditional | bytes 589872 | solution.py:219
  34.3 1.3 %collective-permute-start.31 = (f32[12,24,128]{2,1,0:T(8,128)S(1)}, f32[12,24,128]{2,1,0:T(8,128)}, u32[]{:S(2)}, u32[]{:S(2)}) collective-permute-start(f32[12,24,128]{2,1,0:T(8,128)S(1)} %param.15), channel_id=1, source_target_pairs={{24,31},{25,30},{26,29},{27,28},{28,27},{29,26},{30,25},{31,24}} | collective-permute-start | bytes 442376 | tf_op jit(solution)/shard_map/cond/branch_7_fun/ppermute | solution.py:216
  35.6 0.0 collective-permute-done.31
  35.6 0.9 collective-permute-done.32.west_ref.refs_1_
  36.5 0.0 collective-permute-done.33.east_ref.refs_2_
  36.5 0.2 slabs.1
  36.7 7.2 %conditional.2 = (f32[27,24,128]{2,1,0:T(8,128)}, f32[27,24,128]{2,1,0:T(8,128)}, f32[27,24,128]{2,1,0:T(8,128)}) conditional(s32[]{:T(128)} %clamp.6, (f32[27,24,128]{2,1,0:T(8,128)S(1)}, f32[27,24,128]{2,1,0:T(8,128)S(1)}) %slabs.1, (f32[27,24,128]{2,1,0:T(8,128)S(1)}, f32[27,24,128]{2,1,0:T(8,128)S(1)}) %slabs.1, ...), branch_computations={%region_0.1_spmd, %region_1.2_spmd, %region_2.3_spmd, %region_3.4_... | conditional | bytes 3981456 | solution.py:219
  36.7 1.3 %collective-permute-start.19 = (f32[27,24,128]{2,1,0:T(8,128)S(1)}, f32[27,24,128]{2,1,0:T(8,128)}, u32[]{:S(2)}, u32[]{:S(2)}) collective-permute-start(f32[27,24,128]{2,1,0:T(8,128)S(1)} %get-tuple-element.62), channel_id=1, source_target_pairs={{8,0},{16,8},{24,16},{9,1},{17,9},{25,17},{10,2},{18,10},{26,18},{... | collective-permute-start | bytes 995336 | tf_op jit(solution)/shard_map/cond/branch_6_fun/ppermute | solution.py:209
  38.0 1.4 %collective-permute-start.20 = (f32[27,24,128]{2,1,0:T(8,128)S(1)}, f32[27,24,128]{2,1,0:T(8,128)}, u32[]{:S(2)}, u32[]{:S(2)}) collective-permute-start(f32[27,24,128]{2,1,0:T(8,128)S(1)} %get-tuple-element.61), channel_id=1, source_target_pairs={{24,30},{25,29},{26,28},{27,27},{28,26},{29,25},{30,24},{31,31}} | collective-permute-start | bytes 995336 | tf_op jit(solution)/shard_map/cond/branch_6_fun/ppermute | solution.py:216
  39.4 3.7 %collective-permute-start.18 = (f32[27,24,128]{2,1,0:T(8,128)S(1)}, f32[27,24,128]{2,1,0:T(8,128)}, u32[]{:S(2)}, u32[]{:S(2)}) collective-permute-start(f32[27,24,128]{2,1,0:T(8,128)S(1)} %get-tuple-element.61), channel_id=1, source_target_pairs={{0,8},{8,16},{16,24},{1,9},{9,17},{17,25},{2,10},{10,18},{18,26},{... | collective-permute-start | bytes 995336 | tf_op jit(solution)/shard_map/cond/branch_6_fun/ppermute | solution.py:206
  43.2 0.0 collective-permute-done.19
  43.2 0.0 collective-permute-done.20
  43.2 0.7 collective-permute-done.18
  43.8 0.0 copy-done
  43.8 0.0 copy-done.1
  43.8 14.1 %sweeps.1 = (f32[48,24,256]{2,1,0:T(8,128)S(1)}, f32[21,48,256]{2,1,0:T(8,128)S(1)}) custom-call(s32[3]{0:T(128)S(1)} %pad_add_fusion.where_ref, f32[21]{0:T(128)S(1)} %copy-done, f32[21]{0:T(128)S(1)} %copy-done.1, f32[48,24,256]{2,1,0:T(8,128)S(1)} %get-tuple-element.78.own_ref.refs_0_, f32[5,24,128]{2,1,0:T(8,128)S(1)} %collective-permute-done.32.west_ref.refs_1_, ...), custom_call_target="tpu_custom_call" | custom-call | tf_op jit(solution)/shard_map/sweeps/pallas_call | solution.py:565
  58.0 5.5 %gather.1 = (f32[672,128]{1,0:T(8,128)S(1)}, f32[21,48,256]{2,1,0:T(8,128)}) custom-call(f32[48,24,256]{2,1,0:T(8,128)S(1)} %get-tuple-element.85.fine_ref, f32[21,48,256]{2,1,0:T(8,128)S(1)} %get-tuple-element.86.field_ref, f32[736,128]{1,0:T(8,128)S(1)} %bitcast.12), custom_call_target="tpu_custom_call" | custom-call | tf_op jit(solution)/shard_map/gather/pallas_call | solution.py:646
  63.5 23.9 %all_to_all.10 = f32[32,1,2688]{2,1,0:T(1,128)S(1)} all-to-all(f32[32,1,2688]{2,1,0:T(1,128)S(1)} %bitcast.14), channel_id=1, replica_groups=mesh['lat'=4,'lon'=8] {'lat','lon'}, dimensions={0} | all-to-all | bytes 688128 | tf_op jit(solution)/shard_map/all_to_all | solution.py:60
  87.4 0.8 unpack.1
Async XLA Ops:
  0.6 9.1 %copy-start.4 = (s32[256]{0:T(256)S(1)}, s32[256]{0:T(256)}, u32[]{:S(2)}) copy-start(s32[256]{0:T(256)} %param.29) | copy-start | bytes 3076
  0.6 22.3 %copy-start.2 = (f32[2,48,256]{2,1,0:T(8,128)S(1)}, f32[2,48,256]{2,1,0:T(8,128)}, u32[]{:S(2)}) copy-start(f32[2,48,256]{2,1,0:T(8,128)} %kappa_ref.1) | copy-start | bytes 294916
  0.7 22.3 %copy-start.3 = (s32[48,256]{1,0:T(8,128)S(1)}, s32[48,256]{1,0:T(8,128)}, u32[]{:S(2)}) copy-start(s32[48,256]{1,0:T(8,128)} %bottom_ref.1) | copy-start | bytes 147460
  2.5 20.5 %all-to-all-start = ((f32[32,1,2944]{2,1,0:T(1,128)}), f32[32,1,2944]{2,1,0:T(1,128)S(1)}, u32[]{:S(2)}, u32[]{:S(2)}) async-start(f32[32,1,2944]{2,1,0:T(1,128)} %bitcast.15), calls=%async_computation | async-start | bytes 753664 | tf_op jit(solution)/shard_map/all_to_all | solution.py:60
  29.5 14.4 %copy-start = (f32[21]{0:T(128)S(1)}, f32[21]{0:T(128)}, u32[]{:S(2)}) copy-start(f32[21]{0:T(128)} %scale_ref.1) | copy-start | bytes 256
  29.5 14.3 %copy-start.1 = (f32[21]{0:T(128)S(1)}, f32[21]{0:T(128)}, u32[]{:S(2)}) copy-start(f32[21]{0:T(128)} %sigma_ref.1) | copy-start | bytes 256
  29.5 7.0 %collective-permute-start.32 = (f32[5,24,128]{2,1,0:T(8,128)S(1)}, f32[5,24,128]{2,1,0:T(8,128)S(1)}, u32[]{:S(2)}, u32[]{:S(2)}) collective-permute-start(f32[5,24,128]{2,1,0:T(8,128)S(1)} %get-tuple-element.79), channel_id=1, source_target_pairs={{0,1},{1,2},{2,3},{3,4},{4,5},{5,6},{6,7},{7,0},{8,9},{9,10},{10,1... | collective-permute-start | bytes 184328 | tf_op jit(solution)/shard_map/ppermute | solution.py:200
  30.4 6.0 %collective-permute-start.33 = (f32[5,24,128]{2,1,0:T(8,128)S(1)}, f32[5,24,128]{2,1,0:T(8,128)S(1)}, u32[]{:S(2)}, u32[]{:S(2)}) collective-permute-start(f32[5,24,128]{2,1,0:T(8,128)S(1)} %get-tuple-element.80), channel_id=1, source_target_pairs={{1,0},{2,1},{3,2},{4,3},{5,4},{6,5},{7,6},{0,7},{9,8},{10,9},{11,1... | collective-permute-start | bytes 184328 | tf_op jit(solution)/shard_map/ppermute | solution.py:203
  34.3 1.3 %collective-permute-start.31 = (f32[12,24,128]{2,1,0:T(8,128)S(1)}, f32[12,24,128]{2,1,0:T(8,128)}, u32[]{:S(2)}, u32[]{:S(2)}) collective-permute-start(f32[12,24,128]{2,1,0:T(8,128)S(1)} %param.15), channel_id=1, source_target_pairs={{24,31},{25,30},{26,29},{27,28},{28,27},{29,26},{30,25},{31,24}} | collective-permute-start | bytes 442376 | tf_op jit(solution)/shard_map/cond/branch_7_fun/ppermute | solution.py:216
  36.7 6.5 %collective-permute-start.19 = (f32[27,24,128]{2,1,0:T(8,128)S(1)}, f32[27,24,128]{2,1,0:T(8,128)}, u32[]{:S(2)}, u32[]{:S(2)}) collective-permute-start(f32[27,24,128]{2,1,0:T(8,128)S(1)} %get-tuple-element.62), channel_id=1, source_target_pairs={{8,0},{16,8},{24,16},{9,1},{17,9},{25,17},{10,2},{18,10},{26,18},{... | collective-permute-start | bytes 995336 | tf_op jit(solution)/shard_map/cond/branch_6_fun/ppermute | solution.py:209
  38.0 5.2 %collective-permute-start.20 = (f32[27,24,128]{2,1,0:T(8,128)S(1)}, f32[27,24,128]{2,1,0:T(8,128)}, u32[]{:S(2)}, u32[]{:S(2)}) collective-permute-start(f32[27,24,128]{2,1,0:T(8,128)S(1)} %get-tuple-element.61), channel_id=1, source_target_pairs={{24,30},{25,29},{26,28},{27,27},{28,26},{29,25},{30,24},{31,31}} | collective-permute-start | bytes 995336 | tf_op jit(solution)/shard_map/cond/branch_6_fun/ppermute | solution.py:216
  39.4 4.4 %collective-permute-start.18 = (f32[27,24,128]{2,1,0:T(8,128)S(1)}, f32[27,24,128]{2,1,0:T(8,128)}, u32[]{:S(2)}, u32[]{:S(2)}) collective-permute-start(f32[27,24,128]{2,1,0:T(8,128)S(1)} %get-tuple-element.61), channel_id=1, source_target_pairs={{0,8},{8,16},{16,24},{1,9},{9,17},{17,25},{2,10},{10,18},{18,26},{... | collective-permute-start | bytes 995336 | tf_op jit(solution)/shard_map/cond/branch_6_fun/ppermute | solution.py:206

commit v6 on v5

--- a/solution.py
+++ b/solution.py
@@ -36,14 +36,14 @@
     owners, slots = cell_ref.shape
     for c in range(channels):
         out_ref[pl.ds(c, owners, stride=width), :] = value_ref[pl.ds(c * owners, owners), :]
-    owner = lax.broadcasted_iota(jnp.int32, (owners, slots), 0)
-    count = jnp.zeros((owners, slots), jnp.int32)
-    for d in range(owners):
-        count = jnp.where(owner == d, count_ref[0, d], count)
+    shape = (owners, owners)
+    on_diagonal = lax.broadcasted_iota(jnp.int32, shape, 0) == lane_iota(shape)
+    count = jnp.broadcast_to(count_ref[...].astype(jnp.float32), shape)
+    count = jnp.sum(jnp.where(on_diagonal, count, 0.0), axis=1, keepdims=True)
     cell = cell_ref[...].astype(jnp.float32)
     row = jnp.floor((cell + 0.5) * (1.0 / cols))
     col = cell - row * cols
-    row = jnp.where(lane_iota((owners, slots)) < count, row, -1.0)
+    row = jnp.where(lane_iota((owners, slots)).astype(jnp.float32) < count, row, -1.0)
     out_ref[pl.ds(channels, owners, stride=width), :] = row
     out_ref[pl.ds(channels + 1, owners, stride=width), :] = col
 
@@ -208,20 +208,20 @@
     def south(self, x):
         return lax.ppermute(x, "lat", self.to_south)
 
-    def fold(self, part, send, *operands):
+    def fold(self, first_part, kind, send, *operands):
         first, n = self.first, self.n_lon
 
-        def branch(tile):
-            pairs = [(first + s, first + (tile - s) % n) for s in range(n)]
-            return lambda *xs: send(lambda x: lax.ppermute(x, ("lat", "lon"), pairs), *xs)
-
-        tile = lax.rem(self.centre_tile + n - part, n)
-        return lax.switch(tile, [branch(t) for t in range(n)], *operands)
-
-
-def scatter_kernel(channels, chunk, where_ref, obs_ref, bottom_ref, kappa_ref, *refs):
+        def branch(tile, kind):
+            pairs = [(first + s, first + (tile - first_part(kind) - s) % n) for s in range(n)]
+            return lambda *xs: send(lambda x: lax.ppermute(x, ("lat", "lon"), pairs), kind, *xs)
+
+        branches = [branch(t, k) for t in range(n) for k in (0, 1)]
+        return lax.switch(self.centre_tile * 2 + kind, branches, *operands)
+
+
+def scatter_kernel(channels, chunk, obs_ref, bottom_ref, kappa_ref, *refs):
     own_ref, west_ref, east_ref = refs[:3]
-    part_ref, left_ref, right_ref, sum_ref, blocks_ref = refs[3:]
+    part_refs, (left_ref, right_ref, sum_ref, blocks_ref) = refs[3:5], refs[5:]
     rows, padded, cols = own_ref.shape
     slots = obs_ref.shape[1]
     senders = blocks_ref.shape[0] // padded
@@ -272,19 +272,16 @@
                 ]
     pack_strip(lambda j: own_ref[j, :, :LANES], rows, 0, west_ref)
     pack_strip(lambda j: own_ref[j, :, cols - LANES :], rows, LANES - DEPTH, east_ref)
-    for kind, start in enumerate(part_starts(cols)):
-
-        @pl.when(where_ref[2] == kind)
-        def _():
-            m, shift = divmod(start, LANES)
-            for j in range(DEPTH):
-                x = own_ref[rows - DEPTH + j, :, m * LANES : (m + 1) * LANES]
-                y = own_ref[rows - DEPTH + j, :, (m + 1) * LANES : (m + 2) * LANES]
-                here = lane_iota(x.shape) < LANES - shift
-                part_ref[j] = jnp.where(here, roll_lanes(x, -shift), roll_lanes(y, -shift))
-
-
-def scatter(where, obs, bottom_level, diffusivity, channels, padded):
+    for ref, start in zip(part_refs, part_starts(cols)):
+        m, shift = divmod(start, LANES)
+        for j in range(DEPTH):
+            x = own_ref[rows - DEPTH + j, :, m * LANES : (m + 1) * LANES]
+            y = own_ref[rows - DEPTH + j, :, (m + 1) * LANES : (m + 2) * LANES]
+            here = lane_iota(x.shape) < LANES - shift
+            ref[j] = jnp.where(here, roll_lanes(x, -shift), roll_lanes(y, -shift))
+
+
+def scatter(obs, bottom_level, diffusivity, channels, padded):
     slots = obs.shape[1]
     senders = obs.shape[0] // (channels + 2)
     rows, cols = bottom_level.shape
@@ -293,12 +290,12 @@
     vmem = pl.BlockSpec(memory_space=pltpu.VMEM)
     side = (strip_count(rows), padded, LANES)
     part = (DEPTH, padded, LANES)
-    shapes = [(rows, padded, cols), side, side, part]
+    shapes = [(rows, padded, cols), side, side, part, part]
     shapes = [jax.ShapeDtypeStruct(shape, jnp.float32) for shape in shapes]
     return pl.pallas_call(
         functools.partial(scatter_kernel, channels, chunk),
         out_shape=tuple(shapes),
-        in_specs=[pl.BlockSpec(memory_space=pltpu.SMEM)] + [vmem] * 3,
+        in_specs=[vmem] * 3,
         out_specs=(vmem,) * len(shapes),
         scratch_shapes=[
             pltpu.VMEM((2 * channels * rows, chunk * slots), jnp.bfloat16),
@@ -311,7 +308,7 @@
             flops=4 * senders * slots * padded * rows * cols, bytes_accessed=0, transcendentals=0
         ),
         name="scatter",
-    )(where, obs, bottom_level, diffusivity)
+    )(obs, bottom_level, diffusivity)
 
 
 def east_of(xs, m):
@@ -384,7 +381,7 @@
     return out
 
 
-def make_weights(part, level, scale, sigma, cell_ref, wide_ref, be_ref, bn_ref, root_ref, state_ref):
+def make_weights(part, level, scale, sigma, cell_ref, wide_ref, be_ref, bn_ref, root_ref, source_ref, state_ref):
     total, count = be_ref.shape[:2]
     zero = jnp.zeros((SUB, LANES), jnp.float32)
     below, root_below = [zero] * count, [zero] * count
@@ -404,7 +401,9 @@
             x = x * (1.5 - 0.5 * d * x * x)
             root.append(x)
             root_ref[j, m] = x
-            state_ref[j, m] = start[m] * jnp.where(level < spread(0, m), sigma * (d * x), 0.0)
+            state = start[m] * jnp.where(level < spread(0, m), sigma * (d * x), 0.0)
+            state_ref[j, m] = state
+            source_ref[j, m] = state * (x * x)
         for m in range(count):
             be_ref[j, m] = a_e[m] * root[m] * east_of(root, m)
             bn_ref[j - 1, m] = below[m] * root_below[m] * root[m]
@@ -509,11 +508,11 @@
         scale = jnp.where(c == i, scale_ref[i], scale)
         sigma = jnp.where(c == i, sigma_ref[i], sigma)
     make_weights(
-        part, level.astype(jnp.float32), scale, sigma, cell_ref, wide_ref, be_ref, bn_ref, root_ref, state_ref
+        part, level.astype(jnp.float32), scale, sigma, cell_ref, wide_ref, be_ref, bn_ref, root_ref, source_ref, state_ref
     )
 
     done = 0
-    for _step in range(STEPS):
+    for step in range(STEPS):
 
         def make_source(j, carry):
             for m in range(count):
@@ -521,7 +520,8 @@
                 source_ref[j, m] = state_ref[j, m] * (root * root)
             return carry
 
-        lax.fori_loop(skip + done, total - skip - done, make_source, 0, unroll=4)
+        if step > 0:
+            lax.fori_loop(skip + done, total - skip - done, make_source, 0, unroll=4)
         for some in (SWEEPS - SWEEPS // 2, SWEEPS // 2):
             if some > 0:
                 run_sweeps(
@@ -641,7 +641,7 @@
     rows, padded, cols = fine.shape
     slots = obs.shape[1]
     senders = obs.shape[0] // (channels + 2)
-    pair = 16 if senders % 16 == 0 else 1
+    pair = 32 if senders % 32 == 0 else 1
     vmem = pl.BlockSpec(memory_space=pltpu.VMEM)
     return pl.pallas_call(
         functools.partial(gather_kernel, channels, pair),
@@ -657,7 +657,7 @@
             pltpu.VMEM((senders * padded, slots), jnp.float32),
             pltpu.SemaphoreType.DMA,
         ],
-        compiler_params=params(28),
+        compiler_params=params(44),
         name="gather",
     )(fine, field, obs)
 
@@ -670,14 +670,13 @@
     n_lat, n_lon = lax.axis_size("lat"), lax.axis_size("lon")
     padded = -(-(channels + COEFS) // SUB) * SUB
     vmem = pl.BlockSpec(memory_space=pltpu.VMEM)
-    smem = pl.BlockSpec(memory_space=pltpu.SMEM)
 
     outgoing = pl.pallas_call(
         functools.partial(pack_kernel, channels, channels + 2, cols),
         grid=(1,),
         out_shape=jax.ShapeDtypeStruct((owners * (channels + 2), slots), jnp.float32),
         in_specs=[
-            smem,
+            pl.BlockSpec((1, owners), lambda i: (0, 0)),
             pl.BlockSpec((channels * owners, slots), lambda i: (0, 0)),
             pl.BlockSpec((owners, slots), lambda i: (0, 0)),
         ],
@@ -694,15 +693,15 @@
     where = jnp.stack([is_top, centre_col, kind])
     moves = Moves(n_lat, n_lon, centre // cols)
 
-    own, west, east, part = scatter(where, arrived, bottom_level, diffusivity, channels, padded)
+    own, west, east, *parts = scatter(arrived, bottom_level, diffusivity, channels, padded)
     west, east = moves.east(east), moves.west(west)
-    part = moves.fold(kind, lambda fold, x: fold(x), part)
+    part = moves.fold(lambda k: k, kind, lambda fold, k, *xs: fold(xs[k]), *parts)
     top, low = slabs(own, west, east)
 
-    def send(fold, top, low):
+    def send(fold, _, top, low):
         return moves.north(top), moves.south(low), fold(top)
 
-    around = (west, east, *moves.fold(1 - kind, send, top, low), part)
+    around = (west, east, *moves.fold(lambda k: 1 - k, kind, send, top, low), part)
     fine, field = sweeps(where, own, around, length_scale, sigma, channels)
     local_fit, diffused = gather(fine, field, arrived, channels)
     returned = exchange(local_fit, owners)

time: 88.4 us -> 87 us (0.984); the launches traced: 88.1 us -> 85.4 us
  blocking collectives: 23.9 us -> 22.1 us
  Pallas kernels: 28.9 us -> 27.9 us
    all_to_all x1, blocking collectives: 23.9 us -> 22.1 us  [exchange(): lax.all_to_all(x, ('lat', 'lon'), split_axis=0, concat_axis=0, tiled=True)]
where the time goes in v6:
time: 87 us; the launch traced here: 85.4 us
  Pallas kernels  27.9 us (32%)
  blocking collectives  22.1 us (25%)
  starting transfers between devices  19.9 us (23%)
  waiting for transfers between devices  13.4 us (15%)
  between operations  1.43 us (2%)
    all_to_all x1, blocking collectives, exchange(): lax.all_to_all(x, ('lat', 'lon'), split_axis=0, concat_axis=0, tiled=True)  22.1 us
    pallas_call x1, Pallas kernels, sweeps(): pl.pallas_call(functools.partial(sweep_kernel, channels % SUB), out_shape...  14 us
    all_to_all x1, waiting for transfers between devices, exchange(): lax.all_to_all(x, ('lat', 'lon'), split_axis=0, concat_axis=0, tiled=True)  12 us
    all_to_all x1, starting transfers between devices, exchange(): lax.all_to_all(x, ('lat', 'lon'), split_axis=0, concat_axis=0, tiled=True)  7.3 us
    pallas_call x1, Pallas kernels, scatter(): pl.pallas_call(functools.partial(scatter_kernel, channels, chunk), out_sh...  5.97 us
    pallas_call x1, Pallas kernels, gather(): pl.pallas_call(functools.partial(gather_kernel, channels, pair), out_shap...  5.18 us
    ppermute x1, starting transfers between devices, west(): return lax.ppermute(x, 'lon', self.to_west)  3.84 us
    ppermute x1, starting transfers between devices, north(): return lax.ppermute(x, 'lat', self.to_north)  3.77 us
  transfers between devices with their start and end apart: 7, of which 3 were waited for; matrix products, arithmetic and copies ran while one was open for 1% of the time, Pallas kernels for 0%

profile of v6, /device:TPU:0, one launch (start us, length us, event | category | flops | bytes accessed | tf_op | source)
XLA Modules:
  0.0 85.4 jit_solution(17066776091799137365)
XLA Ops:
  0.6 0.0 copy-start.4
  0.6 0.0 copy-start.2
  0.7 0.0 copy-start.3
  0.7 1.8 %pack.1 = f32[736,128]{1,0:T(8,128)} custom-call(s32[1,32]{1,0:T(1,128)} %count_ref.1, f32[672,128]{1,0:T(8,128)} %bitcast.16, s32[32,128]{1,0:T(8,128)} %bitcast.18), custom_call_target="tpu_custom_call" | custom-call | tf_op jit(solution)/shard_map/pack/pallas_call | solution.py:674
  2.5 7.3 %all-to-all-start = ((f32[32,1,2944]{2,1,0:T(1,128)}), f32[32,1,2944]{2,1,0:T(1,128)S(1)}, u32[]{:S(2)}, u32[]{:S(2)}) async-start(f32[32,1,2944]{2,1,0:T(1,128)} %bitcast.15), calls=%async_computation | async-start | bytes 753664 | tf_op jit(solution)/shard_map/all_to_all | solution.py:60
  9.8 0.0 copy-done.4
  9.8 0.5 slice.3
  11.0 12.0 %all-to-all-done = f32[32,1,2944]{2,1,0:T(1,128)S(1)} async-done(((f32[32,1,2944]{2,1,0:T(1,128)}), f32[32,1,2944]{2,1,0:T(1,128)S(1)}, u32[]{:S(2)}, u32[]{:S(2)}) %all-to-all-start) | async-done | bytes 376864 | tf_op jit(solution)/shard_map/all_to_all | solution.py:60
  23.0 0.0 copy-done.2
  23.0 0.0 copy-done.3
  23.0 6.0 %scatter.1 = (f32[48,24,256]{2,1,0:T(8,128)S(1)}, f32[5,24,128]{2,1,0:T(8,128)S(1)}, f32[5,24,128]{2,1,0:T(8,128)S(1)}, f32[12,24,128]{2,1,0:T(8,128)S(1)}, f32[12,24,128]{2,1,0:T(8,128)S(1)}) custom-call(f32[736,128]{1,0:T(8,128)S(1)} %bitcast.11, s32[48,256]{1,0:T(8,128)S(1)} %copy-done.3, f32[2,48,256]{2,1,0:T(8,128)S(1)} %copy-done.2), custom_call_target="tpu_custom_call" | custom-call | flops 4831838208 | tf_op jit(solution)/shard_map/scatter/pallas_call | solution.py:295
  29.0 0.0 copy-start
  29.0 0.0 copy-start.1
  29.0 0.9 %collective-permute-start.64 = (f32[5,24,128]{2,1,0:T(8,128)S(1)}, f32[5,24,128]{2,1,0:T(8,128)S(1)}, u32[]{:S(2)}, u32[]{:S(2)}) collective-permute-start(f32[5,24,128]{2,1,0:T(8,128)S(1)} %get-tuple-element.144), channel_id=1, source_target_pairs={{0,1},{1,2},{2,3},{3,4},{4,5},{5,6},{6,7},{7,0},{8,9},{9,10},{10,1... | collective-permute-start | bytes 184328 | tf_op jit(solution)/shard_map/ppermute | solution.py:200
  29.9 3.8 %collective-permute-start.65 = (f32[5,24,128]{2,1,0:T(8,128)S(1)}, f32[5,24,128]{2,1,0:T(8,128)S(1)}, u32[]{:S(2)}, u32[]{:S(2)}) collective-permute-start(f32[5,24,128]{2,1,0:T(8,128)S(1)} %get-tuple-element.145), channel_id=1, source_target_pairs={{1,0},{2,1},{3,2},{4,3},{5,4},{6,5},{7,6},{0,7},{9,8},{10,9},{11,1... | collective-permute-start | bytes 184328 | tf_op jit(solution)/shard_map/ppermute | solution.py:203
  33.8 0.1 pad_add_fusion.where_ref
  33.9 1.3 %conditional.3 = (f32[12,24,128]{2,1,0:T(8,128)}) conditional(s32[]{:T(128)} %clamp.4, f32[12,24,128]{2,1,0:T(8,128)S(1)} %get-tuple-element.149, f32[12,24,128]{2,1,0:T(8,128)S(1)} %get-tuple-element.150, f32[12,24,128]{2,1,0:T(8,128)S(1)} %get-tuple-element.149, f32[12,24,128]{2,1,0:T(8,128)S(1)} %get-tuple-element.150, ...), branch_computations={%region_16.17_spmd, %region_17.18_spmd, %region_18.19_spmd, %regio... | conditional | bytes 589872 | solution.py:219
  33.9 1.3 %collective-permute-start.54 = (f32[12,24,128]{2,1,0:T(8,128)S(1)}, f32[12,24,128]{2,1,0:T(8,128)}, u32[]{:S(2)}, u32[]{:S(2)}) collective-permute-start(f32[12,24,128]{2,1,0:T(8,128)S(1)} %param.22), channel_id=1, source_target_pairs={{24,27},{25,26},{26,25},{27,24},{28,31},{29,30},{30,29},{31,28}} | collective-permute-start | bytes 442376 | tf_op jit(solution)/shard_map/cond/branch_6_fun/ppermute | solution.py:216
  35.2 0.0 collective-permute-done.54
  35.2 0.8 collective-permute-done.64.west_ref.refs_1_
  36.0 0.0 collective-permute-done.65.east_ref.refs_2_
  36.0 0.2 slabs.1
  36.2 7.2 %conditional.2 = (f32[27,24,128]{2,1,0:T(8,128)}, f32[27,24,128]{2,1,0:T(8,128)}, f32[27,24,128]{2,1,0:T(8,128)}) conditional(s32[]{:T(128)} %clamp.4, (f32[27,24,128]{2,1,0:T(8,128)S(1)}, f32[27,24,128]{2,1,0:T(8,128)S(1)}) %slabs.1, (f32[27,24,128]{2,1,0:T(8,128)S(1)}, f32[27,24,128]{2,1,0:T(8,128)S(1)}) %slabs.1, ...), branch_computations={%region_0.1_spmd, %region_1.2_spmd, %region_2.3_spmd, %region_3.4_... | conditional | bytes 3981456 | solution.py:219
  36.2 1.3 %collective-permute-start.19 = (f32[27,24,128]{2,1,0:T(8,128)S(1)}, f32[27,24,128]{2,1,0:T(8,128)}, u32[]{:S(2)}, u32[]{:S(2)}) collective-permute-start(f32[27,24,128]{2,1,0:T(8,128)S(1)} %get-tuple-element.110), channel_id=1, source_target_pairs={{8,0},{16,8},{24,16},{9,1},{17,9},{25,17},{10,2},{18,10},{26,18},{... | collective-permute-start | bytes 995336 | tf_op jit(solution)/shard_map/cond/branch_6_fun/ppermute | solution.py:209
  37.5 1.4 %collective-permute-start.20 = (f32[27,24,128]{2,1,0:T(8,128)S(1)}, f32[27,24,128]{2,1,0:T(8,128)}, u32[]{:S(2)}, u32[]{:S(2)}) collective-permute-start(f32[27,24,128]{2,1,0:T(8,128)S(1)} %get-tuple-element.109), channel_id=1, source_target_pairs={{24,26},{25,25},{26,24},{27,31},{28,30},{29,29},{30,28},{31,27}} | collective-permute-start | bytes 995336 | tf_op jit(solution)/shard_map/cond/branch_6_fun/ppermute | solution.py:216
  38.9 3.8 %collective-permute-start.18 = (f32[27,24,128]{2,1,0:T(8,128)S(1)}, f32[27,24,128]{2,1,0:T(8,128)}, u32[]{:S(2)}, u32[]{:S(2)}) collective-permute-start(f32[27,24,128]{2,1,0:T(8,128)S(1)} %get-tuple-element.109), channel_id=1, source_target_pairs={{0,8},{8,16},{16,24},{1,9},{9,17},{17,25},{2,10},{10,18},{18,26},{... | collective-permute-start | bytes 995336 | tf_op jit(solution)/shard_map/cond/branch_6_fun/ppermute | solution.py:206
  42.7 0.0 collective-permute-done.19
  42.7 0.0 collective-permute-done.20
  42.7 0.6 collective-permute-done.18
  43.3 0.0 copy-done
  43.3 0.0 copy-done.1
  43.3 14.0 %sweeps.1 = (f32[48,24,256]{2,1,0:T(8,128)S(1)}, f32[21,48,256]{2,1,0:T(8,128)S(1)}) custom-call(s32[3]{0:T(128)S(1)} %pad_add_fusion.where_ref, f32[21]{0:T(128)S(1)} %copy-done, f32[21]{0:T(128)S(1)} %copy-done.1, f32[48,24,256]{2,1,0:T(8,128)S(1)} %get-tuple-element.143.own_ref.refs_0_, f32[5,24,128]{2,1,0:T(8,128)S(1)} %collective-permute-done.64.west_ref.refs_1_, ...), custom_call_target="tpu_custom_call" | custom-call | tf_op jit(solution)/shard_map/sweeps/pallas_call | solution.py:565
  57.3 5.2 %gather.1 = (f32[672,128]{1,0:T(8,128)S(1)}, f32[21,48,256]{2,1,0:T(8,128)}) custom-call(f32[48,24,256]{2,1,0:T(8,128)S(1)} %get-tuple-element.151.fine_ref, f32[21,48,256]{2,1,0:T(8,128)S(1)} %get-tuple-element.152.field_ref, f32[736,128]{1,0:T(8,128)S(1)} %bitcast.12), custom_call_target="tpu_custom_call" | custom-call | tf_op jit(solution)/shard_map/gather/pallas_call | solution.py:646
  62.5 22.1 %all_to_all.10 = f32[32,1,2688]{2,1,0:T(1,128)S(1)} all-to-all(f32[32,1,2688]{2,1,0:T(1,128)S(1)} %bitcast.14), channel_id=1, replica_groups=mesh['lat'=4,'lon'=8] {'lat','lon'}, dimensions={0} | all-to-all | bytes 688128 | tf_op jit(solution)/shard_map/all_to_all | solution.py:60
  84.7 0.8 unpack.1
Async XLA Ops:
  0.6 9.2 %copy-start.4 = (s32[256]{0:T(256)S(1)}, s32[256]{0:T(256)}, u32[]{:S(2)}) copy-start(s32[256]{0:T(256)} %param.45) | copy-start | bytes 3076
  0.6 22.4 %copy-start.2 = (f32[2,48,256]{2,1,0:T(8,128)S(1)}, f32[2,48,256]{2,1,0:T(8,128)}, u32[]{:S(2)}) copy-start(f32[2,48,256]{2,1,0:T(8,128)} %kappa_ref.1) | copy-start | bytes 294916
  0.7 22.4 %copy-start.3 = (s32[48,256]{1,0:T(8,128)S(1)}, s32[48,256]{1,0:T(8,128)}, u32[]{:S(2)}) copy-start(s32[48,256]{1,0:T(8,128)} %bottom_ref.1) | copy-start | bytes 147460
  2.5 20.5 %all-to-all-start = ((f32[32,1,2944]{2,1,0:T(1,128)}), f32[32,1,2944]{2,1,0:T(1,128)S(1)}, u32[]{:S(2)}, u32[]{:S(2)}) async-start(f32[32,1,2944]{2,1,0:T(1,128)} %bitcast.15), calls=%async_computation | async-start | bytes 753664 | tf_op jit(solution)/shard_map/all_to_all | solution.py:60
  29.0 14.4 %copy-start = (f32[21]{0:T(128)S(1)}, f32[21]{0:T(128)}, u32[]{:S(2)}) copy-start(f32[21]{0:T(128)} %scale_ref.1) | copy-start | bytes 256
  29.0 14.3 %copy-start.1 = (f32[21]{0:T(128)S(1)}, f32[21]{0:T(128)}, u32[]{:S(2)}) copy-start(f32[21]{0:T(128)} %sigma_ref.1) | copy-start | bytes 256
  29.0 7.0 %collective-permute-start.64 = (f32[5,24,128]{2,1,0:T(8,128)S(1)}, f32[5,24,128]{2,1,0:T(8,128)S(1)}, u32[]{:S(2)}, u32[]{:S(2)}) collective-permute-start(f32[5,24,128]{2,1,0:T(8,128)S(1)} %get-tuple-element.144), channel_id=1, source_target_pairs={{0,1},{1,2},{2,3},{3,4},{4,5},{5,6},{6,7},{7,0},{8,9},{9,10},{10,1... | collective-permute-start | bytes 184328 | tf_op jit(solution)/shard_map/ppermute | solution.py:200
  29.9 6.0 %collective-permute-start.65 = (f32[5,24,128]{2,1,0:T(8,128)S(1)}, f32[5,24,128]{2,1,0:T(8,128)S(1)}, u32[]{:S(2)}, u32[]{:S(2)}) collective-permute-start(f32[5,24,128]{2,1,0:T(8,128)S(1)} %get-tuple-element.145), channel_id=1, source_target_pairs={{1,0},{2,1},{3,2},{4,3},{5,4},{6,5},{7,6},{0,7},{9,8},{10,9},{11,1... | collective-permute-start | bytes 184328 | tf_op jit(solution)/shard_map/ppermute | solution.py:203
  33.9 1.3 %collective-permute-start.54 = (f32[12,24,128]{2,1,0:T(8,128)S(1)}, f32[12,24,128]{2,1,0:T(8,128)}, u32[]{:S(2)}, u32[]{:S(2)}) collective-permute-start(f32[12,24,128]{2,1,0:T(8,128)S(1)} %param.22), channel_id=1, source_target_pairs={{24,27},{25,26},{26,25},{27,24},{28,31},{29,30},{30,29},{31,28}} | collective-permute-start | bytes 442376 | tf_op jit(solution)/shard_map/cond/branch_6_fun/ppermute | solution.py:216
  36.2 6.5 %collective-permute-start.19 = (f32[27,24,128]{2,1,0:T(8,128)S(1)}, f32[27,24,128]{2,1,0:T(8,128)}, u32[]{:S(2)}, u32[]{:S(2)}) collective-permute-start(f32[27,24,128]{2,1,0:T(8,128)S(1)} %get-tuple-element.110), channel_id=1, source_target_pairs={{8,0},{16,8},{24,16},{9,1},{17,9},{25,17},{10,2},{18,10},{26,18},{... | collective-permute-start | bytes 995336 | tf_op jit(solution)/shard_map/cond/branch_6_fun/ppermute | solution.py:209
  37.5 5.2 %collective-permute-start.20 = (f32[27,24,128]{2,1,0:T(8,128)S(1)}, f32[27,24,128]{2,1,0:T(8,128)}, u32[]{:S(2)}, u32[]{:S(2)}) collective-permute-start(f32[27,24,128]{2,1,0:T(8,128)S(1)} %get-tuple-element.109), channel_id=1, source_target_pairs={{24,26},{25,25},{26,24},{27,31},{28,30},{29,29},{30,28},{31,27}} | collective-permute-start | bytes 995336 | tf_op jit(solution)/shard_map/cond/branch_6_fun/ppermute | solution.py:216
  38.9 4.4 %collective-permute-start.18 = (f32[27,24,128]{2,1,0:T(8,128)S(1)}, f32[27,24,128]{2,1,0:T(8,128)}, u32[]{:S(2)}, u32[]{:S(2)}) collective-permute-start(f32[27,24,128]{2,1,0:T(8,128)S(1)} %get-tuple-element.109), channel_id=1, source_target_pairs={{0,8},{8,16},{16,24},{1,9},{9,17},{17,25},{2,10},{10,18},{18,26},{... | collective-permute-start | bytes 995336 | tf_op jit(solution)/shard_map/cond/branch_6_fun/ppermute | solution.py:206
